TPU v7x, 32 devices: a whole 2x2x4 slice. The times are simulated.
32 devices in a mesh: dp: 8 (over z, core), tensor: 4 (over y, x).
Axes of the slice: x: 2, y: 2, z: 4, core: 2. Of those that a mesh axis runs over, the one named last changes fastest.
Arguments:
- x_in: bfloat16 [8192, 1536], P(('dp', 'tensor')), may hold values from -6 to 6
- segments: int32 [8192], P('dp'), may hold values from 0 to 4, as said below
- pre_gain: float32 [1536], replicated, may hold values from 0.25 to 1.75
- w_z: bfloat16 [1536, 3072], P('dp', 'tensor'), may hold values from -0.15625 to 0.15625
- w_x: bfloat16 [1536, 3072], P('dp', 'tensor'), may hold values from -0.15625 to 0.15625
- w_bc: bfloat16 [1536, 256], P('dp'), may hold values from -0.15625 to 0.15625
- w_dt: bfloat16 [1536, 48], P('dp', 'tensor'), may hold values from -0.078125 to 0.078125
- conv_x_w: float32 [4, 3072], P(None, 'tensor'), may hold values from -3 to 3
- conv_x_b: float32 [3072], P('tensor'), may hold values from -3 to 3
- conv_bc_w: float32 [4, 256], replicated, may hold values from -3 to 3
- conv_bc_b: float32 [256], replicated, may hold values from -3 to 3
- a_log: float32 [48], P('tensor'), may hold values from 0 to 2
- dt_bias: float32 [48], P('tensor'), may hold values from -7.5 to -2.5
- d_skip: float32 [48], P('tensor'), may hold values from 0.5 to 1.5
- gate_gain: float32 [3072], P('tensor'), may hold values from 0.25 to 1.75
- w_out: bfloat16 [3072, 1536], P('tensor', 'dp'), may hold values from -0.109375 to 0.109375
- cotangent: bfloat16 [8192, 1536], P(('dp', 'tensor')), may hold values from -6 to 6
Outputs:
- block_out: bfloat16 [8192, 1536], P(('dp', 'tensor'))
- grad_x: bfloat16 [8192, 1536], P(('dp', 'tensor'))
- grad_pre_gain: float32 [1536], replicated
- grad_w_z: float32 [1536, 3072], P('dp', 'tensor')
- grad_w_x: float32 [1536, 3072], P('dp', 'tensor')
- grad_w_bc: float32 [1536, 256], P('dp')
- grad_w_dt: float32 [1536, 48], P('dp', 'tensor')
- grad_conv_x_w: float32 [4, 3072], P(None, 'tensor')
- grad_conv_x_b: float32 [3072], P('tensor')
- grad_conv_bc_w: float32 [4, 256], replicated
- grad_conv_bc_b: float32 [256], replicated
- grad_a_log: float32 [48], P('tensor')
- grad_dt_bias: float32 [48], P('tensor')
- grad_d_skip: float32 [48], P('tensor')
- grad_gate_gain: float32 [3072], P('tensor')
- grad_w_out: float32 [3072, 1536], P('tensor', 'dp')
Inputs may be any that keep to these rules, and one draw needn't show every extreme that they name: `segments`: within each packed row of 1024 tokens (those of one index of dp) the numbers start at 0, never fall and rise by at most one from a token to the next; equal numbers mark one document; every row holds exactly five documents.
All inputs are finite; a program needn't handle non-finite values.
Results may differ from a plain program's by a relative error of at most 0.02.
Values may be sent and summed in bfloat16 or wider, within the bound.
A program may use at most 128 MiB of HBM per device.

v0:
```python
import functools
import types

import jax
import jax.numpy as jnp
from jax import lax
from jax.experimental import pallas as pl
from jax.experimental.pallas import tpu as pltpu
from jax.sharding import PartitionSpec as P

HEADDIM = 64
NSTATE = 128
CHUNK = 128
LANES = 128
EPS = 1e-05
LOG2E = 1.4426950408889634
F32 = jnp.float32
BF16 = jnp.bfloat16
VMEM_LIMIT = 62 * 1024 * 1024
exact = lax.Precision.HIGHEST


def dot_nn(a, b):
    return lax.dot_general(a, b, (((1,), (0,)), ((), ())), preferred_element_type=F32)


def dot_nt(a, b):
    return lax.dot_general(a, b, (((1,), (1,)), ((), ())), preferred_element_type=F32)


def dot_tn(a, b):
    return lax.dot_general(a, b, (((0,), (0,)), ((), ())), preferred_element_type=F32)


def sigmoid(v):
    return 1.0 / (1.0 + jnp.exp(-v))


def softplus(v):
    return jnp.maximum(v, 0.0) + jnp.log1p(jnp.exp(-jnp.abs(v)))


def fold_rows(v):
    return jnp.sum(v.reshape(v.shape[0] // 8, 8, v.shape[1]), axis=0)


def split_two(v):
    high = v.astype(BF16)
    return high, (v - high.astype(F32)).astype(BF16)


def tile_iotas():
    shape = (CHUNK, LANES)
    return lax.broadcasted_iota(jnp.int32, shape, 0), lax.broadcasted_iota(jnp.int32, shape, 1)


def chunk_rows(c, pad=0, extra=0):
    return pl.ds(pl.multiple_of(c * CHUNK + pad, 8), CHUNK + extra)


def prepare_steps(c, r):
    row, col = tile_iotas()
    rows = chunk_rows(c)
    lower = (row >= col).astype(F32)
    step = softplus(r.dtr[rows, r.dtr_at : r.dtr_at + LANES] + r.dt_bias[...])
    log_step = step * (-jnp.exp(r.a_log[...]) * LOG2E)
    total = jnp.dot(lower, log_step, precision=exact, preferred_element_type=F32)
    r.step[rows, :] = step
    r.total[rows, :] = total
    r.total_t[pl.ds(pl.multiple_of(c * 16, 16), 16), :] = total.T[:16]


def segment_parts(c, r):
    down = r.seg_down[chunk_rows(c, 8), :]
    across = r.seg_across[pl.ds(c, 1), :]
    before = r.seg_down[pl.ds(pl.multiple_of(c * CHUNK, 8), 8), :][7:8, :]
    last = down[CHUNK - 1 : CHUNK, :]
    carried = (down == before).astype(F32)
    to_end = (down == last).astype(F32)
    carry_on = (last == before).astype(F32)
    return down, across, carried, to_end, carry_on


def masks_back(c, r, down):
    window = r.seg_down[chunk_rows(c, 0, 8), :]
    return [
        (pltpu.roll(window, j, 0)[8 : 8 + CHUNK] == down).astype(F32) for j in range(1, 4)
    ]


def masks_ahead(c, r, down):
    window = r.seg_down[chunk_rows(c, 8, 8), :]
    full = CHUNK + 8
    return [(pltpu.roll(window, full - j, 0)[:CHUNK] == down).astype(F32) for j in range(1, 4)]


def conv_tile(c, ref, at, weight, bias, w_at, masks):
    lanes = slice(at, at + LANES)
    w_lanes = slice(w_at, w_at + LANES)
    here = ref[chunk_rows(c), lanes]
    ahead = ref[pl.ds(pl.multiple_of(jnp.maximum(c * CHUNK - 8, 0), 8), 8), lanes]
    window = jnp.concatenate([ahead, here], axis=0)
    out = here * weight[3:4, w_lanes] + bias[0:1, w_lanes]
    for j in range(1, 4):
        shifted = pltpu.roll(window, j, 0)[8 : 8 + CHUNK]
        out = out + (shifted * masks[j - 1]) * weight[3 - j : 4 - j, w_lanes]
    return out


def pair_columns(tile, p, first):
    left = jnp.broadcast_to(tile[:, 2 * p : 2 * p + 1], (CHUNK, LANES))
    right = jnp.broadcast_to(tile[:, 2 * p + 1 : 2 * p + 2], (CHUNK, LANES))
    return left, right, jnp.where(first, left, right)


def stack_heads(tile, first):
    zero = jnp.zeros_like(tile)
    return jnp.concatenate([jnp.where(first, tile, zero), jnp.where(first, zero, tile)], axis=0)


def scan_chunk(c, r):
    rows = chunk_rows(c)
    row, col = tile_iotas()
    down, across, carried, to_end, carry_on = segment_parts(c, r)
    masks = masks_back(c, r, down)
    maps = []
    for half in range(2):
        pre = conv_tile(c, r.bc, r.bc_at + half * LANES, r.cbw, r.cbb, half * LANES, masks)
        r.pre_bc[rows, half * LANES : (half + 1) * LANES] = pre
        maps.append((pre * sigmoid(pre)).astype(BF16))
    b_map, c_map = maps
    r.maps[rows, :LANES] = b_map
    r.maps[rows, LANES:] = c_map
    scores = jnp.where((down == across) & (row >= col), dot_nt(c_map, b_map), 0.0)
    b_turned = b_map.T
    total = r.total[rows, :]
    step = r.step[rows, :]
    first = col < HEADDIM
    for p in range(r.pairs):
        lanes = slice(p * LANES, (p + 1) * LANES)
        pre = conv_tile(c, r.xr, r.xr_at + p * LANES, r.cxw, r.cxb, p * LANES, masks)
        r.pre_x[rows, lanes] = pre
        chan = pre * sigmoid(pre)
        left, right, both = pair_columns(total, p, first)
        _, _, step_pair = pair_columns(step, p, first)
        fed = step_pair * chan
        stacked = stack_heads(fed.astype(BF16), first)
        mixing = []
        for k, mine in enumerate((left, right)):
            other = r.total_t[pl.ds(c * 16 + 2 * p + k, 1), :]
            mixing.append((scores * jnp.exp2(jnp.minimum(mine - other, 0.0))).astype(BF16))
        within = dot_nn(jnp.concatenate(mixing, axis=1), stacked)
        state = r.state[:, lanes]
        state_low = state.astype(BF16)
        r.states[rows, lanes] = state_low
        decay_in = jnp.exp2(both) * carried
        r.y[rows, lanes] = (
            within + decay_in * dot_nn(c_map, state_low) + r.skip[0:1, lanes] * chan
        )
        last = both[CHUNK - 1 : CHUNK, :]
        decay_out = jnp.exp2(last - both) * to_end
        r.state[:, lanes] = (jnp.exp2(last) * carry_on) * state + dot_nn(
            b_turned, (decay_out * fed).astype(BF16)
        )


def scan_chunk_back(c, r):
    rows = chunk_rows(c)
    row, col = tile_iotas()
    down, across, carried, to_end, carry_on = segment_parts(c, r)
    ahead = masks_ahead(c, r, down)
    b_map = r.maps[rows, :LANES]
    c_map = r.maps[rows, LANES:]
    visible = (down == across) & (row <= col)
    scores = jnp.where(visible, dot_nt(b_map, c_map), 0.0)
    c_turned = c_map.T
    total = r.total[rows, :]
    step = r.step[rows, :]
    first = col < HEADDIM
    d_scores = jnp.zeros((CHUNK, LANES), F32)
    width = r.pairs * LANES
    for p in range(r.pairs):
        lanes = slice(p * LANES, (p + 1) * LANES)
        lows = slice(width + p * LANES, width + (p + 1) * LANES)
        gy_low = r.gy[rows, lanes]
        gy = gy_low.astype(F32)
        pre = r.pre_x[rows, lanes]
        gate = sigmoid(pre)
        chan = pre * gate
        left, right, both = pair_columns(total, p, first)
        _, _, step_pair = pair_columns(step, p, first)
        fed = step_pair * chan
        fed_low = fed.astype(BF16)
        d_mixing = dot_nt(stack_heads(fed_low, first), gy_low)
        mixing = []
        for k, mine in enumerate((left, right)):
            other = r.total_t[pl.ds(c * 16 + 2 * p + k, 1), :]
            decay = jnp.exp2(jnp.minimum(other - mine, 0.0))
            mixing.append((scores * decay).astype(BF16))
            d_scores = d_scores + d_mixing[k * CHUNK : (k + 1) * CHUNK] * decay
        d_state = r.d_state[:, lanes]
        d_state_low = d_state.astype(BF16)
        last = both[CHUNK - 1 : CHUNK, :]
        decay_out = jnp.exp2(last - both) * to_end
        from_state = decay_out * dot_nn(b_map, d_state_low)
        d_fed = dot_nn(jnp.concatenate(mixing, axis=1), stack_heads(gy_low, first)) + from_state
        fed_held = fed_low.astype(F32)
        skip = r.skip[0:1, lanes]
        flow = gy * (r.y[rows, lanes] - skip * chan) - fed_held * d_fed
        direct = chan * d_fed
        for k, part in enumerate((flow, direct)):
            spot = slice(k * CHUNK, (k + 1) * CHUNK)
            r.sums[spot, lanes], r.sums[spot, lows] = split_two(part)
        keep = jnp.exp2(last) * carry_on
        through = jnp.sum(fed_held * from_state, axis=0, keepdims=True) + keep * jnp.sum(
            r.states[rows, lanes].astype(F32) * d_state, axis=0, keepdims=True
        )
        spot = slice(2 * CHUNK, 2 * CHUNK + 16)
        r.sums[spot, lanes], r.sums[spot, lows] = split_two(
            jnp.broadcast_to(through, (16, LANES))
        )
        grad_in = (jnp.exp2(both) * carried * gy).astype(BF16)
        r.grad_in[:, lanes] = grad_in
        r.fed_out[:, lanes] = (decay_out * fed).astype(BF16)
        r.d_state_low[:, lanes] = d_state_low
        r.d_state[:, lanes] = keep * d_state + dot_nn(c_turned, grad_in)
        d_chan = skip * gy + step_pair * d_fed
        r.g_skip[:, lanes] += fold_rows(gy * chan)
        d_pre = d_chan * (gate * (1.0 + pre * (1.0 - gate)))
        conv_back(c, r, d_pre, r.d_pre_x, r.xr, r.xr_at, r.cxw, p * LANES, ahead, r.dx_at, r.g_cxw, r.g_cxb)
    d_scores_low = jnp.where(visible, d_scores, 0.0).astype(BF16)
    d_b = dot_nn(d_scores_low, c_map) + dot_nt(r.fed_out[...], r.d_state_low[...])
    d_c = dot_tn(d_scores_low, b_map) + dot_nt(r.grad_in[...], r.states[rows, :])
    for half, d_map in enumerate((d_b, d_c)):
        pre = r.pre_bc[rows, half * LANES : (half + 1) * LANES]
        gate = sigmoid(pre)
        d_pre = d_map * (gate * (1.0 + pre * (1.0 - gate)))
        conv_back(
            c, r, d_pre, r.d_pre_bc, r.bc, r.bc_at, r.cbw, half * LANES, ahead, r.dbc_at, r.g_cbw, r.g_cbb
        )
    reduced = dot_nn(r.sums[...], r.head_sum[...])
    d_total = jnp.dot(
        (row <= col).astype(F32), reduced[:CHUNK], precision=exact, preferred_element_type=F32
    ) + reduced[2 * CHUNK : 2 * CHUNK + 1]
    a_neg = -jnp.exp(r.a_log[...])
    d_step = reduced[CHUNK : 2 * CHUNK] + a_neg * d_total
    r.g_alog[...] += fold_rows(step * d_total) * a_neg
    d_raw = d_step * sigmoid(r.dtr[rows, r.dtr_at : r.dtr_at + LANES] + r.dt_bias[...])
    r.g_dtb[...] += fold_rows(d_raw)
    r.d_proj[rows, r.ddt_at : r.ddt_at + LANES] = d_raw.astype(BF16)


def conv_back(c, r, d_pre, held, raw, raw_at, weight, at, ahead, out_at, g_w, g_b):
    lanes = slice(at, at + LANES)
    rows = chunk_rows(c)
    held[CHUNK : CHUNK + 8, lanes] = held[0:8, lanes]
    held[0:CHUNK, lanes] = d_pre
    window = held[:, lanes]
    values = raw[rows, raw_at + at : raw_at + at + LANES]
    g_b[:, lanes] += fold_rows(d_pre)
    g_w[24:32, lanes] += fold_rows(d_pre * values)
    d_raw = d_pre * weight[3:4, lanes]
    for j in range(1, 4):
        shifted = pltpu.roll(window, CHUNK + 8 - j, 0)[:CHUNK] * ahead[j - 1]
        d_raw = d_raw + shifted * weight[3 - j : 4 - j, lanes]
        g_w[(3 - j) * 8 : (4 - j) * 8, lanes] += fold_rows(shifted * values)
    r.d_proj[rows, out_at + at : out_at + at + LANES] = d_raw.astype(BF16)


def head_sum_matrix(width):
    shape = (2 * width, LANES)
    lane = lax.broadcasted_iota(jnp.int32, shape, 0)
    lane = jnp.where(lane >= width, lane - width, lane)
    return (lane // HEADDIM == lax.broadcasted_iota(jnp.int32, shape, 1)).astype(BF16)


def layout_of(width):
    return types.SimpleNamespace(
        x=width, bc=2 * width, dt=2 * width + 2 * NSTATE, all=2 * width + 2 * NSTATE + LANES
    )


SMALL_IN = ("seg_down", "seg_across", "cxw", "cxb", "cbw", "cbb", "a_log", "dt_bias", "skip")


def small_inputs(segments, cxw, cxb, cbw, cbb, a_log, dt_bias, d_skip):
    tokens = segments.shape[0]
    seg = segments.astype(F32)
    edge = jnp.full((8,), -1.0, F32)
    down = jnp.broadcast_to(jnp.concatenate([edge, seg, edge])[:, None], (tokens + 16, LANES))
    heads = a_log.shape[0]
    pad = lambda v: jnp.pad(v, (0, LANES - heads))[None, :]
    return (
        down,
        seg.reshape(tokens // CHUNK, CHUNK),
        cxw,
        cxb[None, :],
        cbw,
        cbb[None, :],
        pad(a_log),
        pad(dt_bias),
        jnp.repeat(d_skip, HEADDIM)[None, :],
    )


def forward_kernel(*refs, names, width):
    r = types.SimpleNamespace(**dict(zip(names, refs)))
    at = layout_of(width)
    r.pairs = width // LANES
    r.xr = r.bc = r.dtr = r.proj
    r.xr_at, r.bc_at, r.dtr_at = at.x, at.bc, at.dt
    chunks = r.proj.shape[0] // CHUNK
    r.state[...] = jnp.zeros_like(r.state)

    def body(c, carry):
        prepare_steps(c, r)
        scan_chunk(c, r)
        return carry

    lax.fori_loop(0, chunks, body, 0)


def backward_kernel(*refs, names, width):
    r = types.SimpleNamespace(**dict(zip(names, refs)))
    at = layout_of(width)
    r.pairs = width // LANES
    r.xr = r.bc = r.dtr = r.proj
    r.xr_at, r.bc_at, r.dtr_at = at.x, at.bc, at.dt
    r.dx_at, r.dbc_at, r.ddt_at = 0, width, width + 2 * NSTATE
    start_back(r)
    chunks = r.proj.shape[0] // CHUNK

    def body(i, carry):
        scan_chunk_back(chunks - 1 - i, r)
        return carry

    lax.fori_loop(0, chunks, body, 0)


def start_back(r):
    for ref in (r.d_state, r.d_pre_x, r.d_pre_bc, r.g_cxw, r.g_cxb, r.g_cbw, r.g_cbb):
        ref[...] = jnp.zeros_like(ref)
    for ref in (r.g_skip, r.g_alog, r.g_dtb):
        ref[...] = jnp.zeros_like(ref)
    r.head_sum[...] = head_sum_matrix(r.pairs * LANES)


def call_local(kernel, width, ins, outs, scratch, values, flops):
    names = tuple(ins) + tuple(outs) + tuple(scratch)
    whole = pl.BlockSpec(memory_space=pltpu.VMEM)
    return pl.pallas_call(
        functools.partial(kernel, names=names, width=width),
        out_shape=tuple(jax.ShapeDtypeStruct(*spec) for spec in outs.values()),
        in_specs=[whole] * len(ins),
        out_specs=tuple([whole] * len(outs)),
        scratch_shapes=[pltpu.VMEM(*spec) for spec in scratch.values()],
        compiler_params=pltpu.CompilerParams(vmem_limit_bytes=VMEM_LIMIT),
        cost_estimate=pl.CostEstimate(flops=flops, bytes_accessed=1 << 24, transcendentals=0),
    )(*values)


def mixer_forward(projected, small, width):
    tokens = projected.shape[0]
    outs = dict(
        y=((tokens, width), F32),
        pre_x=((tokens, width), F32),
        pre_bc=((tokens, 2 * NSTATE), F32),
        maps=((tokens, 2 * NSTATE), BF16),
        states=((tokens, width), BF16),
        step=((tokens, LANES), F32),
        total=((tokens, LANES), F32),
        total_t=((tokens // CHUNK * 16, LANES), F32),
    )
    scratch = dict(state=((NSTATE, width), F32))
    return call_local(
        forward_kernel, width, ("proj",) + SMALL_IN, outs, scratch, (projected,) + small, 10**10
    )


BACK_SCRATCH = lambda width: dict(
    d_state=((NSTATE, width), F32),
    d_state_low=((NSTATE, width), BF16),
    grad_in=((CHUNK, width), BF16),
    fed_out=((CHUNK, width), BF16),
    sums=((2 * CHUNK + 16, 2 * width), BF16),
    head_sum=((2 * width, LANES), BF16),
    d_pre_x=((CHUNK + 8, width), F32),
    d_pre_bc=((CHUNK + 8, 2 * NSTATE), F32),
)
GRAD_OUT = lambda width: dict(
    g_cxw=((32, width), F32),
    g_cxb=((8, width), F32),
    g_cbw=((32, 2 * NSTATE), F32),
    g_cbb=((8, 2 * NSTATE), F32),
    g_skip=((8, width), F32),
    g_alog=((8, LANES), F32),
    g_dtb=((8, LANES), F32),
)


def mixer_backward(projected, small, saved, gy, width):
    tokens = projected.shape[0]
    outs = dict(d_proj=((tokens, width + 2 * NSTATE + LANES), BF16), **GRAD_OUT(width))
    ins = ("proj",) + SMALL_IN
    ins = ins + ("y", "pre_x", "pre_bc", "maps", "states", "step", "total", "total_t", "gy")
    return call_local(
        backward_kernel,
        width,
        ins,
        outs,
        BACK_SCRATCH(width),
        (projected,) + small + tuple(saved) + (gy,),
        3 * 10**10,
    )


def on_device(
    x_in,
    segments,
    pre_gain,
    w_z,
    w_x,
    w_bc,
    w_dt,
    conv_x_w,
    conv_x_b,
    conv_bc_w,
    conv_bc_b,
    a_log,
    dt_bias,
    d_skip,
    gate_gain,
    w_out,
    cotangent,
):
    width = w_z.shape[1]
    heads = a_log.shape[0]
    at = layout_of(width)
    values = x_in.astype(F32)
    scale = lax.rsqrt(jnp.mean(values * values, axis=1) + EPS)
    normed = (values * scale[:, None] * pre_gain[None, :]).astype(BF16)
    row_normed = lax.all_gather(normed, "tensor", axis=0, tiled=True)
    mine = jnp.concatenate(
        (w_z, w_x, w_bc, jnp.pad(w_dt, ((0, 0), (0, LANES - heads)))), axis=1
    )
    stacked = lax.all_gather(mine, "dp", axis=0, tiled=True)
    full_out = lax.all_gather(w_out.T, "dp", axis=0, tiled=True)
    projected = jnp.dot(row_normed, stacked, preferred_element_type=F32)
    small = small_inputs(
        segments, conv_x_w, conv_x_b, conv_bc_w, conv_bc_b, a_log, dt_bias, d_skip
    )
    saved = mixer_forward(projected, small, width)
    y = saved[0]
    z_raw = projected[:, :width]
    gate = sigmoid(z_raw)
    gated = y * (z_raw * gate)
    inner_total = width * lax.axis_size("tensor")
    row_cot = lax.all_gather(cotangent, "tensor", axis=0, tiled=True)
    d_mixed = dot_nn(row_cot, full_out)
    weighted = d_mixed * gate_gain[None, :]
    squares, cross = lax.psum(
        (jnp.sum(gated * gated, axis=1), jnp.sum(weighted * gated, axis=1)), "tensor"
    )
    scale_two = lax.rsqrt(squares / inner_total + EPS)
    mixed = (gated * scale_two[:, None] * gate_gain[None, :]).astype(BF16)
    branch = lax.psum_scatter(
        dot_nt(mixed, full_out).astype(BF16), "tensor", scatter_dimension=0, tiled=True
    ).astype(F32)
    block_out = (values + branch).astype(BF16)
    grad_gate_part = jnp.sum(d_mixed * gated * scale_two[:, None], axis=0)
    d_gated = (
        scale_two[:, None] * weighted
        - gated * (scale_two * scale_two * scale_two * cross / inner_total)[:, None]
    )
    gy = (d_gated * (z_raw * gate)).astype(BF16)
    d_z = (d_gated * y * (gate * (1.0 + z_raw * (1.0 - gate)))).astype(BF16)
    d_rest, g_cxw, g_cxb, g_cbw, g_cbb, g_skip, g_alog, g_dtb = mixer_backward(
        projected, small, saved, gy, width
    )
    d_proj = jnp.concatenate((d_z, d_rest), axis=1)
    d_normed = lax.psum_scatter(
        dot_nt(d_proj, stacked).astype(BF16), "tensor", scatter_dimension=0, tiled=True
    ).astype(F32)
    proj_part = dot_tn(row_normed, d_proj)
    out_part = dot_tn(row_cot, mixed)
    owned = lax.psum_scatter(
        jnp.concatenate((proj_part, out_part), axis=1).astype(BF16),
        "dp",
        scatter_dimension=0,
        tiled=True,
    ).astype(F32)
    grad_w_bc = lax.psum(owned[:, at.bc : at.dt].astype(BF16), "tensor").astype(F32)
    pre_weighted = d_normed * pre_gain[None, :]
    grad_pre_part = jnp.sum(d_normed * values * scale[:, None], axis=0)
    feature_sum = jnp.sum(pre_weighted * values, axis=1)
    grad_x = (
        cotangent.astype(F32)
        + scale[:, None] * pre_weighted
        - values * (scale * scale * scale * feature_sum / values.shape[1])[:, None]
    ).astype(BF16)
    over_taps = lambda v: jnp.sum(v.reshape(4, 8, v.shape[1]), axis=1)
    over_rows = lambda v: jnp.sum(v, axis=0)
    grad_gate_gain, grad_cxw, grad_cxb, grad_alog, grad_dtb, grad_skip = lax.psum(
        (
            grad_gate_part,
            over_taps(g_cxw),
            over_rows(g_cxb),
            over_rows(g_alog)[:heads],
            over_rows(g_dtb)[:heads],
            jnp.sum(over_rows(g_skip).reshape(heads, HEADDIM), axis=1),
        ),
        "dp",
    )
    grad_pre_gain, grad_cbw, grad_cbb = lax.psum(
        (grad_pre_part, over_taps(g_cbw), over_rows(g_cbb)), ("dp", "tensor")
    )
    return (
        block_out,
        grad_x,
        grad_pre_gain,
        owned[:, :width],
        owned[:, width : at.bc],
        grad_w_bc,
        owned[:, at.dt : at.dt + heads],
        grad_cxw,
        grad_cxb,
        grad_cbw,
        grad_cbb,
        grad_alog,
        grad_dtb,
        grad_skip,
        grad_gate_gain,
        owned[:, at.all :].T,
    )


def solution(mesh):
    tokens = P(("dp", "tensor"), None)
    both = P("dp", "tensor")
    heads = P("tensor")
    return jax.shard_map(
        on_device,
        mesh=mesh,
        in_specs=(
            tokens,
            P("dp"),
            P(),
            both,
            both,
            P("dp", None),
            both,
            P(None, "tensor"),
            heads,
            P(),
            P(),
            heads,
            heads,
            heads,
            heads,
            P("tensor", "dp"),
            tokens,
        ),
        out_specs=(
            tokens,
            tokens,
            P(),
            both,
            both,
            P("dp", None),
            both,
            P(None, "tensor"),
            heads,
            P(),
            P(),
            heads,
            heads,
            heads,
            heads,
            P("tensor", "dp"),
        ),
        check_vma=False,
    )
```

profile of v0, /device:TPU:0, one launch (start us, length us, event | category | flops | bytes accessed | tf_op | source)
XLA Modules:
  0.0 493.3 jit_solution(11177077352580560727)
XLA Ops:
  7.3 1.5 fusion.6
  8.8 2.3 fusion.8
  11.3 0.9 fusion.14
  16.1 41.8 %all-gather.5.cloned.1.call-done = bf16[1024,1536]{1,0:T(8,128)(2,1)} async-done(((bf16[256,1536]{1,0:T(8,128)(2,1)}), bf16[1024,1536]{1,0:T(8,128)(2,1)}) %all-gather.5.cloned.1.call-update) | async-done | bytes 3145744 | tf_op jit(solution)/shard_map/all_gather | solution.py:442
  57.9 63.8 %all-gather.7.cloned.1.call-done = bf16[1536,1920]{1,0:T(8,128)(2,1)} async-done(((bf16[192,1920]{1,0:T(8,128)(2,1)}), bf16[1536,1920]{1,0:T(8,128)(2,1)}) %all-gather.7.cloned.1.call-update) | async-done | bytes 5898256 | tf_op jit(solution)/shard_map/all_gather | solution.py:446
  121.7 11.9 %fusion.24.refs_0_ = f32[1024,1920]{1,0:T(8,128)} fusion(bf16[1024,1536]{1,0:T(8,128)(2,1)} %all-gather.5.cloned.1.call-done, bf16[1536,1920]{1,0:T(8,128)(2,1)} %all-gather.7.cloned.1.call-done), kind=kOutput, calls=%fused_computation.55 | convolution fusion | flops 6039797760 | bytes 16908288 | tf_op jit(solution)/shard_map/dot_general | solution.py:448
  133.6 1.0 broadcast_in_dim.12.refs_1_
  134.6 17.4 %shard_map.288 = (f32[1024,768]{1,0:T(8,128)}, f32[1024,768]{1,0:T(8,128)}, f32[1024,256]{1,0:T(8,128)}, bf16[1024,256]{1,0:T(8,128)(2,1)}, bf16[1024,768]{1,0:T...) custom-call(f32[1024,1920]{1,0:T(8,128)} %fusion.24.refs_0_, ...), custom_call_target="tpu_custom_call" | custom-call | flops 10000000000 | bytes 16777216 | tf_op jit(solution)/shard_map/pallas_call | solution.py:351
  151.9 3.8 multiply_reduce_fusion.2
  155.8 9.9 %psum.84 = f32[1024]{0:T(1024)S(1)} all-reduce(f32[1024]{0:T(1024)S(1)} %get-tuple-element.93), channel_id=1, replica_groups=mesh['dp'=8,'tensor'=4] {'tensor'}, use_global_device_ids=true, to_apply=%region_2.3 | all-reduce | flops 1024 | bytes 8192 | tf_op jit(solution)/shard_map/psum | solution.py:461
  165.7 32.7 %all-gather.11.cloned.1.call-done = bf16[1024,1536]{1,0:T(8,128)(2,1)} async-done(((bf16[256,1536]{1,0:T(8,128)(2,1)}), bf16[1024,1536]{1,0:T(8,128)(2,1)}) %all-gather.11.cloned.1.call-update) | async-done | bytes 3145744 | tf_op jit(solution)/shard_map/all_gather | solution.py:458
  198.5 7.1 %multiply_reduce_fusion = (f32[768]{0:T(1024)S(1)}, f32[1024]{0:T(1024)S(1)}, f32[1024,768]{1,0:T(8,128)}) fusion(f32[1024,768]{1,0:T(8,128)S(1)} %get-tuple-element.94, f32[1024]{0:T(1024)S(1)} %add_rsqrt_fusion, f32[768]{0:T(1024)S(1)} %copy-done.22, bf16[1024,1536]{1,0:T(8,128)(2,1)} %all-gather.11.cloned.1.call-done, ...), kind=kOutput, calls=%fused_computation.12 | convolution fusion | flops 2420635904 | bytes 11810816 | tf_op jit(solution)/shard_map/dot_general | solution.py:24
  205.5 8.9 %psum.85 = f32[1024]{0:T(1024)S(1)} all-reduce(f32[1024]{0:T(1024)S(1)} %get-tuple-element.81), channel_id=1, replica_groups=mesh['dp'=8,'tensor'=4] {'tensor'}, use_global_device_ids=true, to_apply=%region_5.6 | all-reduce | flops 1024 | bytes 8192 | tf_op jit(solution)/shard_map/psum | solution.py:461
  214.5 5.9 %multiply_convert_fusion.1 = (bf16[1024,768]{1,0:T(8,128)(2,1)}, bf16[1024,768]{1,0:T(8,128)(2,1)}) fusion(f32[1024,768]{1,0:T(8,128)} %get-tuple-element.32.refs_10_, f32[1024,1920]{1,0:T(8,128)} %fusion.24.refs_0_, f32[1024,768]{1,0:T(8,128)S(1)} %get-tuple-element.94, f32[1024]{0:T(1024)S(1)} %fusion.17, f32[1024,768]{1,0:T(8,128)} %get-tuple-element.103, ...), kind=kLoop, calls=%fused_computation.14 | loop fusion | flops 13369344 | bytes 15739904 | tf_op jit(solution)/shard_map/convert_element_type | solution.py:476
  220.3 27.3 %shard_map.289 = (bf16[1024,1152]{1,0:T(8,128)(2,1)}, f32[32,768]{1,0:T(8,128)}, f32[8,768]{1,0:T(8,128)}, f32[32,256]{1,0:T(8,128)}, f32[8,256]{1,0:T(8,128)}, ...) custom-call(f32[1024,1920]{1,0:T(8,128)} %fusion.24.refs_0_, f32[1040,128]{1,0:T(8,128)} %broadcast_in_dim.12.refs_1_, ...), custom_call_target="tpu_custom_call" | custom-call | flops 30000001024 | bytes 16777216 | tf_op jit(solution)/shard_map/pallas_call | solution.py:351
  247.6 10.8 %convolution_convert_fusion.1 = bf16[1024,1536]{1,0:T(8,128)(2,1)} fusion(bf16[1536,1920]{1,0:T(8,128)(2,1)} %all-gather.7.cloned.1.call-done, bf16[1024,1152]{1,0:T(8,128)(2,1)} %get-tuple-element.40, bf16[1024,768]{1,0:T(8,128)(2,1)S(1)} %copy-done.6), kind=kOutput, calls=%fused_computation.3 | convolution fusion | flops 6049234944 | bytes 12976128 | tf_op jit(solution)/shard_map/dot_general | solution.py:28
  258.5 1.8 copy-done.2
  260.3 5.9 %convolution_convert_fusion.2 = bf16[1024,1536]{1,0:T(8,128)(2,1)} fusion(bf16[1536,768]{1,0:T(8,128)(2,1)} %all-gather.9.cloned.1.call-done, f32[1024,768]{1,0:T(8,128)S(1)} %copy-done.2, f32[768]{0:T(1024)S(1)} %copy-done.22, f32[1024]{0:T(1024)S(1)} %add_rsqrt_fusion), kind=kOutput, calls=%fused_computation.4 | convolution fusion | flops 2419851264 | bytes 8657920 | tf_op jit(solution)/shard_map/dot_general | solution.py:28
  266.5 6.2 %fusion.1 = bf16[1536,768]{1,0:T(8,128)(2,1)} fusion(bf16[1024,1536]{1,0:T(8,128)(2,1)} %all-gather.11.cloned.1.call-done, f32[1024,768]{1,0:T(8,128)S(1)} %copy-done.2, f32[768]{0:T(1024)S(1)} %copy-done.22, f32[1024]{0:T(1024)S(1)} %add_rsqrt_fusion), kind=kOutput, calls=%fused_computation.21 | convolution fusion | flops 2419458048 | bytes 8657920 | tf_op jit(solution)/shard_map/dot_general | solution.py:32
  272.8 8.6 %convolution_convert_fusion = bf16[1536,1920]{1,0:T(8,128)(2,1)} fusion(bf16[1024,1536]{1,0:T(8,128)(2,1)S(1)} %copy-done.26, bf16[1024,1152]{1,0:T(8,128)(2,1)S(1)} %copy-done.27, bf16[1024,768]{1,0:T(8,128)(2,1)S(1)} %copy-done.7), kind=kOutput, calls=%fused_computation.1 | convolution fusion | flops 6050611200 | bytes 12976128 | tf_op jit(solution)/shard_map/dot_general | solution.py:32
  281.4 6.5 %pad_maximum_fusion = bf16[1536,2688]{1,0:T(8,128)(2,1)} fusion(bf16[1536,768]{1,0:T(8,128)(2,1)S(1)} %copy-done.5, bf16[1536,1920]{1,0:T(8,128)(2,1)} %convolution_convert_fusion), kind=kLoop, calls=%fused_computation | loop fusion | flops 16515072 | bytes 16515072 | tf_op jit(solution)/shard_map/concatenate | solution.py:487
  289.0 27.6 %all-reduce.4 = (f32[4,768]{1,0:T(4,128)}, f32[768]{0:T(1024)}, f32[12]{0:T(128)}, f32[12]{0:T(128)}, f32[12]{0:T(128)}, /*index=5*/f32[768]{0:T(1024)}) all-reduce(f32[4,768]{1,0:T(4,128)S(1)} %bitcast_reduce_fusion, f32[768]{0:T(1024)S(1)} %reduce_sum.132, f32[12]{0:T(128)S(1)} %bitcast.27, ...), channel_id=1, replica_groups=mesh['dp'=8,'tensor'=4] {'dp'}, use_global_device_ids=true, to_apply=%region_13.14 | all-reduce | flops 4644 | bytes 37152 | tf_op jit(solution)/shard_map/psum | solution.py:503
  316.7 1.6 fusion.12
  318.3 37.2 %all-reduce.3 = (f32[1536]{0:T(1024)}, f32[4,256]{1,0:T(4,128)}, f32[256]{0:T(256)}) all-reduce(f32[1536]{0:T(1024)S(1)} %get-tuple-element.82, f32[4,256]{1,0:T(4,128)S(1)} %bitcast_reduce_fusion.1, f32[256]{0:T(256)S(1)} %reduce_sum.134), channel_id=1, replica_groups=mesh['dp'=8,'tensor'=4] {'dp','tensor'}, use_global_device_ids=true, to_apply=%region_9.10 | all-reduce | flops 2816 | bytes 22528 | tf_op jit(solution)/shard_map/psum | solution.py:514
  355.6 3.1 fusion.5
  358.7 82.1 %reduce-scatter.8.cloned.1.call-done = bf16[192,2688]{1,0:T(8,128)(2,1)} async-done(((bf16[1536,2688]{1,0:T(8,128)(2,1)}), bf16[192,2688]{1,0:T(8,128)(2,1)}) %reduce-scatter.8.cloned.1.call-update) | async-done | bytes 1032208 | tf_op jit(solution)/shard_map/reduce_scatter | solution.py:486
  440.9 1.6 slice.36
  442.5 2.1 fusion.23
  444.8 0.9 slice_bitcast_fusion
  445.7 0.7 copy.42
  446.4 38.5 %all-reduce.7.cloned.1.call-done = bf16[192,256]{1,0:T(8,128)(2,1)} async-done(((bf16[192,256]{1,0:T(8,128)(2,1)}), bf16[192,256]{1,0:T(8,128)(2,1)}) %all-reduce.7.cloned.1.call-update) | async-done | bytes 98320 | tf_op jit(solution)/shard_map/psum | solution.py:492
  484.8 1.6 convert_element_type.66
  (97 shorter events, 5.7 us)
Async XLA Ops:
  7.2 3.9 copy-start.16
  7.2 4.1 copy-start.10
  7.2 4.1 copy-start.8
  7.2 4.1 copy-start.9
  7.2 6.4 %copy-start.19 = (f32[768]{0:T(1024)S(1)}, f32[768]{0:T(1024)}, u32[]{:S(2)}) copy-start(f32[768]{0:T(1024)} %param.25) | copy-start | bytes 9220
  7.2 6.9 %copy-start.23 = (f32[12]{0:T(128)S(1)}, f32[12]{0:T(128)}, u32[]{:S(2)}) copy-start(f32[12]{0:T(128)} %param.30) | copy-start | bytes 148
  7.2 7.7 %copy-start.18 = (s32[1024]{0:T(1024)S(1)}, s32[1024]{0:T(1024)}, u32[]{:S(2)}) copy-start(s32[1024]{0:T(1024)} %param.18) | copy-start | bytes 12292
  7.3 8.3 %copy-start.24 = (f32[12]{0:T(128)S(1)}, f32[12]{0:T(128)}, u32[]{:S(2)}) copy-start(f32[12]{0:T(128)} %param.29) | copy-start | bytes 148
  7.3 8.3 %copy-start.25 = (f32[12]{0:T(128)S(1)}, f32[12]{0:T(128)}, u32[]{:S(2)}) copy-start(f32[12]{0:T(128)} %param.28) | copy-start | bytes 148
  7.3 50.6 %all-gather.5.cloned.1.call-start = ((), (), s32[]{:S(2)}) async-start(), calls=%async_computation.3 | async-start | bytes 3932160 | tf_op jit(solution)/shard_map/all_gather | solution.py:442
  11.1 110.6 %all-gather.7.cloned.1.call-start = ((), (), s32[]{:S(2)}) async-start(), calls=%async_computation.4 | async-start | bytes 6635520 | tf_op jit(solution)/shard_map/all_gather | solution.py:446
  12.2 153.5 %all-gather.9.cloned.1.call-start = ((), (), s32[]{:S(2)}) async-start(), calls=%async_computation.5 | async-start | bytes 2654208 | tf_op jit(solution)/shard_map/all_gather | solution.py:447
  13.0 185.5 %all-gather.11.cloned.1.call-start = ((), (), s32[]{:S(2)}) async-start(), calls=%async_computation.7 | async-start | bytes 3932160 | tf_op jit(solution)/shard_map/all_gather | solution.py:458
  13.5 303.1 %reduce-scatter.6.cloned.1.call-start = ((), (), s32[]{:S(2)}) async-start(), calls=%async_computation.8 | async-start | bytes 3932160 | tf_op jit(solution)/shard_map/reduce_scatter | solution.py:481
  151.9 46.5 %copy-start.22 = (f32[768]{0:T(1024)S(1)}, f32[768]{0:T(1024)}, u32[]{:S(2)}) copy-start(f32[768]{0:T(1024)} %param.31) | copy-start | bytes 9220
  155.7 58.7 %copy-start.1 = (f32[1024,768]{1,0:T(8,128)}, f32[1024,768]{1,0:T(8,128)S(1)}, u32[]{:S(2)}) copy-start(f32[1024,768]{1,0:T(8,128)S(1)} %get-tuple-element.94) | copy-start | bytes 9437188
  220.3 27.3 %copy-start.6 = (bf16[1024,768]{1,0:T(8,128)(2,1)S(1)}, bf16[1024,768]{1,0:T(8,128)(2,1)}, u32[]{:S(2)}) copy-start(bf16[1024,768]{1,0:T(8,128)(2,1)} %get-tuple-element.95) | copy-start | bytes 4718596
  258.4 1.9 copy-start.2
  258.4 97.2 %reduce-scatter.4.cloned.1.call-start = ((), (), s32[]{:S(2)}) async-start(), calls=%async_computation.6 | async-start | bytes 3932160 | tf_op jit(solution)/shard_map/reduce_scatter | solution.py:466
  266.2 174.6 %reduce-scatter.8.cloned.1.call-start = ((), (), s32[]{:S(2)}) async-start(), calls=%async_computation.9 | async-start | bytes 9289728 | tf_op jit(solution)/shard_map/reduce_scatter | solution.py:486
  266.5 6.3 %copy-start.7 = (bf16[1024,768]{1,0:T(8,128)(2,1)S(1)}, bf16[1024,768]{1,0:T(8,128)(2,1)}, u32[]{:S(2)}) copy-start(bf16[1024,768]{1,0:T(8,128)(2,1)} %get-tuple-element.95) | copy-start | bytes 4718596
  266.5 6.2 %copy-start.26 = (bf16[1024,1536]{1,0:T(8,128)(2,1)S(1)}, bf16[1024,1536]{1,0:T(8,128)(2,1)}, u32[]{:S(2)}) copy-start(bf16[1024,1536]{1,0:T(8,128)(2,1)} %all-gather.5.cloned.1.call-done) | copy-start | bytes 9437188
  266.5 6.2 %copy-start.27 = (bf16[1024,1152]{1,0:T(8,128)(2,1)S(1)}, bf16[1024,1152]{1,0:T(8,128)(2,1)}, u32[]{:S(2)}) copy-start(bf16[1024,1152]{1,0:T(8,128)(2,1)} %get-tuple-element.40) | copy-start | bytes 7077892
  272.8 8.6 %copy-start.5 = (bf16[1536,768]{1,0:T(8,128)(2,1)S(1)}, bf16[1536,768]{1,0:T(8,128)(2,1)}, u32[]{:S(2)}) copy-start(bf16[1536,768]{1,0:T(8,128)(2,1)} %fusion.1) | copy-start | bytes 7077892
  287.9 0.8 copy-start.14
  287.9 1.0 copy-start.11
  288.0 28.7 %copy-start.13 = (f32[32,256]{1,0:T(8,128)S(1)}, f32[32,256]{1,0:T(8,128)}, u32[]{:S(2)}) copy-start(f32[32,256]{1,0:T(8,128)} %get-tuple-element.43) | copy-start | bytes 98308
  288.0 28.7 %copy-start = (bf16[256,1536]{1,0:T(8,128)(2,1)S(1)}, bf16[256,1536]{1,0:T(8,128)(2,1)}, u32[]{:S(2)}) copy-start(bf16[256,1536]{1,0:T(8,128)(2,1)} %param.17) | copy-start | bytes 2359300
  288.0 28.7 %copy-start.12 = (f32[1536]{0:T(1024)S(1)}, f32[1536]{0:T(1024)}, u32[]{:S(2)}) copy-start(f32[1536]{0:T(1024)} %param.19) | copy-start | bytes 18436
  288.0 67.6 %copy-start.4 = (bf16[256,1536]{1,0:T(8,128)(2,1)S(1)}, bf16[256,1536]{1,0:T(8,128)(2,1)}, u32[]{:S(2)}) copy-start(bf16[256,1536]{1,0:T(8,128)(2,1)} %param.33) | copy-start | bytes 2359300
  288.0 196.8 %all-reduce.7.cloned.1.call-start = ((), (), s32[]{:S(2)}) async-start(), calls=%async_computation.10 | async-start | bytes 196608 | tf_op jit(solution)/shard_map/psum | solution.py:492
  440.9 3.8 copy-start.3
  (4 other events, 2.9 us)
Sparse Core Ops, SparseCore 0:
  11.2 46.6 all-gather.4
  60.1 61.4 all-gather.6
  123.3 30.2 all-gather.8
  155.3 43.0 all-gather.10
  258.5 43.9 reduce-scatter.5
  305.4 44.7 reduce-scatter.3
  352.5 88.3 reduce-scatter.7
  444.6 40.1 all-reduce.6
where the time goes:
time: 494 us; the launch traced here: 493 us
  waiting for transfers between devices  260 us (53%)
  blocking collectives  83.7 us (17%)
  matrix products  50.5 us (10%)
  Pallas kernels  44.7 us (9%)
  other arithmetic  28.2 us (6%)
  between operations  14.5 us (3%)
  local copies, waits for them, and re-layouts  10.9 us (2%)
    reduce_scatter x1, waiting for transfers between devices, on_device(): lax.psum_scatter(jnp.concatenate((proj_part, out_part), axis=1).astype(BF...  82.1 us
    all_gather x1, waiting for transfers between devices, on_device(): stacked = lax.all_gather(mine, 'dp', axis=0, tiled=True)  63.8 us
    pallas_call x2, Pallas kernels, call_local(): pl.pallas_call(functools.partial(kernel, names=names, width=width), out_s...  44.7 us
    all_gather x1, waiting for transfers between devices, on_device(): row_normed = lax.all_gather(normed, 'tensor', axis=0, tiled=True)  41.8 us
    psum x1, waiting for transfers between devices, on_device(): lax.psum(owned[:, at.bc:at.dt].astype(BF16), 'tensor').astype(F32)  38.5 us
    psum x1, blocking collectives, on_device(): lax.psum((grad_pre_part, over_taps(g_cbw), over_rows(g_cbb)), ('dp', 'ten...  37.2 us
    all_gather x1, waiting for transfers between devices, on_device(): row_cot = lax.all_gather(cotangent, 'tensor', axis=0, tiled=True)  32.7 us
    psum x1, blocking collectives, on_device(): lax.psum((grad_gate_part, over_taps(g_cxw), over_rows(g_cxb), over_rows(g...  27.6 us
  transfers between devices with their start and end apart: 8, of which 5 were waited for; matrix products, arithmetic and copies ran while one was open for 11% of the time, Pallas kernels for 4%

commit v1 on v0

--- a/solution.py
+++ b/solution.py
@@ -303,13 +303,20 @@
     )
 
 
+def take_projections(r, width):
+    r.pairs = width // LANES
+    if hasattr(r, "proj"):
+        at = layout_of(width)
+        r.xr = r.bc = r.dtr = r.proj
+        r.xr_at, r.bc_at, r.dtr_at = at.x, at.bc, at.dt
+    else:
+        r.xr_at = r.bc_at = r.dtr_at = 0
+
+
 def forward_kernel(*refs, names, width):
     r = types.SimpleNamespace(**dict(zip(names, refs)))
-    at = layout_of(width)
-    r.pairs = width // LANES
-    r.xr = r.bc = r.dtr = r.proj
-    r.xr_at, r.bc_at, r.dtr_at = at.x, at.bc, at.dt
-    chunks = r.proj.shape[0] // CHUNK
+    take_projections(r, width)
+    chunks = r.dtr.shape[0] // CHUNK
     r.state[...] = jnp.zeros_like(r.state)
 
     def body(c, carry):
@@ -322,13 +329,10 @@
 
 def backward_kernel(*refs, names, width):
     r = types.SimpleNamespace(**dict(zip(names, refs)))
-    at = layout_of(width)
-    r.pairs = width // LANES
-    r.xr = r.bc = r.dtr = r.proj
-    r.xr_at, r.bc_at, r.dtr_at = at.x, at.bc, at.dt
+    take_projections(r, width)
     r.dx_at, r.dbc_at, r.ddt_at = 0, width, width + 2 * NSTATE
     start_back(r)
-    chunks = r.proj.shape[0] // CHUNK
+    chunks = r.dtr.shape[0] // CHUNK
 
     def body(i, carry):
         scan_chunk_back(chunks - 1 - i, r)
@@ -398,19 +402,445 @@
 )
 
 
+SAVED = ("y", "pre_x", "pre_bc", "maps", "states", "step", "total", "total_t")
+
+
 def mixer_backward(projected, small, saved, gy, width):
-    tokens = projected.shape[0]
+    tokens = gy.shape[0]
     outs = dict(d_proj=((tokens, width + 2 * NSTATE + LANES), BF16), **GRAD_OUT(width))
-    ins = ("proj",) + SMALL_IN
-    ins = ins + ("y", "pre_x", "pre_bc", "maps", "states", "step", "total", "total_t", "gy")
+    ins = (("proj",) if len(projected) == 1 else ("xr", "bc", "dtr")) + SMALL_IN
+    ins = ins + SAVED + ("gy",)
     return call_local(
         backward_kernel,
         width,
         ins,
         outs,
         BACK_SCRATCH(width),
-        (projected,) + small + tuple(saved) + (gy,),
+        tuple(projected) + small + tuple(saved) + (gy,),
         3 * 10**10,
+    )
+
+
+LAST_Z = 3
+UP, DOWN, PAIR_LOW, PAIR_HIGH = range(4)
+
+
+def place():
+    dp = lax.axis_index("dp")
+    tp = lax.axis_index("tensor")
+    z = dp // 2
+    core = dp - 2 * z
+    x = lax.rem(tp, 2)
+    y = tp // 2
+    near_x = y * 2 + (1 - x)
+    near_y = (1 - y) * 2 + x
+    across = (1 - y) * 2 + (1 - x)
+    return types.SimpleNamespace(
+        dp=dp,
+        tp=tp,
+        z=z,
+        core=core,
+        mate=dp + 1 - 2 * core,
+        near_x=near_x,
+        near_y=near_y,
+        across=across,
+    )
+
+
+def device(w, dp=None, tp=None):
+    return {"dp": w.dp if dp is None else dp, "tensor": w.tp if tp is None else tp}
+
+
+def greet(w):
+    barrier = pltpu.get_barrier_semaphore()
+
+    def tell(**where):
+        pl.semaphore_signal(
+            barrier, inc=1, device_id=device(w, **where), device_id_type=pl.DeviceIdType.MESH
+        )
+
+    tell(dp=w.mate)
+    tell(tp=w.near_x)
+    tell(tp=w.near_y)
+    tell(tp=w.across)
+    pl.when(w.z < LAST_Z)(lambda: tell(dp=w.dp + 2))
+    pl.when(w.z > 0)(lambda: tell(dp=w.dp - 2))
+    below = (w.z + LAST_Z - 1) // LAST_Z
+    above = (2 * LAST_Z - 1 - w.z) // LAST_Z
+    pl.semaphore_wait(barrier, 4 + below + above)
+
+
+def remote(src, dst, send, recv, where):
+    return pltpu.make_async_remote_copy(
+        src_ref=src,
+        dst_ref=dst,
+        send_sem=send,
+        recv_sem=recv,
+        device_id=where,
+        device_id_type=pl.DeviceIdType.MESH,
+    )
+
+
+class LineGather:
+    def __init__(self, w, ref, send, recv):
+        self.w, self.ref, self.send, self.recv = w, ref, send, recv
+        self.rows = ref.shape[0] // (2 * (LAST_Z + 1))
+
+    def shard(self, z, core):
+        start = pl.multiple_of((z * 2 + core) * self.rows, 16)
+        return self.ref.at[pl.ds(start, self.rows)]
+
+    def copy(self, z, step, kind):
+        w = self.w
+        part = self.shard(z, w.core)
+        to = {UP: w.dp + 2, DOWN: w.dp - 2}.get(kind, w.mate)
+        return remote(
+            part,
+            part,
+            self.send.at[step, kind],
+            self.recv.at[z * 2 + w.core],
+            device(w, dp=to),
+        )
+
+    def arrived(self, z, core):
+        part = self.shard(z, core)
+        remote(
+            part, part, self.send.at[0, 0], self.recv.at[z * 2 + core], device(self.w)
+        ).wait_recv()
+
+    def relay(self, step, act=None):
+        w = self.w
+
+        def low():
+            z = w.z - step
+            if act is None and step > 0:
+                self.arrived(z, w.core)
+            do = act or (lambda copy: copy.start())
+            pl.when(w.z < LAST_Z)(lambda: do(self.copy(z, step, UP)))
+            do(self.copy(z, step, PAIR_LOW))
+            if step == 0:
+                pl.when(w.z > 0)(lambda: do(self.copy(z, step, DOWN)))
+
+        def high():
+            z = w.z + step
+            if act is None:
+                self.arrived(z, w.core)
+            do = act or (lambda copy: copy.start())
+            pl.when(w.z > 0)(lambda: do(self.copy(z, step, DOWN)))
+            do(self.copy(z, step, PAIR_HIGH))
+
+        if step == 0:
+            low()
+        else:
+            pl.when(w.z >= step)(low)
+            pl.when(w.z <= LAST_Z - step)(high)
+
+    def finish(self):
+        for z in range(LAST_Z + 1):
+            self.arrived(z, 1 - self.w.core)
+
+    def drain(self):
+        for step in range(LAST_Z + 1):
+            self.relay(step, lambda copy: copy.wait_send())
+
+
+class RowGather:
+    def __init__(self, w, ref, send, recv):
+        self.w, self.ref, self.send, self.recv = w, ref, send, recv
+        self.rows = ref.shape[0] // 4
+
+    def block(self, slot, half=None):
+        rows = self.rows if half is None else self.rows // 2
+        start = slot * self.rows + (0 if half is None else half * rows)
+        return self.ref.at[pl.ds(pl.multiple_of(start, 16), rows)]
+
+    def copy(self, i):
+        w = self.w
+        part, to = (
+            (self.block(w.tp), w.near_x),
+            (self.block(w.tp), w.near_y),
+            (self.block(w.near_x, 0), w.near_y),
+            (self.block(w.near_y, 1), w.near_x),
+        )[i]
+        return remote(part, part, self.send.at[i], self.recv.at[i], device(w, tp=to))
+
+    def start(self):
+        for i in range(2):
+            self.copy(i).start()
+
+    def hand_on(self):
+        for i in range(2):
+            self.copy(i).wait_recv()
+            self.copy(i + 2).start()
+
+    def finish(self):
+        for i in range(2, 4):
+            self.copy(i).wait_recv()
+
+    def drain(self):
+        for i in range(4):
+            self.copy(i).wait_send()
+
+
+def norm_rows(x_ref, gain_ref, out_ref, start):
+    rows = 64
+
+    def body(i, carry):
+        here = pl.ds(pl.multiple_of(i * rows, rows), rows)
+        values = x_ref[here, :].astype(F32)
+        scale = lax.rsqrt(jnp.mean(values * values, axis=1, keepdims=True) + EPS)
+        there = pl.ds(pl.multiple_of(start + i * rows, 16), rows)
+        out_ref[there, :] = (values * scale * gain_ref[...]).astype(BF16)
+        return carry
+
+    lax.fori_loop(0, x_ref.shape[0] // rows, body, 0)
+
+
+def by_rows(total, rows, body):
+    def step(i, carry):
+        body(pl.ds(pl.multiple_of(i * rows, rows), rows))
+        return carry
+
+    lax.fori_loop(0, total // rows, step, 0)
+
+
+def gate_chunk(c, r):
+    rows = chunk_rows(c)
+    square = jnp.zeros((CHUNK, LANES), F32)
+    cross = jnp.zeros((CHUNK, LANES), F32)
+    for p in range(r.pairs):
+        lanes = slice(p * LANES, (p + 1) * LANES)
+        z = r.z[rows, lanes]
+        gated = r.y[rows, lanes] * (z * sigmoid(z))
+        square = square + gated * gated
+        cross = cross + r.d_mixed[rows, lanes] * r.gain[0:1, lanes] * gated
+    half = r.parts.shape[1] // 2
+    mine = r.parts.at[r.w.tp]
+    mine[pl.ds(c, 1), :] = jnp.sum(square.T, axis=0, keepdims=True)
+    mine[pl.ds(half + c, 1), :] = jnp.sum(cross.T, axis=0, keepdims=True)
+
+
+class SumExchange:
+    def __init__(self, w, ref, send, recv):
+        self.w, self.ref, self.send, self.recv = w, ref, send, recv
+
+    def copies(self):
+        w = self.w
+        mine = self.ref.at[w.tp]
+        return [
+            remote(mine, mine, self.send.at[i], self.recv.at[i], device(w, tp=to))
+            for i, to in enumerate((w.near_x, w.near_y, w.across))
+        ]
+
+    def start(self):
+        for copy in self.copies():
+            copy.start()
+
+    def finish(self):
+        for copy in self.copies():
+            copy.wait()
+
+
+def phase_one(r):
+    w = r.w
+    width = r.pairs * LANES
+    tokens = r.row_normed.shape[0]
+    chunks = tokens // CHUNK
+    own = pl.ds(pl.multiple_of(w.dp * r.w_x.shape[0], 16), r.w_x.shape[0])
+    r.full_x[own, :width] = r.w_x[...]
+    r.full_x[own, width : width + 2 * NSTATE] = r.w_bc[...]
+    r.full_x[own, width + 2 * NSTATE :] = r.w_dt[...]
+    r.full_out[own, :] = r.w_out[...]
+    r.full_z[own, :] = r.w_z[...]
+    shard_x = LineGather(w, r.full_x, r.send_w.at[0], r.recv_w.at[0])
+    shard_out = LineGather(w, r.full_out, r.send_w.at[1], r.recv_w.at[1])
+    shard_z = LineGather(w, r.full_z, r.send_w.at[2], r.recv_w.at[2])
+    row_n = RowGather(w, r.row_normed, r.send_r.at[0], r.recv_r.at[0])
+    row_c = RowGather(w, r.row_cot, r.send_r.at[1], r.recv_r.at[1])
+    sums = SumExchange(w, r.parts, r.send_s, r.recv_s)
+    block = r.x_in.shape[0]
+    start = pl.multiple_of(w.tp * block, block)
+    greet(w)
+    shard_x.relay(0)
+    norm_rows(r.x_in, r.pre_gain, r.row_normed, start)
+    row_n.start()
+    r.row_cot[pl.ds(start, block), :] = r.cot[...]
+    r.state[...] = jnp.zeros_like(r.state)
+    shard_x.relay(1)
+    row_n.hand_on()
+    row_c.start()
+    shard_x.relay(2)
+    shard_x.relay(3)
+    shard_out.relay(0)
+    row_n.finish()
+    shard_x.finish()
+    shard_out.relay(1)
+
+    def project_x(rows):
+        out = dot_nn(r.row_normed[rows, :], r.full_x[...])
+        r.xr[rows, :] = out[:, :width]
+        r.bc[rows, :] = out[:, width : width + 2 * NSTATE]
+        r.dtr[rows, :] = out[:, width + 2 * NSTATE :]
+
+    by_rows(tokens, 256, project_x)
+    shard_out.relay(2)
+
+    def body(c, carry):
+        prepare_steps(c, r)
+        scan_chunk(c, r)
+
+        @pl.when(c == 1)
+        def _():
+            shard_out.relay(3)
+            shard_z.relay(0)
+
+        @pl.when(c == 3)
+        def _():
+            shard_z.relay(1)
+            row_c.hand_on()
+
+        @pl.when(c == 5)
+        def _():
+            shard_z.relay(2)
+
+        return carry
+
+    lax.fori_loop(0, chunks, body, 0)
+    shard_z.relay(3)
+    row_c.finish()
+    shard_out.finish()
+
+    def mix_back(rows):
+        r.d_mixed[rows, :] = dot_nn(r.row_cot[rows, :], r.full_out[...])
+
+    by_rows(tokens, 256, mix_back)
+    shard_z.finish()
+
+    def project_z(rows):
+        r.z[rows, :] = dot_nn(r.row_normed[rows, :], r.full_z[...])
+
+    by_rows(tokens, 256, project_z)
+
+    def gate(c, carry):
+        gate_chunk(c, r)
+        return carry
+
+    lax.fori_loop(0, chunks, gate, 0)
+    sums.start()
+    for item in (shard_x, shard_out, shard_z, row_n, row_c):
+        item.drain()
+    sums.finish()
+
+
+ONE_IN = ("x_in", "pre_gain", "w_z", "w_x", "w_bc", "w_dt", "w_out", "gain", "cot") + SMALL_IN
+ONE_OUT = lambda tokens, features, width: dict(
+    row_normed=((tokens, features), BF16),
+    row_cot=((tokens, features), BF16),
+    full_x=((features, width + 2 * NSTATE + LANES), BF16),
+    full_z=((features, width), BF16),
+    full_out=((features, width), BF16),
+    z=((tokens, width), F32),
+    xr=((tokens, width), F32),
+    bc=((tokens, 2 * NSTATE), F32),
+    dtr=((tokens, LANES), F32),
+    y=((tokens, width), F32),
+    pre_x=((tokens, width), F32),
+    pre_bc=((tokens, 2 * NSTATE), F32),
+    maps=((tokens, 2 * NSTATE), BF16),
+    states=((tokens, width), BF16),
+    step=((tokens, LANES), F32),
+    total=((tokens, LANES), F32),
+    total_t=((tokens // CHUNK * 16, LANES), F32),
+    d_mixed=((tokens, width), F32),
+    parts=((4, 2 * (tokens // CHUNK), LANES), F32),
+)
+
+
+def one_kernel(*refs, names, width):
+    r = types.SimpleNamespace(**dict(zip(names, refs)))
+    r.w = place()
+    r.pairs = width // LANES
+    r.xr_at = r.bc_at = r.dtr_at = 0
+    phase_one(r)
+
+
+def gather_forward(args, small, width):
+    x_in, pre_gain, w_z, w_x, w_bc, w_dt, w_out, gate_gain, cotangent = args
+    features = x_in.shape[1]
+    tokens = x_in.shape[0] * 4
+    outs = ONE_OUT(tokens, features, width)
+    scratch = dict(state=((NSTATE, width), F32))
+    names = ONE_IN + tuple(outs) + tuple(scratch)
+    names = names + ("send_w", "recv_w", "send_r", "recv_r", "send_s", "recv_s")
+    values = (
+        x_in,
+        pre_gain[None, :],
+        w_z,
+        w_x,
+        w_bc,
+        jnp.pad(w_dt, ((0, 0), (0, LANES - w_dt.shape[1]))),
+        w_out.T,
+        gate_gain[None, :],
+        cotangent,
+    )
+    whole = pl.BlockSpec(memory_space=pltpu.VMEM)
+    dma = pltpu.SemaphoreType.DMA
+    out = pl.pallas_call(
+        functools.partial(one_kernel, names=names, width=width),
+        out_shape=tuple(jax.ShapeDtypeStruct(*spec) for spec in outs.values()),
+        in_specs=[whole] * len(ONE_IN),
+        out_specs=tuple([whole] * len(outs)),
+        scratch_shapes=[pltpu.VMEM(*spec) for spec in scratch.values()]
+        + [dma((3, 4, 4)), dma((3, 8)), dma((2, 4)), dma((2, 4)), dma((3,)), dma((3,))],
+        compiler_params=pltpu.CompilerParams(
+            vmem_limit_bytes=VMEM_LIMIT, collective_id=0, has_side_effects=True
+        ),
+        cost_estimate=pl.CostEstimate(
+            flops=2 * 10**10, bytes_accessed=1 << 26, transcendentals=0
+        ),
+    )(*values, *small)
+    return types.SimpleNamespace(**dict(zip(outs, out)))
+
+
+def forward_plain(args, small, width):
+    x_in, pre_gain, w_z, w_x, w_bc, w_dt, w_out, gate_gain, cotangent = args
+    heads = w_dt.shape[1]
+    at = layout_of(width)
+    values = x_in.astype(F32)
+    scale = lax.rsqrt(jnp.mean(values * values, axis=1) + EPS)
+    normed = (values * scale[:, None] * pre_gain[None, :]).astype(BF16)
+    row_normed = lax.all_gather(normed, "tensor", axis=0, tiled=True)
+    mine = jnp.concatenate(
+        (w_z, w_x, w_bc, jnp.pad(w_dt, ((0, 0), (0, LANES - heads)))), axis=1
+    )
+    stacked = lax.all_gather(mine, "dp", axis=0, tiled=True)
+    full_out = lax.all_gather(w_out.T, "dp", axis=0, tiled=True)
+    projected = jnp.dot(row_normed, stacked, preferred_element_type=F32)
+    saved = mixer_forward(projected, small, width)
+    row_cot = lax.all_gather(cotangent, "tensor", axis=0, tiled=True)
+    y = saved[0]
+    z_raw = projected[:, :width]
+    gated = y * (z_raw * sigmoid(z_raw))
+    d_mixed = dot_nn(row_cot, full_out)
+    squares, cross = lax.psum(
+        (
+            jnp.sum(gated * gated, axis=1),
+            jnp.sum(d_mixed * gate_gain[None, :] * gated, axis=1),
+        ),
+        "tensor",
+    )
+    return types.SimpleNamespace(
+        row_normed=row_normed,
+        row_cot=row_cot,
+        full_z=stacked[:, :width],
+        full_x=stacked[:, width:],
+        full_out=full_out,
+        z=z_raw,
+        projected=(projected,),
+        saved=saved,
+        d_mixed=d_mixed,
+        squares=squares,
+        cross=cross,
     )
 
 
@@ -436,35 +866,29 @@
     width = w_z.shape[1]
     heads = a_log.shape[0]
     at = layout_of(width)
+    small = small_inputs(
+        segments, conv_x_w, conv_x_b, conv_bc_w, conv_bc_b, a_log, dt_bias, d_skip
+    )
+    args = (x_in, pre_gain, w_z, w_x, w_bc, w_dt, w_out, gate_gain, cotangent)
+    if lax.axis_size("dp") == 2 * (LAST_Z + 1) and lax.axis_size("tensor") == 4:
+        f = gather_forward(args, small, width)
+        f.projected = (f.xr, f.bc, f.dtr)
+        f.saved = tuple(getattr(f, name) for name in SAVED)
+        squares, cross = jnp.sum(f.parts, axis=0).reshape(2, -1)
+    else:
+        f = forward_plain(args, small, width)
+        squares, cross = f.squares, f.cross
+    y, z_raw, d_mixed = f.saved[0], f.z, f.d_mixed
     values = x_in.astype(F32)
     scale = lax.rsqrt(jnp.mean(values * values, axis=1) + EPS)
-    normed = (values * scale[:, None] * pre_gain[None, :]).astype(BF16)
-    row_normed = lax.all_gather(normed, "tensor", axis=0, tiled=True)
-    mine = jnp.concatenate(
-        (w_z, w_x, w_bc, jnp.pad(w_dt, ((0, 0), (0, LANES - heads)))), axis=1
-    )
-    stacked = lax.all_gather(mine, "dp", axis=0, tiled=True)
-    full_out = lax.all_gather(w_out.T, "dp", axis=0, tiled=True)
-    projected = jnp.dot(row_normed, stacked, preferred_element_type=F32)
-    small = small_inputs(
-        segments, conv_x_w, conv_x_b, conv_bc_w, conv_bc_b, a_log, dt_bias, d_skip
-    )
-    saved = mixer_forward(projected, small, width)
-    y = saved[0]
-    z_raw = projected[:, :width]
     gate = sigmoid(z_raw)
     gated = y * (z_raw * gate)
     inner_total = width * lax.axis_size("tensor")
-    row_cot = lax.all_gather(cotangent, "tensor", axis=0, tiled=True)
-    d_mixed = dot_nn(row_cot, full_out)
     weighted = d_mixed * gate_gain[None, :]
-    squares, cross = lax.psum(
-        (jnp.sum(gated * gated, axis=1), jnp.sum(weighted * gated, axis=1)), "tensor"
-    )
     scale_two = lax.rsqrt(squares / inner_total + EPS)
     mixed = (gated * scale_two[:, None] * gate_gain[None, :]).astype(BF16)
     branch = lax.psum_scatter(
-        dot_nt(mixed, full_out).astype(BF16), "tensor", scatter_dimension=0, tiled=True
+        dot_nt(mixed, f.full_out).astype(BF16), "tensor", scatter_dimension=0, tiled=True
     ).astype(F32)
     block_out = (values + branch).astype(BF16)
     grad_gate_part = jnp.sum(d_mixed * gated * scale_two[:, None], axis=0)
@@ -475,14 +899,17 @@
     gy = (d_gated * (z_raw * gate)).astype(BF16)
     d_z = (d_gated * y * (gate * (1.0 + z_raw * (1.0 - gate)))).astype(BF16)
     d_rest, g_cxw, g_cxb, g_cbw, g_cbb, g_skip, g_alog, g_dtb = mixer_backward(
-        projected, small, saved, gy, width
+        f.projected, small, f.saved, gy, width
     )
     d_proj = jnp.concatenate((d_z, d_rest), axis=1)
     d_normed = lax.psum_scatter(
-        dot_nt(d_proj, stacked).astype(BF16), "tensor", scatter_dimension=0, tiled=True
+        (dot_nt(d_z, f.full_z) + dot_nt(d_rest, f.full_x)).astype(BF16),
+        "tensor",
+        scatter_dimension=0,
+        tiled=True,
     ).astype(F32)
-    proj_part = dot_tn(row_normed, d_proj)
-    out_part = dot_tn(row_cot, mixed)
+    proj_part = dot_tn(f.row_normed, d_proj)
+    out_part = dot_tn(f.row_cot, mixed)
     owned = lax.psum_scatter(
         jnp.concatenate((proj_part, out_part), axis=1).astype(BF16),
         "dp",

time: 494 us -> 404 us (0.82)
  waiting for transfers between devices: 260 us -> 121 us
  Pallas kernels: 44.7 us -> 133 us
  blocking collectives: 83.7 us -> 64 us
  matrix products: 50.5 us -> 34.5 us
  other arithmetic: 28.2 us -> 22.9 us
    all_gather x4 -> x0, waiting for transfers between devices: 138 us -> none  [the longest x1 63.8 us: on_device(): stacked = lax.all_gather(mine, 'dp', axis=0, tiled=True)]
    pallas_call x0 -> x1, Pallas kernels: none -> 106 us  [gather_forward(): pl.pallas_call(functools.partial(one_kernel, names=names, width=width), o...]
    dot_general x2 -> x0, matrix products: 19 us -> none  [the longest x1 11.9 us: on_device(): projected = jnp.dot(row_normed, stacked, preferred_element_type=F32)]
    psum x2 -> x0, blocking collectives: 18.9 us -> none  [on_device(): lax.psum((jnp.sum(gated * gated, axis=1), jnp.sum(weighted * gated, axis=...]
    pallas_call x2 -> x1, Pallas kernels: 44.7 us -> 26.5 us  [call_local(): pl.pallas_call(functools.partial(kernel, names=names, width=width), out_s...]
    dot_general x2 -> x3, matrix products: 16.7 us -> 20.7 us  [dot_nt(): lax.dot_general(a, b, (((1,), (1,)), ((), ())), preferred_element_type=F32)]
  transfers between devices with their start and end apart: 8 -> 4, of which waited for: 5 -> 2; matrix products, arithmetic and copies ran while one was open for 11% -> 9% of each run, Pallas kernels for 4% -> 0%
where the time goes in v1:
time: 404 us
  Pallas kernels  133 us (33%)
  waiting for transfers between devices  121 us (30%)
  blocking collectives  64 us (16%)
  matrix products  34.5 us (9%)
  other arithmetic  22.9 us (6%)
  between operations  14 us (3%)
  local copies, waits for them, and re-layouts  13.9 us (3%)
    pallas_call x1, Pallas kernels, gather_forward(): pl.pallas_call(functools.partial(one_kernel, names=names, width=width), o...  106 us
    reduce_scatter x1, waiting for transfers between devices, on_device(): lax.psum_scatter(jnp.concatenate((proj_part, out_part), axis=1).astype(BF...  82.9 us
    psum x1, waiting for transfers between devices, on_device(): lax.psum(owned[:, at.bc:at.dt].astype(BF16), 'tensor').astype(F32)  38.1 us
    psum x1, blocking collectives, on_device(): lax.psum((grad_pre_part, over_taps(g_cbw), over_rows(g_cbb)), ('dp', 'ten...  37.4 us
    psum x1, blocking collectives, on_device(): lax.psum((grad_gate_part, over_taps(g_cxw), over_rows(g_cxb), over_rows(g...  26.6 us
    pallas_call x1, Pallas kernels, call_local(): pl.pallas_call(functools.partial(kernel, names=names, width=width), out_s...  26.5 us
    dot_general x3, matrix products, dot_nt(): lax.dot_general(a, b, (((1,), (1,)), ((), ())), preferred_element_type=F32)  20.7 us
    dot_general x2, matrix products, dot_tn(): lax.dot_general(a, b, (((0,), (0,)), ((), ())), preferred_element_type=F32)  13.8 us
  transfers between devices with their start and end apart: 4, of which 2 were waited for; matrix products, arithmetic and copies ran while one was open for 9% of the time, Pallas kernels for 0%

profile of v1, /device:TPU:0, one launch (start us, length us, event | category | flops | bytes accessed | tf_op | source)
XLA Modules:
  0.0 403.6 jit_solution(16652613721173873699)
XLA Ops:
  7.2 1.3 convert_bitcast_fusion
  8.5 0.7 broadcast_in_dim.44
  9.2 0.7 broadcast_in_dim_reshape.3.refs_17_.refs_11_
  9.9 1.3 broadcast_in_dim.19.refs_12_.refs_6_
  11.2 0.8 copy.36
  12.0 1.3 broadcast_in_dim.16.refs_1_
  13.3 1.3 broadcast_in_dim.17.refs_7_
  14.6 1.2 pad_bitcast_fusion
  15.8 0.6 pad.11.refs_5_
  16.4 1.0 broadcast_in_dim.18.refs_9_.refs_3_
  17.4 106.2 %shard_map.288 = (bf16[1024,1536]{1,0:T(8,128)(2,1)}, bf16[1024,1536]{1,0:T(8,128)(2,1)}, bf16[1536,1152]{1,0:T(8,128)(2,1)}, bf16[1536,768]{1,0:T(8,128)(2,1)},...) custom-call(bf16[256,1536]{1,0:T(8,128)(2,1)} %refs_0_.1, ...), custom_call_target="tpu_custom_call" | custom-call | flops 20000000000 | bytes 67108864 | tf_op jit(solution)/shard_map/pallas_call | solution.py:788
  123.6 0.8 reduce_sum.117
  124.5 6.2 %multiply_convert_fusion = (bf16[1024,768]{1,0:T(8,128)(2,1)}, bf16[1024,768]{1,0:T(8,128)(2,1)S(1)}, f32[768]{0:T(1024)S(1)}, bf16[1024,768]{1,0:T(8,128)(2,1)S(1)}) fusion(f32[1024]{0:T(1024)S(1)} %fusion.14, f32[1024,768]{1,0:T(8,128)} %get-tuple-element.47, f32[768]{0:T(1024)S(1)} %copy-done.11, f32[1024]{0:T(1024)S(1)} %fusion.17, ...), kind=kLoop, calls=%fused_computation.9 | loop fusion | flops 18873600 | bytes 14170112 | tf_op jit(solution)/shard_map/convert_element_type | solution.py:899
  130.7 4.6 %fusion.22 = f32[1024,1536]{1,0:T(8,128)} fusion(bf16[1024,768]{1,0:T(8,128)(2,1)S(1)} %get-tuple-element.114, bf16[1536,768]{1,0:T(8,128)(2,1)S(1)} %copy-done.15), kind=kOutput, calls=%fused_computation.50 | convolution fusion | flops 2415919104 | bytes 10223616 | tf_op jit(solution)/shard_map/dot_general | solution.py:28
  135.2 26.5 %shard_map.289 = (bf16[1024,1152]{1,0:T(8,128)(2,1)}, f32[32,768]{1,0:T(8,128)}, f32[8,768]{1,0:T(8,128)}, f32[32,256]{1,0:T(8,128)}, f32[8,256]{1,0:T(8,128)}, ...) custom-call(f32[1024,768]{1,0:T(8,128)} %get-tuple-element.49.refs_0_, ...), custom_call_target="tpu_custom_call" | custom-call | flops 30000001024 | bytes 16777216 | tf_op jit(solution)/shard_map/pallas_call | solution.py:355
  161.8 10.5 %add_convert_fusion = bf16[1024,1536]{1,0:T(8,128)(2,1)} fusion(f32[1024,1536]{1,0:T(8,128)} %fusion.22, bf16[1024,1152]{1,0:T(8,128)(2,1)} %get-tuple-element.59, bf16[1536,1152]{1,0:T(8,128)(2,1)} %get-tuple-element.60), kind=kOutput, calls=%fused_computation.2 | convolution fusion | flops 3627024384 | bytes 15335424 | tf_op jit(solution)/shard_map/dot_general | solution.py:28
  172.5 5.7 %convolution_convert_fusion.1 = bf16[1024,1536]{1,0:T(8,128)(2,1)} fusion(bf16[1024,768]{1,0:T(8,128)(2,1)S(1)} %get-tuple-element.116, bf16[1536,768]{1,0:T(8,128)(2,1)} %get-tuple-element.46), kind=kOutput, calls=%fused_computation.6 | convolution fusion | flops 2417491968 | bytes 7077888 | tf_op jit(solution)/shard_map/dot_general | solution.py:28
  178.3 5.2 %convolution_convert_fusion.2 = bf16[1536,768]{1,0:T(8,128)(2,1)S(1)} fusion(bf16[1024,1536]{1,0:T(8,128)(2,1)} %get-tuple-element.62, bf16[1024,768]{1,0:T(8,128)(2,1)} %copy-done.4), kind=kOutput, calls=%fused_computation.7 | convolution fusion | flops 2417098752 | bytes 7077888 | tf_op jit(solution)/shard_map/dot_general | solution.py:32
  183.5 8.6 %convolution_convert_fusion = bf16[1536,1920]{1,0:T(8,128)(2,1)} fusion(bf16[1024,1536]{1,0:T(8,128)(2,1)S(1)} %copy-done.16, bf16[1024,1152]{1,0:T(8,128)(2,1)S(1)} %copy-done.17, bf16[1024,768]{1,0:T(8,128)(2,1)S(1)} %copy-done.3), kind=kOutput, calls=%fused_computation.1 | convolution fusion | flops 6050611200 | bytes 12976128 | tf_op jit(solution)/shard_map/dot_general | solution.py:32
  192.1 6.5 %pad_maximum_fusion = bf16[1536,2688]{1,0:T(8,128)(2,1)} fusion(bf16[1536,768]{1,0:T(8,128)(2,1)S(1)} %convolution_convert_fusion.2, bf16[1536,1920]{1,0:T(8,128)(2,1)} %convolution_convert_fusion), kind=kLoop, calls=%fused_computation | loop fusion | flops 16515072 | bytes 16515072 | tf_op jit(solution)/shard_map/concatenate | solution.py:914
  199.7 26.6 %all-reduce.4 = (f32[4,768]{1,0:T(4,128)}, f32[768]{0:T(1024)}, f32[12]{0:T(128)}, f32[12]{0:T(128)}, f32[12]{0:T(128)}, /*index=5*/f32[768]{0:T(1024)}) all-reduce(f32[4,768]{1,0:T(4,128)S(1)} %bitcast_reduce_fusion, f32[768]{0:T(1024)S(1)} %reduce_sum.122, f32[12]{0:T(128)S(1)} %bitcast.33, ...), channel_id=1, replica_groups=mesh['dp'=8,'tensor'=4] {'dp'}, use_global_device_ids=true, to_apply=%region_10.11 | all-reduce | flops 4644 | bytes 37152 | tf_op jit(solution)/shard_map/psum | solution.py:930
  226.6 1.6 fusion.12
  228.2 37.4 %all-reduce.3 = (f32[1536]{0:T(1024)}, f32[4,256]{1,0:T(4,128)}, f32[256]{0:T(256)}) all-reduce(f32[1536]{0:T(1024)S(1)} %get-tuple-element.102, f32[4,256]{1,0:T(4,128)S(1)} %bitcast_reduce_fusion.1, f32[256]{0:T(256)S(1)} %reduce_sum.124), channel_id=1, replica_groups=mesh['dp'=8,'tensor'=4] {'dp','tensor'}, use_global_device_ids=true, to_apply=%region_6.7 | all-reduce | flops 2816 | bytes 22528 | tf_op jit(solution)/shard_map/psum | solution.py:941
  265.6 3.1 fusion.7
  268.8 82.9 %reduce-scatter.8.cloned.1.call-done = bf16[192,2688]{1,0:T(8,128)(2,1)} async-done(((bf16[1536,2688]{1,0:T(8,128)(2,1)}), bf16[192,2688]{1,0:T(8,128)(2,1)}) %reduce-scatter.8.cloned.1.call-update) | async-done | bytes 1032208 | tf_op jit(solution)/shard_map/reduce_scatter | solution.py:913
  351.7 1.6 slice.33
  353.4 1.4 convert_element_type.61
  354.7 1.1 fusion.21
  355.8 0.9 slice_bitcast_fusion
  356.7 0.7 copy.38
  357.4 38.1 %all-reduce.7.cloned.1.call-done = bf16[192,256]{1,0:T(8,128)(2,1)} async-done(((bf16[192,256]{1,0:T(8,128)(2,1)}), bf16[192,256]{1,0:T(8,128)(2,1)}) %all-reduce.7.cloned.1.call-update) | async-done | bytes 98320 | tf_op jit(solution)/shard_map/psum | solution.py:919
  395.5 1.6 convert_element_type.62
  (63 shorter events, 1.8 us)
Async XLA Ops:
  7.2 219.4 %reduce-scatter.6.cloned.1.call-start = ((), (), s32[]{:S(2)}) async-start(), calls=%async_computation.4 | async-start | bytes 3932160 | tf_op jit(solution)/shard_map/reduce_scatter | solution.py:905
  17.4 107.0 %copy-start.11 = (f32[768]{0:T(1024)S(1)}, f32[768]{0:T(1024)}, u32[]{:S(2)}) copy-start(f32[768]{0:T(1024)} %param.31) | copy-start | bytes 9220
  124.4 6.2 %copy-start.15 = (bf16[1536,768]{1,0:T(8,128)(2,1)S(1)}, bf16[1536,768]{1,0:T(8,128)(2,1)}, u32[]{:S(2)}) copy-start(bf16[1536,768]{1,0:T(8,128)(2,1)} %get-tuple-element.48) | copy-start | bytes 7077892
  130.6 4.6 %copy-start.2 = (bf16[1024,768]{1,0:T(8,128)(2,1)}, bf16[1024,768]{1,0:T(8,128)(2,1)S(1)}, u32[]{:S(2)}) copy-start(bf16[1024,768]{1,0:T(8,128)(2,1)S(1)} %get-tuple-element.114) | copy-start | bytes 4718596
  130.6 41.8 %copy-start.4 = (bf16[1024,768]{1,0:T(8,128)(2,1)}, bf16[1024,768]{1,0:T(8,128)(2,1)S(1)}, u32[]{:S(2)}) copy-start(bf16[1024,768]{1,0:T(8,128)(2,1)S(1)} %get-tuple-element.116) | copy-start | bytes 4718596
  172.2 93.4 %reduce-scatter.4.cloned.1.call-start = ((), (), s32[]{:S(2)}) async-start(), calls=%async_computation.3 | async-start | bytes 3932160 | tf_op jit(solution)/shard_map/reduce_scatter | solution.py:890
  178.2 173.5 %reduce-scatter.8.cloned.1.call-start = ((), (), s32[]{:S(2)}) async-start(), calls=%async_computation.5 | async-start | bytes 9289728 | tf_op jit(solution)/shard_map/reduce_scatter | solution.py:913
  178.2 5.2 %copy-start.3 = (bf16[1024,768]{1,0:T(8,128)(2,1)S(1)}, bf16[1024,768]{1,0:T(8,128)(2,1)}, u32[]{:S(2)}) copy-start(bf16[1024,768]{1,0:T(8,128)(2,1)} %copy-done.2) | copy-start | bytes 4718596
  178.3 5.2 %copy-start.16 = (bf16[1024,1536]{1,0:T(8,128)(2,1)S(1)}, bf16[1024,1536]{1,0:T(8,128)(2,1)}, u32[]{:S(2)}) copy-start(bf16[1024,1536]{1,0:T(8,128)(2,1)} %get-tuple-element.61) | copy-start | bytes 9437188
  178.3 5.2 %copy-start.17 = (bf16[1024,1152]{1,0:T(8,128)(2,1)S(1)}, bf16[1024,1152]{1,0:T(8,128)(2,1)}, u32[]{:S(2)}) copy-start(bf16[1024,1152]{1,0:T(8,128)(2,1)} %get-tuple-element.59) | copy-start | bytes 7077892
  198.6 0.7 copy-start.10
  198.6 0.9 copy-start.9
  198.6 1.0 copy-start.14
  198.6 1.0 copy-start.13
  198.6 1.0 copy-start.12
  198.6 1.0 copy-start.6
  198.7 27.6 %copy-start.8 = (f32[32,256]{1,0:T(8,128)S(1)}, f32[32,256]{1,0:T(8,128)}, u32[]{:S(2)}) copy-start(f32[32,256]{1,0:T(8,128)} %get-tuple-element.65) | copy-start | bytes 98308
  198.7 27.6 %copy-start = (bf16[256,1536]{1,0:T(8,128)(2,1)S(1)}, bf16[256,1536]{1,0:T(8,128)(2,1)}, u32[]{:S(2)}) copy-start(bf16[256,1536]{1,0:T(8,128)(2,1)} %refs_0_.1) | copy-start | bytes 2359300
  198.7 27.9 %copy-start.7 = (f32[1536]{0:T(1024)S(1)}, f32[1536]{0:T(1024)}, u32[]{:S(2)}) copy-start(f32[1536]{0:T(1024)} %param.19) | copy-start | bytes 18436
  198.7 66.9 %copy-start.5 = (bf16[256,1536]{1,0:T(8,128)(2,1)S(1)}, bf16[256,1536]{1,0:T(8,128)(2,1)}, u32[]{:S(2)}) copy-start(bf16[256,1536]{1,0:T(8,128)(2,1)} %refs_8_.1) | copy-start | bytes 2359300
  198.7 196.8 %all-reduce.7.cloned.1.call-start = ((), (), s32[]{:S(2)}) async-start(), calls=%async_computation.6 | async-start | bytes 196608 | tf_op jit(solution)/shard_map/psum | solution.py:919
  351.7 3.0 copy-start.1
Sparse Core Ops, SparseCore 0:
  172.4 40.7 reduce-scatter.5
  216.1 44.7 reduce-scatter.3
  263.2 88.4 reduce-scatter.7
  355.3 40.1 all-reduce.6

commit v2 on v1

--- a/solution.py
+++ b/solution.py
@@ -421,8 +421,8 @@
     )
 
 
+UP, DOWN, PAIR_LOW, PAIR_HIGH = range(4)
 LAST_Z = 3
-UP, DOWN, PAIR_LOW, PAIR_HIGH = range(4)
 
 
 def place():
@@ -430,20 +430,17 @@
     tp = lax.axis_index("tensor")
     z = dp // 2
     core = dp - 2 * z
-    x = lax.rem(tp, 2)
     y = tp // 2
-    near_x = y * 2 + (1 - x)
-    near_y = (1 - y) * 2 + x
-    across = (1 - y) * 2 + (1 - x)
+    x = tp - 2 * y
     return types.SimpleNamespace(
         dp=dp,
         tp=tp,
         z=z,
         core=core,
         mate=dp + 1 - 2 * core,
-        near_x=near_x,
-        near_y=near_y,
-        across=across,
+        near_x=y * 2 + (1 - x),
+        near_y=(1 - y) * 2 + x,
+        across=(1 - y) * 2 + (1 - x),
     )
 
 
@@ -451,23 +448,24 @@
     return {"dp": w.dp if dp is None else dp, "tensor": w.tp if tp is None else tp}
 
 
+def other_z(w, k):
+    return lax.rem(w.z + k, LAST_Z + 1) * 2 + w.core
+
+
+def peers(w):
+    rows = [device(w, tp=t) for t in (w.near_x, w.near_y, w.across)]
+    return rows + [device(w, dp=w.mate)] + [device(w, dp=other_z(w, k)) for k in (1, 2, 3)]
+
+
+def tell(sem, where):
+    pl.semaphore_signal(sem, inc=1, device_id=where, device_id_type=pl.DeviceIdType.MESH)
+
+
 def greet(w):
     barrier = pltpu.get_barrier_semaphore()
-
-    def tell(**where):
-        pl.semaphore_signal(
-            barrier, inc=1, device_id=device(w, **where), device_id_type=pl.DeviceIdType.MESH
-        )
-
-    tell(dp=w.mate)
-    tell(tp=w.near_x)
-    tell(tp=w.near_y)
-    tell(tp=w.across)
-    pl.when(w.z < LAST_Z)(lambda: tell(dp=w.dp + 2))
-    pl.when(w.z > 0)(lambda: tell(dp=w.dp - 2))
-    below = (w.z + LAST_Z - 1) // LAST_Z
-    above = (2 * LAST_Z - 1 - w.z) // LAST_Z
-    pl.semaphore_wait(barrier, 4 + below + above)
+    for where in peers(w):
+        tell(barrier, where)
+    pl.semaphore_wait(barrier, len(peers(w)))
 
 
 def remote(src, dst, send, recv, where):
@@ -510,22 +508,21 @@
 
     def relay(self, step, act=None):
         w = self.w
+        do = act or (lambda copy: copy.start())
 
         def low():
             z = w.z - step
             if act is None and step > 0:
                 self.arrived(z, w.core)
-            do = act or (lambda copy: copy.start())
             pl.when(w.z < LAST_Z)(lambda: do(self.copy(z, step, UP)))
-            do(self.copy(z, step, PAIR_LOW))
             if step == 0:
                 pl.when(w.z > 0)(lambda: do(self.copy(z, step, DOWN)))
+            do(self.copy(z, step, PAIR_LOW))
 
         def high():
             z = w.z + step
             if act is None:
                 self.arrived(z, w.core)
-            do = act or (lambda copy: copy.start())
             pl.when(w.z > 0)(lambda: do(self.copy(z, step, DOWN)))
             do(self.copy(z, step, PAIR_HIGH))
 
@@ -550,9 +547,7 @@
         self.rows = ref.shape[0] // 4
 
     def block(self, slot, half=None):
-        rows = self.rows if half is None else self.rows // 2
-        start = slot * self.rows + (0 if half is None else half * rows)
-        return self.ref.at[pl.ds(pl.multiple_of(start, 16), rows)]
+        return row_block(self.ref, self.rows, slot, half)
 
     def copy(self, i):
         w = self.w
@@ -582,7 +577,207 @@
             self.copy(i).wait_send()
 
 
-def norm_rows(x_ref, gain_ref, out_ref, start):
+def row_block(ref, rows, slot, half=None):
+    start = slot * rows
+    if half is not None:
+        rows = rows // 2
+        start = start + half * rows
+    return ref.at[pl.ds(pl.multiple_of(start, 16), rows)]
+
+
+def add_into(ref, other):
+    rows = 64 if ref.shape[0] % 64 == 0 else ref.shape[0]
+
+    def body(i, carry):
+        here = pl.ds(pl.multiple_of(i * rows, rows), rows)
+        ref[here, :] = (ref[here, :].astype(F32) + other[here, :].astype(F32)).astype(BF16)
+        return carry
+
+    lax.fori_loop(0, ref.shape[0] // rows, body, 0)
+
+
+class RowScatter:
+    def __init__(self, w, part, far, near, send, recv):
+        self.w, self.part, self.far, self.near, self.send, self.recv = w, part, far, near, send, recv
+        self.rows = part.shape[0] // 4
+
+    def block(self, slot, half=None):
+        return row_block(self.part, self.rows, slot, half)
+
+    def copy(self, i):
+        w = self.w
+        half = lambda k, h: row_block(self.near.at[k], self.rows, 0, h)
+        src, dst, to = (
+            (lambda: self.block(w.across, 0), lambda: self.far.at[0], w.near_x),
+            (lambda: self.block(w.across, 1), lambda: self.far.at[1], w.near_y),
+            (lambda: self.block(w.near_x, 0), lambda: half(0, 0), w.near_x),
+            (lambda: self.block(w.near_y, 1), lambda: half(1, 1), w.near_y),
+            (lambda: self.block(w.near_x, 1), lambda: half(0, 1), w.near_x),
+            (lambda: self.block(w.near_y, 0), lambda: half(1, 0), w.near_y),
+        )[i]
+        return remote(src(), dst(), self.send.at[i], self.recv.at[i], device(w, tp=to))
+
+    def start(self, *which):
+        for i in which:
+            self.copy(i).start()
+
+    def hand_on(self):
+        w = self.w
+        self.copy(1).wait_recv()
+        add_into(self.block(w.near_x, 1), self.far.at[1])
+        self.copy(4).start()
+        self.copy(0).wait_recv()
+        add_into(self.block(w.near_y, 0), self.far.at[0])
+        self.copy(5).start()
+
+    def finish(self):
+        for i in range(2, 6):
+            self.copy(i).wait_recv()
+
+    def total(self, here, there):
+        total = self.part[there, :].astype(F32)
+        return total + self.near[0, here, :].astype(F32) + self.near[1, here, :].astype(F32)
+
+    def drain(self):
+        for i in range(6):
+            self.copy(i).wait_send()
+
+
+class LineScatter:
+    def __init__(self, w, shard, pair, up, down, send, recv):
+        self.w, self.shard, self.pair, self.up, self.down = w, shard, pair, up, down
+        self.send, self.recv = send, recv
+        self.rows = pair.shape[0] // (LAST_Z + 1)
+
+    def slot(self, ref, i):
+        return ref.at[pl.ds(pl.multiple_of(i * self.rows, 16), self.rows)]
+
+    def pair_copy(self, z):
+        w = self.w
+        return remote(
+            self.shard(z, 1 - w.core),
+            self.slot(self.pair, z),
+            self.send.at[z],
+            self.recv.at[z],
+            device(w, dp=w.mate),
+        )
+
+    def up_copy(self, z):
+        return remote(
+            self.shard(z, self.w.core),
+            self.slot(self.up, z - 1),
+            self.send.at[3 + z],
+            self.recv.at[3 + z],
+            device(self.w, dp=self.w.dp + 2),
+        )
+
+    def down_copy(self, z):
+        return remote(
+            self.shard(z, self.w.core),
+            self.slot(self.down, z),
+            self.send.at[7 + z],
+            self.recv.at[7 + z],
+            device(self.w, dp=self.w.dp - 2),
+        )
+
+    def pair_add(self):
+        def body(z, carry):
+            self.pair_copy(z).wait_recv()
+            add_into(self.shard(z, self.w.core), self.slot(self.pair, z))
+            return carry
+
+        lax.fori_loop(0, LAST_Z + 1, body, 0)
+
+    def launch(self):
+        @pl.when(self.w.z == 0)
+        def _():
+            for z in (3, 2, 1):
+                self.up_copy(z).start()
+
+        @pl.when(self.w.z == LAST_Z)
+        def _():
+            for z in (0, 1, 2):
+                self.down_copy(z).start()
+
+    def pass_up(self, z):
+        self.up_copy(z).wait_recv()
+        add_into(self.shard(z, self.w.core), self.slot(self.up, z - 1))
+        self.up_copy(z).start()
+
+    def pass_down(self, z):
+        self.down_copy(z).wait_recv()
+        add_into(self.shard(z, self.w.core), self.slot(self.down, z))
+        self.down_copy(z).start()
+
+    def step(self, k):
+        w = self.w
+        if k == 0:
+            pl.when(w.z == 1)(lambda: self.pass_up(3))
+            pl.when(w.z == 2)(lambda: self.pass_down(0))
+        else:
+
+            @pl.when(w.z == 1)
+            def _():
+                self.pass_up(2)
+                self.pass_down(0)
+
+            @pl.when(w.z == 2)
+            def _():
+                self.pass_down(1)
+                self.pass_up(3)
+
+    def finish(self, out):
+        w = self.w
+        out[...] = self.shard(w.z, w.core)[...].astype(F32)
+
+        @pl.when(w.z > 0)
+        def _():
+            self.up_copy(w.z).wait_recv()
+            out[...] += self.slot(self.up, w.z - 1)[...].astype(F32)
+
+        @pl.when(w.z < LAST_Z)
+        def _():
+            self.down_copy(w.z).wait_recv()
+            out[...] += self.slot(self.down, w.z)[...].astype(F32)
+
+    def drain(self):
+        w = self.w
+
+        def body(z, carry):
+            self.pair_copy(z).wait_send()
+            return carry
+
+        lax.fori_loop(0, LAST_Z + 1, body, 0)
+        for z in range(1, LAST_Z + 1):
+            pl.when(w.z < z)(lambda z=z: self.up_copy(z).wait_send())
+        for z in range(LAST_Z):
+            pl.when(w.z > z)(lambda z=z: self.down_copy(z).wait_send())
+
+
+class Exchange:
+    def __init__(self, ref, mine, targets, send, recv):
+        self.ref, self.mine, self.targets, self.send, self.recv = ref, mine, targets, send, recv
+
+    def copy(self, i):
+        part = self.ref.at[self.mine]
+        return remote(part, part, self.send.at[i], self.recv.at[i], self.targets[i])
+
+    def start(self):
+        for i in range(len(self.targets)):
+            self.copy(i).start()
+
+    def finish(self):
+        for i in range(len(self.targets)):
+            self.copy(i).wait()
+
+    def total(self):
+        total = self.ref[0].astype(F32)
+        for i in range(1, self.ref.shape[0]):
+            total = total + self.ref[i].astype(F32)
+        return total
+
+
+def norm_rows(x_ref, gain, out_ref, start):
     rows = 64
 
     def body(i, carry):
@@ -590,7 +785,7 @@
         values = x_ref[here, :].astype(F32)
         scale = lax.rsqrt(jnp.mean(values * values, axis=1, keepdims=True) + EPS)
         there = pl.ds(pl.multiple_of(start + i * rows, 16), rows)
-        out_ref[there, :] = (values * scale * gain_ref[...]).astype(BF16)
+        out_ref[there, :] = (values * scale * gain).astype(BF16)
         return carry
 
     lax.fori_loop(0, x_ref.shape[0] // rows, body, 0)
@@ -604,77 +799,197 @@
     lax.fori_loop(0, total // rows, step, 0)
 
 
-def gate_chunk(c, r):
+def over_chunks(r, body):
+    def step(c, carry):
+        body(c)
+        return carry
+
+    lax.fori_loop(0, r.chunks, step, 0)
+
+
+def turned(row):
+    return jnp.broadcast_to(row, (CHUNK, LANES)).T
+
+
+def gated_tile(c, r, p):
+    rows, lanes = chunk_rows(c), slice(p * LANES, (p + 1) * LANES)
+    z = r.z[rows, lanes]
+    gate = sigmoid(z)
+    return z, gate, r.y[rows, lanes]
+
+
+def square_chunk(c, r):
+    square = jnp.zeros((CHUNK, LANES), F32)
+    for p in range(r.pairs):
+        z, gate, y = gated_tile(c, r, p)
+        gated = y * (z * gate)
+        square = square + gated * gated
+    r.squares.at[r.w.tp][pl.ds(c, 1), :] = jnp.sum(square.T, axis=0, keepdims=True)
+
+
+def cross_chunk(c, r):
     rows = chunk_rows(c)
-    square = jnp.zeros((CHUNK, LANES), F32)
     cross = jnp.zeros((CHUNK, LANES), F32)
     for p in range(r.pairs):
         lanes = slice(p * LANES, (p + 1) * LANES)
-        z = r.z[rows, lanes]
-        gated = r.y[rows, lanes] * (z * sigmoid(z))
-        square = square + gated * gated
-        cross = cross + r.d_mixed[rows, lanes] * r.gain[0:1, lanes] * gated
-    half = r.parts.shape[1] // 2
-    mine = r.parts.at[r.w.tp]
-    mine[pl.ds(c, 1), :] = jnp.sum(square.T, axis=0, keepdims=True)
-    mine[pl.ds(half + c, 1), :] = jnp.sum(cross.T, axis=0, keepdims=True)
-
-
-class SumExchange:
-    def __init__(self, w, ref, send, recv):
-        self.w, self.ref, self.send, self.recv = w, ref, send, recv
-
-    def copies(self):
-        w = self.w
-        mine = self.ref.at[w.tp]
-        return [
-            remote(mine, mine, self.send.at[i], self.recv.at[i], device(w, tp=to))
-            for i, to in enumerate((w.near_x, w.near_y, w.across))
-        ]
-
-    def start(self):
-        for copy in self.copies():
-            copy.start()
-
-    def finish(self):
-        for copy in self.copies():
-            copy.wait()
+        z, gate, y = gated_tile(c, r, p)
+        cross = cross + r.d_mixed[rows, lanes] * r.gain[0:1, lanes] * (y * (z * gate))
+    r.crosses.at[r.w.tp][pl.ds(c, 1), :] = jnp.sum(cross.T, axis=0, keepdims=True)
+
+
+def slot_sum(ref, c):
+    total = ref[0, pl.ds(c, 1), :]
+    for i in range(1, 4):
+        total = total + ref[i, pl.ds(c, 1), :]
+    return total
+
+
+def scale_two_row(c, r):
+    return lax.rsqrt(slot_sum(r.squares, c) / (r.pairs * LANES * 4) + EPS)
+
+
+def mix_chunk(c, r):
+    rows = chunk_rows(c)
+    scale = turned(scale_two_row(c, r))
+    for p in range(r.pairs):
+        lanes = slice(p * LANES, (p + 1) * LANES)
+        z, gate, y = gated_tile(c, r, p)
+        r.mixed[rows, lanes] = (y * (z * gate) * scale * r.gain[0:1, lanes]).astype(BF16)
+
+
+def gate_back_chunk(c, r):
+    rows = chunk_rows(c)
+    row = scale_two_row(c, r)
+    pull = turned(row * row * row * slot_sum(r.crosses, c) / (r.pairs * LANES * 4))
+    scale = turned(row)
+    for p in range(r.pairs):
+        lanes = slice(p * LANES, (p + 1) * LANES)
+        z, gate, y = gated_tile(c, r, p)
+        silu = z * gate
+        gated = y * silu
+        scaled = r.d_mixed[rows, lanes] * scale
+        r.g_gate[:, lanes] += fold_rows(scaled * gated)
+        d_gated = scaled * r.gain[0:1, lanes] - gated * pull
+        r.gy[rows, lanes] = (d_gated * silu).astype(BF16)
+        r.d_z[rows, lanes] = (d_gated * y * (gate * (1.0 + z * (1.0 - gate)))).astype(BF16)
+
+
+def ends_first(i):
+    odd = lax.rem(i, 2)
+    return (1 - odd) * (LAST_Z - i // 2) + odd * (i // 2)
+
+
+def weight_parts(left, right, scatter, store):
+    block = left.shape[1] // (LAST_Z + 1)
+
+    def body(i, carry):
+        z = ends_first(i)
+        lanes = pl.ds(pl.multiple_of(z * block, LANES), block)
+        store(z, dot_tn(left[:, lanes], right[...]).astype(BF16))
+        scatter.pair_copy(z).start()
+        return carry
+
+    lax.fori_loop(0, LAST_Z + 1, body, 0)
+
+
+def flat_shard(ref, rows):
+    return lambda z, core: ref.at[pl.ds(pl.multiple_of((z * 2 + core) * rows, 16), rows)]
+
+
+def flat_store(ref, rows):
+    def store(z, value):
+        ref[pl.ds(pl.multiple_of(z * 2 * rows, 16), 2 * rows), :] = value
+
+    return store
+
+
+def side_shard(ref, rows, width):
+    return lambda z, core: ref.at[
+        pl.ds(pl.multiple_of(z * rows, 16), rows),
+        pl.ds(pl.multiple_of(core * width, LANES), width),
+    ]
+
+
+def side_store(ref, rows, width):
+    def store(z, value):
+        here = pl.ds(pl.multiple_of(z * rows, 16), rows)
+        ref[here, :width] = value[:rows]
+        ref[here, width : 2 * width] = value[rows:]
+
+    return store
+
+
+def prepare_inputs(r):
+    w, width = r.w, r.pairs * LANES
+    heads = r.a_log_in.shape[0]
+    shard = r.w_x.shape[0]
+    own = pl.ds(pl.multiple_of(w.dp * shard, 16), shard)
+    r.full_x[own, :width] = r.w_x[...]
+    r.full_x[own, width : width + 2 * NSTATE] = r.w_bc[...]
+    r.turn[...] = jnp.zeros_like(r.turn)
+    r.turn[0:heads, 0:shard] = r.w_dt[...]
+    r.full_x[own, width + 2 * NSTATE :] = r.turn[...].T[:shard]
+
+
+def prepare_small(r):
+    heads = r.a_log_in.shape[0]
+    w, width = r.w, r.pairs * LANES
+    for ref in (r.a_log, r.dt_bias):
+        ref[...] = jnp.zeros_like(ref)
+    r.a_log[0:1, 0:heads] = r.a_log_in[...].reshape(1, heads)
+    r.dt_bias[0:1, 0:heads] = r.dt_bias_in[...].reshape(1, heads)
+    r.cxb[...] = r.cxb_in[...].reshape(1, width)
+    r.cbb[...] = r.cbb_in[...].reshape(1, 2 * NSTATE)
+    r.gain[...] = r.gain_in[...].reshape(1, width)
+    skip = r.d_skip_in[...].reshape(1, heads)
+    first = lax.broadcasted_iota(jnp.int32, (1, LANES), 1) < HEADDIM
+    for p in range(r.pairs):
+        pair = jnp.where(first, skip[:, 2 * p : 2 * p + 1], skip[:, 2 * p + 1 : 2 * p + 2])
+        r.skip[:, p * LANES : (p + 1) * LANES] = pair
+    r.seg_across[...] = r.segments[...].reshape(r.chunks, CHUNK).astype(F32)
+    edge = jnp.full((8, LANES), -1.0, F32)
+    r.seg_down[0:8, :] = edge
+    r.seg_down[r.chunks * CHUNK + 8 :, :] = edge
+
+    def body(c):
+        r.seg_down[chunk_rows(c, 8), :] = turned(r.seg_across[pl.ds(c, 1), :])
+
+    over_chunks(r, body)
 
 
 def phase_one(r):
     w = r.w
     width = r.pairs * LANES
     tokens = r.row_normed.shape[0]
-    chunks = tokens // CHUNK
-    own = pl.ds(pl.multiple_of(w.dp * r.w_x.shape[0], 16), r.w_x.shape[0])
-    r.full_x[own, :width] = r.w_x[...]
-    r.full_x[own, width : width + 2 * NSTATE] = r.w_bc[...]
-    r.full_x[own, width + 2 * NSTATE :] = r.w_dt[...]
-    r.full_out[own, :] = r.w_out[...]
-    r.full_z[own, :] = r.w_z[...]
-    shard_x = LineGather(w, r.full_x, r.send_w.at[0], r.recv_w.at[0])
-    shard_out = LineGather(w, r.full_out, r.send_w.at[1], r.recv_w.at[1])
-    shard_z = LineGather(w, r.full_z, r.send_w.at[2], r.recv_w.at[2])
-    row_n = RowGather(w, r.row_normed, r.send_r.at[0], r.recv_r.at[0])
-    row_c = RowGather(w, r.row_cot, r.send_r.at[1], r.recv_r.at[1])
-    sums = SumExchange(w, r.parts, r.send_s, r.recv_s)
     block = r.x_in.shape[0]
     start = pl.multiple_of(w.tp * block, block)
+    shard = r.w_x.shape[0]
+    own = pl.ds(pl.multiple_of(w.dp * shard, 16), shard)
+    prepare_inputs(r)
     greet(w)
-    shard_x.relay(0)
-    norm_rows(r.x_in, r.pre_gain, r.row_normed, start)
-    row_n.start()
+    r.shard_x.relay(0)
+    norm_rows(r.x_in, r.pre_gain[...].reshape(1, r.x_in.shape[1]), r.row_normed, start)
+    r.row_n.start()
+    moves = [
+        pltpu.make_async_copy(src, dst.at[own], r.s_m.at[i])
+        for i, (src, dst) in enumerate(((r.w_out, r.full_out), (r.w_z, r.full_z)))
+    ]
+    for move in moves:
+        move.start()
     r.row_cot[pl.ds(start, block), :] = r.cot[...]
     r.state[...] = jnp.zeros_like(r.state)
-    shard_x.relay(1)
-    row_n.hand_on()
-    row_c.start()
-    shard_x.relay(2)
-    shard_x.relay(3)
-    shard_out.relay(0)
-    row_n.finish()
-    shard_x.finish()
-    shard_out.relay(1)
+    prepare_small(r)
+    for move in moves:
+        move.wait()
+    r.shard_x.relay(1)
+    r.row_n.hand_on()
+    r.row_c.start()
+    r.shard_x.relay(2)
+    r.shard_x.relay(3)
+    r.shard_z.relay(0)
+    r.row_n.finish()
+    r.shard_x.finish()
+    r.shard_z.relay(1)
 
     def project_x(rows):
         out = dot_nn(r.row_normed[rows, :], r.full_x[...])
@@ -683,123 +998,477 @@
         r.dtr[rows, :] = out[:, width + 2 * NSTATE :]
 
     by_rows(tokens, 256, project_x)
-    shard_out.relay(2)
-
-    def body(c, carry):
+    r.shard_z.relay(2)
+
+    def body(c):
         prepare_steps(c, r)
         scan_chunk(c, r)
 
         @pl.when(c == 1)
         def _():
-            shard_out.relay(3)
-            shard_z.relay(0)
+            r.shard_z.relay(3)
+            r.shard_out.relay(0)
 
         @pl.when(c == 3)
         def _():
-            shard_z.relay(1)
-            row_c.hand_on()
+            r.shard_out.relay(1)
+            r.row_c.hand_on()
 
         @pl.when(c == 5)
         def _():
-            shard_z.relay(2)
-
-        return carry
-
-    lax.fori_loop(0, chunks, body, 0)
-    shard_z.relay(3)
-    row_c.finish()
-    shard_out.finish()
+            r.shard_out.relay(2)
+
+    over_chunks(r, body)
+
+
+def phase_mid(r):
+    w = r.w
+    tokens = r.row_normed.shape[0]
+    r.shard_z.finish()
+
+    def project_z(rows):
+        r.z[rows, :] = dot_nn(r.row_normed[rows, :], r.full_z[...])
+
+    by_rows(tokens, 256, project_z)
+    over_chunks(r, lambda c: square_chunk(c, r))
+    r.ex_squares.start()
+    r.shard_out.relay(3)
+    r.row_c.finish()
+    r.ex_squares.finish()
+    over_chunks(r, lambda c: mix_chunk(c, r))
+    weight_parts(r.row_cot, r.mixed, r.grad_out, flat_store(r.out_part, r.shard_rows))
+    r.shard_out.finish()
 
     def mix_back(rows):
         r.d_mixed[rows, :] = dot_nn(r.row_cot[rows, :], r.full_out[...])
 
     by_rows(tokens, 256, mix_back)
-    shard_z.finish()
-
-    def project_z(rows):
-        r.z[rows, :] = dot_nn(r.row_normed[rows, :], r.full_z[...])
-
-    by_rows(tokens, 256, project_z)
-
-    def gate(c, carry):
-        gate_chunk(c, r)
+    r.grad_out.pair_add()
+    r.grad_out.launch()
+    over_chunks(r, lambda c: cross_chunk(c, r))
+    r.ex_crosses.start()
+    block = r.x_in.shape[0]
+
+    def share(slot):
+        rows = pl.ds(pl.multiple_of(slot * block, block), block)
+        tile = 512
+
+        def body(n, carry):
+            cols = pl.ds(pl.multiple_of(n * tile, tile), tile)
+            r.part[rows, cols] = dot_nt(r.mixed[rows, :], r.full_out[cols, :]).astype(BF16)
+            return carry
+
+        lax.fori_loop(0, r.part.shape[1] // tile, body, 0)
+
+    share(w.across)
+    r.out_rows.start(0, 1)
+    share(w.near_x)
+    r.out_rows.start(2)
+    share(w.near_y)
+    r.out_rows.start(3)
+    share(w.tp)
+    r.ex_crosses.finish()
+    for item in (r.shard_x, r.shard_z, r.shard_out, r.row_n, r.row_c):
+        item.drain()
+    r.g_gate[...] = jnp.zeros_like(r.g_gate)
+    over_chunks(r, lambda c: gate_back_chunk(c, r))
+    r.grad_out.step(0)
+    r.out_rows.hand_on()
+    tell(r.free_pair, device(w, dp=w.mate))
+    pl.semaphore_wait(r.free_pair, 1)
+    weight_parts(r.row_normed, r.d_z, r.grad_z, flat_store(r.full_out, r.shard_rows))
+
+
+def phase_back(r):
+    w = r.w
+    block = r.x_in.shape[0]
+    start_back(r)
+    r.grad_z.pair_add()
+    tell(r.free_pair, device(w, dp=w.mate))
+    r.grad_z.launch()
+
+    def body(i, carry):
+        scan_chunk_back(r.chunks - 1 - i, r)
+
+        @pl.when(i == 1)
+        def _():
+            r.grad_out.step(1)
+
+        @pl.when(i == 3)
+        def _():
+            r.grad_out.finish(r.o_w_out)
+            r.grad_out.drain()
+            tell(r.free_line, device(w, dp=other_z(w, 1)))
+            tell(r.free_line, device(w, dp=other_z(w, 3)))
+            r.grad_z.step(0)
+
+        @pl.when(i == 5)
+        def _():
+            r.out_rows.finish()
+            step = 64
+
+            def add(k, carry):
+                here = pl.ds(pl.multiple_of(k * step, step), step)
+                there = pl.ds(pl.multiple_of(w.tp * block + k * step, 16), step)
+                total = r.x_in[here, :].astype(F32) + r.out_rows.total(here, there)
+                r.o_block[here, :] = total.astype(BF16)
+                return carry
+
+            lax.fori_loop(0, block // step, add, 0)
+            r.out_rows.drain()
+            tell(r.free_row, device(w, tp=w.near_x))
+            tell(r.free_row, device(w, tp=w.near_y))
+            r.grad_z.step(1)
+
         return carry
 
-    lax.fori_loop(0, chunks, gate, 0)
-    sums.start()
-    for item in (shard_x, shard_out, shard_z, row_n, row_c):
+    lax.fori_loop(0, r.chunks, body, 0)
+
+
+def phase_last(r):
+    w = r.w
+    width = r.pairs * LANES
+    block = r.x_in.shape[0]
+    weight_parts(
+        r.row_normed, r.d_rest.at[:, pl.ds(width, 2 * NSTATE + LANES)], r.grad_bc, flat_store(r.bc_part, r.shard_rows)
+    )
+    r.g_pre[...] = jnp.zeros_like(r.g_pre)
+    pl.semaphore_wait(r.free_row, 2)
+
+    def share(slot):
+        rows = pl.ds(pl.multiple_of(slot * block, block), block)
+        tile = 512
+
+        def body(n, carry):
+            cols = pl.ds(pl.multiple_of(n * tile, tile), tile)
+            out = dot_nt(r.d_z[rows, :], r.full_z[cols, :]) + dot_nt(
+                r.d_rest[rows, :], r.full_x[cols, :]
+            )
+            r.part[rows, cols] = out.astype(BF16)
+            r.g_pre[:, cols] += fold_rows(out * r.row_normed[rows, cols].astype(F32))
+            return carry
+
+        lax.fori_loop(0, r.part.shape[1] // tile, body, 0)
+
+    r.grad_bc.pair_add()
+    r.grad_bc.launch()
+    share(w.across)
+    r.in_rows.start(0, 1)
+    share(w.near_x)
+    r.in_rows.start(2)
+    r.grad_bc.step(0)
+    share(w.near_y)
+    r.in_rows.start(3)
+    share(w.tp)
+    pack_small(r)
+    r.ex_pair.start()
+    r.grad_bc.step(1)
+    pl.semaphore_wait(r.free_pair, 1)
+    weight_parts(
+        r.row_normed,
+        r.d_rest.at[:, pl.ds(0, width)],
+        r.grad_x_part,
+        side_store(r.row_cot, r.shard_rows, width),
+    )
+    r.grad_z.finish(r.o_w_z)
+    r.in_rows.hand_on()
+    r.ex_pair.finish()
+    r.small_z.at[w.z][...] = r.ex_pair.total()
+    r.ex_z.start()
+    r.grad_x_part.pair_add()
+    pl.semaphore_wait(r.free_line, 2)
+    r.grad_x_part.launch()
+    r.grad_bc.finish(r.bc_sum)
+    r.o_w_dt[...] = r.bc_sum[:, 2 * NSTATE :]
+    r.bc_slots.at[w.tp][...] = r.bc_sum[:, : 2 * NSTATE].astype(BF16)
+    r.ex_bc.start()
+    r.ex_z.finish()
+    total = r.ex_z.total()
+    r.o_small[...] = total[:SMALL_DP]
+    r.small_t.at[w.tp][...] = total[SMALL_DP:]
+    r.ex_t.start()
+    r.grad_x_part.step(0)
+    r.ex_bc.finish()
+    r.o_w_bc[...] = r.ex_bc.total()
+    r.ex_t.finish()
+    r.o_shared[...] = r.ex_t.total()
+    r.grad_x_part.step(1)
+    r.in_rows.finish()
+    gain = r.pre_gain[...].reshape(1, r.x_in.shape[1])
+    step = 64
+
+    def body(k, carry):
+        here = pl.ds(pl.multiple_of(k * step, step), step)
+        there = pl.ds(pl.multiple_of(w.tp * block + k * step, 16), step)
+        values = r.x_in[here, :].astype(F32)
+        scale = lax.rsqrt(jnp.mean(values * values, axis=1, keepdims=True) + EPS)
+        weighted = r.in_rows.total(here, there) * gain
+        along = jnp.mean(weighted * values, axis=1, keepdims=True)
+        grad = r.cot[here, :].astype(F32) + scale * weighted
+        r.o_grad_x[here, :] = (grad - values * (scale * scale * scale * along)).astype(BF16)
+        return carry
+
+    lax.fori_loop(0, block // step, body, 0)
+    r.grad_x_part.finish(r.o_w_x)
+    for item in (r.grad_z, r.grad_bc, r.grad_x_part, r.in_rows):
         item.drain()
-    sums.finish()
-
-
-ONE_IN = ("x_in", "pre_gain", "w_z", "w_x", "w_bc", "w_dt", "w_out", "gain", "cot") + SMALL_IN
-ONE_OUT = lambda tokens, features, width: dict(
-    row_normed=((tokens, features), BF16),
-    row_cot=((tokens, features), BF16),
-    full_x=((features, width + 2 * NSTATE + LANES), BF16),
-    full_z=((features, width), BF16),
-    full_out=((features, width), BF16),
-    z=((tokens, width), F32),
-    xr=((tokens, width), F32),
-    bc=((tokens, 2 * NSTATE), F32),
-    dtr=((tokens, LANES), F32),
-    y=((tokens, width), F32),
-    pre_x=((tokens, width), F32),
-    pre_bc=((tokens, 2 * NSTATE), F32),
-    maps=((tokens, 2 * NSTATE), BF16),
-    states=((tokens, width), BF16),
-    step=((tokens, LANES), F32),
-    total=((tokens, LANES), F32),
-    total_t=((tokens // CHUNK * 16, LANES), F32),
-    d_mixed=((tokens, width), F32),
-    parts=((4, 2 * (tokens // CHUNK), LANES), F32),
+
+
+SMALL_DP = 48
+SMALL_ALL = 24
+
+
+def pack_small(r):
+    mine = r.small_pair.at[r.w.core]
+    mine[...] = jnp.zeros_like(mine)
+
+    def put(at, ref, first, count):
+        for p in range(count):
+            lanes = slice(p * LANES, (p + 1) * LANES)
+            mine[at + p : at + p + 1, :] = jnp.sum(
+                ref[first : first + 8, lanes], axis=0, keepdims=True
+            )
+        return at + count
+
+    at = put(0, r.g_gate, 0, r.pairs)
+    for k in range(4):
+        at = put(at, r.g_cxw, 8 * k, r.pairs)
+    at = put(at, r.g_cxb, 0, r.pairs)
+    at = put(at, r.g_skip, 0, r.pairs)
+    at = put(at, r.g_alog, 0, 1)
+    at = put(at, r.g_dtb, 0, 1)
+    at = put(SMALL_DP, r.g_pre, 0, r.g_pre.shape[1] // LANES)
+    for k in range(4):
+        at = put(at, r.g_cbw, 8 * k, 2)
+    put(at, r.g_cbb, 0, 2)
+
+
+RAW_IN = (
+    "x_in",
+    "segments",
+    "pre_gain",
+    "w_z",
+    "w_x",
+    "w_bc",
+    "w_dt",
+    "cxw",
+    "cxb_in",
+    "cbw",
+    "cbb_in",
+    "a_log_in",
+    "dt_bias_in",
+    "d_skip_in",
+    "gain_in",
+    "w_out",
+    "cot",
 )
 
 
-def one_kernel(*refs, names, width):
+def whole_kernel(*refs, names, width):
     r = types.SimpleNamespace(**dict(zip(names, refs)))
-    r.w = place()
+    r.w = w = place()
     r.pairs = width // LANES
+    r.chunks = r.row_normed.shape[0] // CHUNK
+    r.shard_rows = r.w_x.shape[0]
     r.xr_at = r.bc_at = r.dtr_at = 0
+    r.dx_at, r.dbc_at, r.ddt_at = 0, width, width + 2 * NSTATE
+    r.shard_x = LineGather(w, r.full_x, r.s_w.at[0], r.r_w.at[0])
+    r.shard_z = LineGather(w, r.full_z, r.s_w.at[1], r.r_w.at[1])
+    r.shard_out = LineGather(w, r.full_out, r.s_w.at[2], r.r_w.at[2])
+    r.row_n = RowGather(w, r.row_normed, r.s_r.at[0], r.r_r.at[0])
+    r.row_c = RowGather(w, r.row_cot, r.s_r.at[1], r.r_r.at[1])
+    r.out_rows = RowScatter(w, r.part, r.far, r.near, r.s_q.at[0], r.r_q.at[0])
+    r.in_rows = RowScatter(w, r.part, r.far, r.near, r.s_q.at[1], r.r_q.at[1])
+    rows = r.shard_rows
+    scatter = lambda i, shard, pair, up, down: LineScatter(
+        w, shard, pair, up, down, r.s_l.at[i], r.r_l.at[i]
+    )
+    r.grad_out = scatter(0, flat_shard(r.out_part, rows), r.pair, r.up, r.down)
+    r.grad_z = scatter(1, flat_shard(r.full_out, rows), r.pair, r.up_z, r.down_z)
+    r.grad_x_part = scatter(3, side_shard(r.row_cot, rows, width), r.pair, r.up, r.down)
+    in_row = [device(w, tp=t) for t in (w.near_x, w.near_y, w.across)]
+    in_line = [device(w, dp=other_z(w, k)) for k in (1, 2, 3)]
+    exchange = lambda i, ref, mine, targets: Exchange(ref, mine, targets, r.s_e.at[i], r.r_e.at[i])
+    r.ex_squares = exchange(0, r.squares, w.tp, in_row)
+    r.ex_crosses = exchange(1, r.crosses, w.tp, in_row)
+    r.ex_pair = exchange(2, r.small_pair, w.core, [device(w, dp=w.mate)])
+    r.ex_z = exchange(3, r.small_z, w.z, in_line)
+    r.ex_t = exchange(4, r.small_t, w.tp, in_row)
+    r.ex_bc = exchange(5, r.bc_slots, w.tp, in_row)
+    tokens = r.chunks * CHUNK
     phase_one(r)
 
-
-def gather_forward(args, small, width):
-    x_in, pre_gain, w_z, w_x, w_bc, w_dt, w_out, gate_gain, cotangent = args
-    features = x_in.shape[1]
-    tokens = x_in.shape[0] * 4
-    outs = ONE_OUT(tokens, features, width)
-    scratch = dict(state=((NSTATE, width), F32))
-    names = ONE_IN + tuple(outs) + tuple(scratch)
-    names = names + ("send_w", "recv_w", "send_r", "recv_r", "send_s", "recv_s")
-    values = (
-        x_in,
-        pre_gain[None, :],
-        w_z,
-        w_x,
-        w_bc,
-        jnp.pad(w_dt, ((0, 0), (0, LANES - w_dt.shape[1]))),
-        w_out.T,
-        gate_gain[None, :],
-        cotangent,
-    )
+    def middle(z, d_mixed, mixed):
+        r.z, r.d_mixed, r.mixed = z, d_mixed, mixed
+        phase_mid(r)
+
+    pl.run_scoped(
+        middle,
+        pltpu.VMEM((tokens, width), F32),
+        pltpu.VMEM((tokens, width), F32),
+        pltpu.VMEM((tokens, width), BF16),
+    )
+    later = dict(BACK_SCRATCH(width), bc_part=((r.full_x.shape[0], 2 * NSTATE + LANES), BF16))
+
+    def rest(d_rest, *buffers):
+        r.d_rest = r.d_proj = d_rest
+        for name, buffer in zip(later, buffers):
+            setattr(r, name, buffer)
+        r.grad_bc = scatter(2, flat_shard(r.bc_part, rows), r.pair_bc, r.up_bc, r.down_bc)
+        phase_back(r)
+        phase_last(r)
+
+    pl.run_scoped(
+        rest,
+        pltpu.VMEM((tokens, width + 2 * NSTATE + LANES), BF16),
+        *[pltpu.VMEM(*spec) for spec in later.values()],
+    )
+
+
+def whole_call(args, width):
+    x_in, w_x = args[0], args[4]
+    features, block = x_in.shape[1], x_in.shape[0]
+    tokens = block * 4
+    shard = w_x.shape[0]
+    rest = 2 * NSTATE + LANES
+    chunks = tokens // CHUNK
+    outs = dict(
+        o_block=((block, features), BF16),
+        o_grad_x=((block, features), BF16),
+        o_w_z=((shard, width), F32),
+        o_w_x=((shard, width), F32),
+        o_w_bc=((shard, 2 * NSTATE), F32),
+        o_w_dt=((shard, LANES), F32),
+        o_w_out=((shard, width), F32),
+        o_small=((SMALL_DP, LANES), F32),
+        o_shared=((SMALL_ALL, LANES), F32),
+    )
+    scratch = dict(
+        row_normed=((tokens, features), BF16),
+        row_cot=((tokens, features), BF16),
+        full_x=((features, width + rest), BF16),
+        full_z=((features, width), BF16),
+        full_out=((features, width), BF16),
+        xr=((tokens, width), F32),
+        bc=((tokens, 2 * NSTATE), F32),
+        dtr=((tokens, LANES), F32),
+        y=((tokens, width), F32),
+        pre_x=((tokens, width), F32),
+        pre_bc=((tokens, 2 * NSTATE), F32),
+        maps=((tokens, 2 * NSTATE), BF16),
+        states=((tokens, width), BF16),
+        state=((NSTATE, width), F32),
+        step=((tokens, LANES), F32),
+        total=((tokens, LANES), F32),
+        total_t=((chunks * 16, LANES), F32),
+        seg_down=((tokens + 16, LANES), F32),
+        seg_across=((chunks, LANES), F32),
+        turn=((LANES, 2 * LANES), BF16),
+        a_log=((1, LANES), F32),
+        dt_bias=((1, LANES), F32),
+        cxb=((1, width), F32),
+        cbb=((1, 2 * NSTATE), F32),
+        gain=((1, width), F32),
+        skip=((1, width), F32),
+        squares=((4, chunks, LANES), F32),
+        crosses=((4, chunks, LANES), F32),
+        gy=((tokens, width), BF16),
+        d_z=((tokens, width), BF16),
+        part=((tokens, features), BF16),
+        far=((2, block // 2, features), BF16),
+        near=((2, block, features), BF16),
+        out_part=((features, width), BF16),
+        pair=((4 * shard, width), BF16),
+        pair_bc=((4 * shard, rest), BF16),
+        up=((3 * shard, width), BF16),
+        down=((3 * shard, width), BF16),
+        up_z=((3 * shard, width), BF16),
+        down_z=((3 * shard, width), BF16),
+        up_bc=((3 * shard, rest), BF16),
+        down_bc=((3 * shard, rest), BF16),
+        bc_sum=((shard, rest), F32),
+        bc_slots=((4, shard, 2 * NSTATE), BF16),
+        small_pair=((2, SMALL_DP + SMALL_ALL, LANES), F32),
+        small_z=((4, SMALL_DP + SMALL_ALL, LANES), F32),
+        small_t=((4, SMALL_ALL, LANES), F32),
+        g_gate=((8, width), F32),
+        g_pre=((8, features), F32),
+        **GRAD_OUT(width),
+    )
+    dma = pltpu.SemaphoreType.DMA
+    signal = pltpu.SemaphoreType.REGULAR
+    semaphores = dict(
+        s_w=dma((3, 4, 4)),
+        r_w=dma((3, 8)),
+        s_r=dma((2, 4)),
+        r_r=dma((2, 4)),
+        s_q=dma((2, 6)),
+        r_q=dma((2, 6)),
+        s_l=dma((4, 10)),
+        r_l=dma((4, 10)),
+        s_e=dma((6, 3)),
+        r_e=dma((6, 3)),
+        s_m=dma((2,)),
+        free_pair=signal,
+        free_line=signal,
+        free_row=signal,
+    )
+    names = RAW_IN + tuple(outs) + tuple(scratch) + tuple(semaphores)
+    values = list(args)
+    values[6] = values[6].T
+    values[15] = values[15].T
     whole = pl.BlockSpec(memory_space=pltpu.VMEM)
-    dma = pltpu.SemaphoreType.DMA
     out = pl.pallas_call(
-        functools.partial(one_kernel, names=names, width=width),
+        functools.partial(whole_kernel, names=names, width=width),
         out_shape=tuple(jax.ShapeDtypeStruct(*spec) for spec in outs.values()),
-        in_specs=[whole] * len(ONE_IN),
+        in_specs=[
+            pl.BlockSpec(memory_space=pl.ANY) if name in ("w_z", "w_out") else whole
+            for name in RAW_IN
+        ],
         out_specs=tuple([whole] * len(outs)),
         scratch_shapes=[pltpu.VMEM(*spec) for spec in scratch.values()]
-        + [dma((3, 4, 4)), dma((3, 8)), dma((2, 4)), dma((2, 4)), dma((3,)), dma((3,))],
+        + list(semaphores.values()),
         compiler_params=pltpu.CompilerParams(
             vmem_limit_bytes=VMEM_LIMIT, collective_id=0, has_side_effects=True
         ),
         cost_estimate=pl.CostEstimate(
-            flops=2 * 10**10, bytes_accessed=1 << 26, transcendentals=0
+            flops=5 * 10**10, bytes_accessed=1 << 26, transcendentals=0
         ),
-    )(*values, *small)
+    )(*values)
     return types.SimpleNamespace(**dict(zip(outs, out)))
+
+
+def on_device_whole(*args):
+    width = args[3].shape[1]
+    heads = args[11].shape[0]
+    features = args[0].shape[1]
+    o = whole_call(args, width)
+    pairs = width // LANES
+    small = o.o_small
+    rows = lambda at, count: small[at : at + count].reshape(count * LANES)
+    taps = small[pairs : 5 * pairs].reshape(4, width)
+    skip = jnp.sum(rows(6 * pairs, pairs).reshape(heads, HEADDIM), axis=1)
+    shared = o.o_shared.reshape(-1)
+    taps_bc = shared[features : features + 4 * 2 * NSTATE].reshape(4, 2 * NSTATE)
+    at = features + 4 * 2 * NSTATE
+    return (
+        o.o_block,
+        o.o_grad_x,
+        shared[:features] / args[2],
+        o.o_w_z,
+        o.o_w_x,
+        o.o_w_bc,
+        o.o_w_dt[:, :heads],
+        taps,
+        rows(5 * pairs, pairs),
+        taps_bc,
+        shared[at : at + 2 * NSTATE],
+        small[7 * pairs, :heads],
+        small[7 * pairs + 1, :heads],
+        skip,
+        rows(0, pairs),
+        o.o_w_out.T,
+    )
 
 
 def forward_plain(args, small, width):
@@ -870,14 +1539,8 @@
         segments, conv_x_w, conv_x_b, conv_bc_w, conv_bc_b, a_log, dt_bias, d_skip
     )
     args = (x_in, pre_gain, w_z, w_x, w_bc, w_dt, w_out, gate_gain, cotangent)
-    if lax.axis_size("dp") == 2 * (LAST_Z + 1) and lax.axis_size("tensor") == 4:
-        f = gather_forward(args, small, width)
-        f.projected = (f.xr, f.bc, f.dtr)
-        f.saved = tuple(getattr(f, name) for name in SAVED)
-        squares, cross = jnp.sum(f.parts, axis=0).reshape(2, -1)
-    else:
-        f = forward_plain(args, small, width)
-        squares, cross = f.squares, f.cross
+    f = forward_plain(args, small, width)
+    squares, cross = f.squares, f.cross
     y, z_raw, d_mixed = f.saved[0], f.z, f.d_mixed
     values = x_in.astype(F32)
     scale = lax.rsqrt(jnp.mean(values * values, axis=1) + EPS)
@@ -965,8 +1628,9 @@
     tokens = P(("dp", "tensor"), None)
     both = P("dp", "tensor")
     heads = P("tensor")
+    line = mesh.shape["dp"] == 2 * (LAST_Z + 1) and mesh.shape["tensor"] == 4
     return jax.shard_map(
-        on_device,
+        on_device_whole if line else on_device,
         mesh=mesh,
         in_specs=(
             tokens,

time: 404 us -> 205 us (0.51)
  waiting for transfers between devices: 121 us -> 0 us
  blocking collectives: 64 us -> 0 us
  Pallas kernels: 133 us -> 189 us
  matrix products: 34.5 us -> 0 us
  other arithmetic: 22.9 us -> 1.24 us
  between operations: 14 us -> 0.69 us
    reduce_scatter x3 -> x0, waiting for transfers between devices: 83 us -> none  [the longest x1 82.9 us: on_device(): lax.psum_scatter(jnp.concatenate((proj_part, out_part), axis=1).astype(BF...]
    psum x2 -> x0, blocking collectives: 64 us -> none  [the longest x1 37.4 us: on_device(): lax.psum((grad_pre_part, over_taps(g_cbw), over_rows(g_cbb)), ('dp', 'ten...]
    pallas_call x2 -> x1, Pallas kernels: 133 us -> 189 us  [whole_call(): pl.pallas_call(functools.partial(whole_kernel, names=names, width=width),...]
    psum x1 -> x0, waiting for transfers between devices: 38.1 us -> none  [on_device(): lax.psum(owned[:, at.bc:at.dt].astype(BF16), 'tensor').astype(F32)]
    dot_general x5 -> x0, matrix products: 34.5 us -> none  [the longest x3 20.7 us: dot_nt(): lax.dot_general(a, b, (((1,), (1,)), ((), ())), preferred_element_type=F32)]
    convert_element_type x4 -> x0, other arithmetic: 12.3 us -> none  [the longest x1 6.19 us: on_device(): gy = (d_gated * (z_raw * gate)).astype(BF16)]
    broadcast_in_dim x6 -> x0, local copies, waits for them, and re-layouts: 6.74 us -> none  [the longest x1 1.3 us: gather_forward(): pre_gain[None, :]]
    concatenate x1 -> x0, other arithmetic: 6.51 us -> none  [on_device(): jnp.concatenate((proj_part, out_part), axis=1).astype(BF16)]
  transfers between devices with their start and end apart: 4 -> 0, of which waited for: 2 -> 0; matrix products, arithmetic and copies ran while one was open for 9% -> 0% of each run, Pallas kernels for 0% -> 0%
where the time goes in v2:
time: 205 us
  Pallas kernels  189 us (92%)
  local copies, waits for them, and re-layouts  13.4 us (7%)
    pallas_call x1, Pallas kernels, whole_call(): pl.pallas_call(functools.partial(whole_kernel, names=names, width=width),...  189 us
    unnamed x23, local copies, waits for them, and re-layouts  8.16 us

profile of v2, /device:TPU:0, one launch (start us, length us, event | category | flops | bytes accessed | tf_op | source)
XLA Modules:
  0.0 204.6 jit_solution(4525433772482853813)
XLA Ops:
  0.7 0.0 copy-start.7
  0.7 189.3 %shard_map.288 = (bf16[256,1536]{1,0:T(8,128)(2,1)}, bf16[256,1536]{1,0:T(8,128)(2,1)}, f32[192,768]{1,0:T(8,128)}, f32[192,768]{1,0:T(8,128)}, f32[192,256]{1,0...) custom-call(bf16[256,1536]{1,0:T(8,128)(2,1)} %refs_0_.1, ...), custom_call_target="tpu_custom_call" | custom-call | flops 49999998976 | bytes 67108864 | tf_op jit(solution)/shard_map/pallas_call | solution.py:1421
  190.0 0.0 copy-start.5
  190.0 1.4 slice_bitcast_fusion
  191.3 0.1 reshape_reshape.3
  191.4 0.6 reduce_sum.9
  192.0 1.3 slice_bitcast_fusion.3
  193.3 0.7 slice.40
  194.0 0.0 copy-start.6
  194.0 0.6 reshape.49
  194.6 0.0 copy-done.7
  194.6 0.1 copy-done.6
  194.7 0.6 bitcast_divide_fusion
  195.3 0.6 reshape.51
  196.0 0.6 slice_bitcast_fusion.2
  196.5 0.0 copy-done.5
  196.5 0.7 copy.33
  197.2 0.0 copy-start
  197.2 2.1 %copy.40 = bf16[256,1536]{1,0:T(8,128)(2,1)} copy(bf16[256,1536]{1,0:T(8,128)(2,1)} %get-tuple-element.71) | data formatting | bytes 1572864
  199.3 0.0 copy-done
  199.3 0.0 copy-start.3
  199.3 0.9 copy.41
  200.2 0.5 copy-done.3
  200.7 0.0 copy-start.2
  200.7 0.8 copy.42
  201.5 0.5 copy-done.2
  202.0 0.0 copy-start.4
  202.0 0.8 copy.43
  202.8 0.3 copy-done.4
  203.1 0.7 copy.44
  203.8 0.0 copy-done.1
  203.8 0.8 copy.45
  (2 shorter events, 0.0 us)
Async XLA Ops:
  0.7 194.0 %copy-start.7 = (f32[1536]{0:T(1024)S(1)}, f32[1536]{0:T(1024)}, u32[]{:S(2)}) copy-start(f32[1536]{0:T(1024)} %refs_2_.1) | copy-start | bytes 18436
  190.0 6.6 %copy-start.5 = (f32[192,128]{1,0:T(8,128)S(1)}, f32[192,128]{1,0:T(8,128)}, u32[]{:S(2)}) copy-start(f32[192,128]{1,0:T(8,128)} %get-tuple-element.31) | copy-start | bytes 294916
  194.0 0.7 copy-start.6
  197.2 2.1 %copy-start = (bf16[256,1536]{1,0:T(8,128)(2,1)S(1)}, bf16[256,1536]{1,0:T(8,128)(2,1)}, u32[]{:S(2)}) copy-start(bf16[256,1536]{1,0:T(8,128)(2,1)} %get-tuple-element.72) | copy-start | bytes 2359300
  199.3 1.3 copy-start.3
  200.7 1.3 copy-start.2
  202.0 1.1 copy-start.4
  202.0 1.8 copy-start.1

commit v3 on v2

--- a/solution.py
+++ b/solution.py
@@ -421,8 +421,10 @@
     )
 
 
-UP, DOWN, PAIR_LOW, PAIR_HIGH = range(4)
+UP, DOWN, PAIR = range(3)
 LAST_Z = 3
+STEP_ROWS = 16
+PARTS = 2
 
 
 def place():
@@ -479,52 +481,53 @@
     )
 
 
+def settle(ref, send, recv, where, sent=True):
+    copy = remote(ref, ref, send, recv, where)
+    if sent:
+        copy.wait_send()
+    else:
+        copy.wait_recv()
+
+
 class LineGather:
-    def __init__(self, w, ref, send, recv):
-        self.w, self.ref, self.send, self.recv = w, ref, send, recv
+    def __init__(self, w, ref, send, recv, parts):
+        self.w, self.ref, self.send, self.recv, self.parts = w, ref, send, recv, parts
         self.rows = ref.shape[0] // (2 * (LAST_Z + 1))
-
-    def shard(self, z, core):
-        start = pl.multiple_of((z * 2 + core) * self.rows, 16)
-        return self.ref.at[pl.ds(start, self.rows)]
-
-    def copy(self, z, step, kind):
+        self.joint = recv.at[parts * (LAST_Z + 1)]
+
+    def shard(self, z, core, part):
+        rows = self.rows // self.parts
+        start = pl.multiple_of((z * 2 + core) * self.rows + part * rows, 16)
+        return self.ref.at[pl.ds(start, rows)]
+
+    def copy(self, z, kind, part):
         w = self.w
-        part = self.shard(z, w.core)
+        block = self.shard(z, w.core, part)
         to = {UP: w.dp + 2, DOWN: w.dp - 2}.get(kind, w.mate)
-        return remote(
-            part,
-            part,
-            self.send.at[step, kind],
-            self.recv.at[z * 2 + w.core],
-            device(w, dp=to),
-        )
-
-    def arrived(self, z, core):
-        part = self.shard(z, core)
-        remote(
-            part, part, self.send.at[0, 0], self.recv.at[z * 2 + core], device(self.w)
-        ).wait_recv()
-
-    def relay(self, step, act=None):
+        recv = self.joint if kind == PAIR else self.recv.at[part * (LAST_Z + 1) + z]
+        return remote(block, block, self.send.at[kind], recv, device(w, dp=to))
+
+    def relay(self, step):
+        for part in range(self.parts):
+            self.relay_part(step, part)
+
+    def relay_part(self, step, part):
         w = self.w
-        do = act or (lambda copy: copy.start())
 
         def low():
             z = w.z - step
-            if act is None and step > 0:
-                self.arrived(z, w.core)
-            pl.when(w.z < LAST_Z)(lambda: do(self.copy(z, step, UP)))
+            if step > 0:
+                self.copy(z, UP, part).wait_recv()
+            pl.when(w.z < LAST_Z)(lambda: self.copy(z, UP, part).start())
             if step == 0:
-                pl.when(w.z > 0)(lambda: do(self.copy(z, step, DOWN)))
-            do(self.copy(z, step, PAIR_LOW))
+                pl.when(w.z > 0)(lambda: self.copy(z, DOWN, part).start())
+            self.copy(z, PAIR, part).start()
 
         def high():
             z = w.z + step
-            if act is None:
-                self.arrived(z, w.core)
-            pl.when(w.z > 0)(lambda: do(self.copy(z, step, DOWN)))
-            do(self.copy(z, step, PAIR_HIGH))
+            self.copy(z, DOWN, part).wait_recv()
+            pl.when(w.z > 0)(lambda: self.copy(z, DOWN, part).start())
+            self.copy(z, PAIR, part).start()
 
         if step == 0:
             low()
@@ -532,13 +535,27 @@
             pl.when(w.z >= step)(low)
             pl.when(w.z <= LAST_Z - step)(high)
 
+    def some(self, count):
+        return self.ref.at[pl.ds(0, count * self.rows)]
+
     def finish(self):
-        for z in range(LAST_Z + 1):
-            self.arrived(z, 1 - self.w.core)
+        where = device(self.w, dp=self.w.mate)
+        settle(self.some(LAST_Z + 1), self.send.at[PAIR], self.joint, where, sent=False)
 
     def drain(self):
-        for step in range(LAST_Z + 1):
-            self.relay(step, lambda copy: copy.wait_send())
+        w = self.w
+        settle(self.some(LAST_Z + 1), self.send.at[PAIR], self.joint, device(w, dp=w.mate))
+        for z in range(LAST_Z):
+            pl.when(w.z == z)(
+                lambda z=z: settle(
+                    self.some(z + 1), self.send.at[UP], self.joint, device(w, dp=w.mate)
+                )
+            )
+            pl.when(w.z == LAST_Z - z)(
+                lambda z=z: settle(
+                    self.some(z + 1), self.send.at[DOWN], self.joint, device(w, dp=w.mate)
+                )
+            )
 
 
 class RowGather:
@@ -546,35 +563,37 @@
         self.w, self.ref, self.send, self.recv = w, ref, send, recv
         self.rows = ref.shape[0] // 4
 
-    def block(self, slot, half=None):
-        return row_block(self.ref, self.rows, slot, half)
-
     def copy(self, i):
         w = self.w
-        part, to = (
-            (self.block(w.tp), w.near_x),
-            (self.block(w.tp), w.near_y),
-            (self.block(w.near_x, 0), w.near_y),
-            (self.block(w.near_y, 1), w.near_x),
+        slot, half, to = (
+            (w.tp, 0, w.near_x),
+            (w.tp, 1, w.near_y),
+            (w.tp, 1, w.near_x),
+            (w.tp, 0, w.near_y),
+            (w.near_x, 0, w.near_y),
+            (w.near_y, 1, w.near_x),
         )[i]
-        return remote(part, part, self.send.at[i], self.recv.at[i], device(w, tp=to))
+        block = row_block(self.ref, self.rows, slot, half)
+        return remote(block, block, self.send, self.recv.at[min(i, 2)], device(w, tp=to))
 
     def start(self):
-        for i in range(2):
+        for i in range(4):
             self.copy(i).start()
 
     def hand_on(self):
         for i in range(2):
             self.copy(i).wait_recv()
-            self.copy(i + 2).start()
+            self.copy(i + 4).start()
+
+    def some(self, count):
+        return self.ref.at[pl.ds(0, count * self.rows)]
 
     def finish(self):
-        for i in range(2, 4):
-            self.copy(i).wait_recv()
+        where = device(self.w, tp=self.w.near_x)
+        settle(self.some(2), self.send, self.recv.at[2], where, sent=False)
 
     def drain(self):
-        for i in range(4):
-            self.copy(i).wait_send()
+        settle(self.some(3), self.send, self.recv.at[2], device(self.w, tp=self.w.near_x))
 
 
 def row_block(ref, rows, slot, half=None):
@@ -590,7 +609,7 @@
 
     def body(i, carry):
         here = pl.ds(pl.multiple_of(i * rows, rows), rows)
-        ref[here, :] = (ref[here, :].astype(F32) + other[here, :].astype(F32)).astype(BF16)
+        ref[here, :] = (ref[here, :].astype(F32) + other[here, :].astype(F32)).astype(ref.dtype)
         return carry
 
     lax.fori_loop(0, ref.shape[0] // rows, body, 0)
@@ -615,7 +634,7 @@
             (lambda: self.block(w.near_x, 1), lambda: half(0, 1), w.near_x),
             (lambda: self.block(w.near_y, 0), lambda: half(1, 0), w.near_y),
         )[i]
-        return remote(src(), dst(), self.send.at[i], self.recv.at[i], device(w, tp=to))
+        return remote(src(), dst(), self.send, self.recv.at[min(i, 2)], device(w, tp=to))
 
     def start(self, *which):
         for i in which:
@@ -630,84 +649,95 @@
         add_into(self.block(w.near_y, 0), self.far.at[0])
         self.copy(5).start()
 
+    def some(self, count):
+        return self.part.at[pl.ds(0, count * self.rows)]
+
     def finish(self):
-        for i in range(2, 6):
-            self.copy(i).wait_recv()
+        where = device(self.w, tp=self.w.near_x)
+        settle(self.some(2), self.send, self.recv.at[2], where, sent=False)
 
     def total(self, here, there):
         total = self.part[there, :].astype(F32)
         return total + self.near[0, here, :].astype(F32) + self.near[1, here, :].astype(F32)
 
     def drain(self):
-        for i in range(6):
-            self.copy(i).wait_send()
+        settle(self.some(3), self.send, self.recv.at[2], device(self.w, tp=self.w.near_x))
 
 
 class LineScatter:
-    def __init__(self, w, shard, pair, up, down, send, recv):
+    def __init__(self, w, shard, pair, up, down, pair_sem, line_sem, parts):
         self.w, self.shard, self.pair, self.up, self.down = w, shard, pair, up, down
-        self.send, self.recv = send, recv
+        self.pair_sem, self.line_sem, self.parts = pair_sem, line_sem, parts
         self.rows = pair.shape[0] // (LAST_Z + 1)
 
     def slot(self, ref, i):
         return ref.at[pl.ds(pl.multiple_of(i * self.rows, 16), self.rows)]
+
+    def piece(self, ref, part):
+        rows = self.rows // self.parts
+        return ref.at[pl.ds(part * rows, rows)]
 
     def pair_copy(self, z):
         w = self.w
         return remote(
             self.shard(z, 1 - w.core),
             self.slot(self.pair, z),
-            self.send.at[z],
-            self.recv.at[z],
+            self.pair_sem.at[LAST_Z + 1],
+            self.pair_sem.at[z],
             device(w, dp=w.mate),
         )
 
-    def up_copy(self, z):
+    def up_copy(self, z, part):
         return remote(
-            self.shard(z, self.w.core),
-            self.slot(self.up, z - 1),
-            self.send.at[3 + z],
-            self.recv.at[3 + z],
+            self.piece(self.shard(z, self.w.core), part),
+            self.piece(self.slot(self.up, z - 1), part),
+            self.line_sem.at[0],
+            self.line_sem.at[2 + part * LAST_Z + z - 1],
             device(self.w, dp=self.w.dp + 2),
         )
 
-    def down_copy(self, z):
+    def down_copy(self, z, part):
         return remote(
-            self.shard(z, self.w.core),
-            self.slot(self.down, z),
-            self.send.at[7 + z],
-            self.recv.at[7 + z],
+            self.piece(self.shard(z, self.w.core), part),
+            self.piece(self.slot(self.down, z), part),
+            self.line_sem.at[1],
+            self.line_sem.at[2 + (self.parts + part) * LAST_Z + z],
             device(self.w, dp=self.w.dp - 2),
         )
 
-    def pair_add(self):
-        def body(z, carry):
-            self.pair_copy(z).wait_recv()
-            add_into(self.shard(z, self.w.core), self.slot(self.pair, z))
-            return carry
-
-        lax.fori_loop(0, LAST_Z + 1, body, 0)
-
-    def launch(self):
-        @pl.when(self.w.z == 0)
-        def _():
-            for z in (3, 2, 1):
-                self.up_copy(z).start()
-
-        @pl.when(self.w.z == LAST_Z)
-        def _():
-            for z in (0, 1, 2):
-                self.down_copy(z).start()
+    def launch(self, z):
+        w = self.w
+        self.pair_copy(z).wait_recv()
+
+        def every(send):
+            for part in range(self.parts):
+                add_into(self.piece(self.shard(z, w.core), part), self.piece(self.slot(self.pair, z), part))
+                if send is not None:
+                    send(z, part).start()
+
+        low = (w.z == 0) & (z > 0)
+        high = (w.z == LAST_Z) & (z < LAST_Z)
+        pl.when(low)(lambda: every(self.up_copy))
+        pl.when(high)(lambda: every(self.down_copy))
+        pl.when(jnp.logical_not(low | high))(lambda: every(None))
 
     def pass_up(self, z):
-        self.up_copy(z).wait_recv()
-        add_into(self.shard(z, self.w.core), self.slot(self.up, z - 1))
-        self.up_copy(z).start()
+        for part in range(self.parts):
+            self.up_copy(z, part).wait_recv()
+            add_into(
+                self.piece(self.shard(z, self.w.core), part),
+                self.piece(self.slot(self.up, z - 1), part),
+            )
+            self.up_copy(z, part).start()
 
     def pass_down(self, z):
-        self.down_copy(z).wait_recv()
-        add_into(self.shard(z, self.w.core), self.slot(self.down, z))
-        self.down_copy(z).start()
+        for part in range(self.parts):
+            self.down_copy(z, part).wait_recv()
+            add_into(
+                self.piece(self.shard(z, self.w.core), part),
+                self.piece(self.slot(self.down, z), part),
+            )
+            self.down_copy(z, part).start()
 
     def step(self, k):
         w = self.w
@@ -728,47 +758,54 @@
 
     def finish(self, out):
         w = self.w
-        out[...] = self.shard(w.z, w.core)[...].astype(F32)
-
-        @pl.when(w.z > 0)
-        def _():
-            self.up_copy(w.z).wait_recv()
-            out[...] += self.slot(self.up, w.z - 1)[...].astype(F32)
-
-        @pl.when(w.z < LAST_Z)
-        def _():
-            self.down_copy(w.z).wait_recv()
-            out[...] += self.slot(self.down, w.z)[...].astype(F32)
+        own = self.shard(w.z, w.core)
+        rows = self.rows // self.parts
+
+        def add(part, copy, slot):
+            here = pl.ds(part * rows, rows)
+            copy(w.z, part).wait_recv()
+            out[here, :] += self.piece(slot, part)[...].astype(F32)
+
+        out[...] = own[...].astype(F32)
+        for part in range(self.parts):
+            pl.when(w.z > 0)(
+                lambda part=part: add(part, self.up_copy, self.slot(self.up, w.z - 1))
+            )
+            pl.when(w.z < LAST_Z)(
+                lambda part=part: add(part, self.down_copy, self.slot(self.down, w.z))
+            )
+
+    def drain_pair(self):
+        where = device(self.w, dp=self.w.mate)
+        settle(self.pair, self.pair_sem.at[LAST_Z + 1], self.pair_sem.at[0], where)
 
     def drain(self):
         w = self.w
-
-        def body(z, carry):
-            self.pair_copy(z).wait_send()
-            return carry
-
-        lax.fori_loop(0, LAST_Z + 1, body, 0)
-        for z in range(1, LAST_Z + 1):
-            pl.when(w.z < z)(lambda z=z: self.up_copy(z).wait_send())
+        where = device(w, dp=w.mate)
         for z in range(LAST_Z):
-            pl.when(w.z > z)(lambda z=z: self.down_copy(z).wait_send())
+            sent = self.up.at[pl.ds(0, (LAST_Z - z) * self.rows)]
+            pl.when(w.z == z)(
+                lambda sent=sent: settle(sent, self.line_sem.at[0], self.line_sem.at[2], where)
+            )
+            pl.when(w.z == LAST_Z - z)(
+                lambda sent=sent: settle(sent, self.line_sem.at[1], self.line_sem.at[2], where)
+            )
 
 
 class Exchange:
-    def __init__(self, ref, mine, targets, send, recv):
-        self.ref, self.mine, self.targets, self.send, self.recv = ref, mine, targets, send, recv
-
-    def copy(self, i):
+    def __init__(self, ref, mine, targets, sems):
+        self.ref, self.mine, self.targets, self.sems = ref, mine, targets, sems
+
+    def start(self):
         part = self.ref.at[self.mine]
-        return remote(part, part, self.send.at[i], self.recv.at[i], self.targets[i])
-
-    def start(self):
-        for i in range(len(self.targets)):
-            self.copy(i).start()
+        for target in self.targets:
+            remote(part, part, self.sems.at[0], self.sems.at[1], target).start()
 
     def finish(self):
-        for i in range(len(self.targets)):
-            self.copy(i).wait()
+        count = len(self.targets)
+        some = self.ref.at[pl.ds(0, count)]
+        for sent in (False, True):
+            settle(some, self.sems.at[0], self.sems.at[1], self.targets[0], sent=sent)
 
     def total(self):
         total = self.ref[0].astype(F32)
@@ -879,17 +916,27 @@
     return (1 - odd) * (LAST_Z - i // 2) + odd * (i // 2)
 
 
-def weight_parts(left, right, scatter, store):
-    block = left.shape[1] // (LAST_Z + 1)
-
+def weight_parts(make, scatter):
     def body(i, carry):
         z = ends_first(i)
+        make(z)
+        scatter.pair_copy(z).start()
+        pl.when(i > 0)(lambda: scatter.launch(ends_first(i - 1)))
+        return carry
+
+    lax.fori_loop(0, LAST_Z + 1, body, 0)
+    scatter.launch(ends_first(LAST_Z))
+    scatter.drain_pair()
+
+
+def product_maker(left, right, store):
+    block = left.shape[1] // (LAST_Z + 1)
+
+    def make(z):
         lanes = pl.ds(pl.multiple_of(z * block, LANES), block)
         store(z, dot_tn(left[:, lanes], right[...]).astype(BF16))
-        scatter.pair_copy(z).start()
-        return carry
-
-    lax.fori_loop(0, LAST_Z + 1, body, 0)
+
+    return make
 
 
 def flat_shard(ref, rows):
@@ -919,16 +966,46 @@
     return store
 
 
-def prepare_inputs(r):
-    w, width = r.w, r.pairs * LANES
-    heads = r.a_log_in.shape[0]
+def own_rows(r):
     shard = r.w_x.shape[0]
-    own = pl.ds(pl.multiple_of(w.dp * shard, 16), shard)
-    r.full_x[own, :width] = r.w_x[...]
-    r.full_x[own, width : width + 2 * NSTATE] = r.w_bc[...]
+    return pl.ds(pl.multiple_of(r.w.dp * shard, 16), shard)
+
+
+def input_moves(r):
+    width = r.pairs * LANES
+    own = own_rows(r)
+    block = r.cot.shape[0]
+    mine = pl.ds(pl.multiple_of(r.w.tp * block, block), block)
+    moves = (
+        (r.w_x, r.full_x.at[own, pl.ds(0, width)]),
+        (r.w_bc, r.full_x.at[own, pl.ds(width, 2 * NSTATE)]),
+        (r.x_in, r.x_held),
+        (r.w_z, r.full_z.at[own]),
+        (r.w_out, r.full_out.at[own]),
+        (r.cot, r.row_cot.at[mine]),
+    )
+    return [pltpu.make_async_copy(src, dst, r.s_m.at[i]) for i, (src, dst) in enumerate(moves)]
+
+
+def place_steps(r):
+    heads, shard = r.w_dt.shape
+    mine = r.steps_t.at[pl.ds(pl.multiple_of(r.w.dp * STEP_ROWS, STEP_ROWS), STEP_ROWS)]
     r.turn[...] = jnp.zeros_like(r.turn)
     r.turn[0:heads, 0:shard] = r.w_dt[...]
-    r.full_x[own, width + 2 * NSTATE :] = r.turn[...].T[:shard]
+    mine[...] = r.turn[0:STEP_ROWS, :]
+
+
+def turn_steps(r):
+    shard = r.w_x.shape[0]
+
+    def body(d, carry):
+        r.turn[0:STEP_ROWS, :] = r.steps_t[
+            pl.ds(pl.multiple_of(d * STEP_ROWS, STEP_ROWS), STEP_ROWS), :
+        ]
+        r.full_dt[pl.ds(pl.multiple_of(d * shard, 16), shard), :] = r.turn[...].T[:shard]
+        return carry
+
+    lax.fori_loop(0, 2 * (LAST_Z + 1), body, 0)
 
 
 def prepare_small(r):
@@ -961,44 +1038,46 @@
     w = r.w
     width = r.pairs * LANES
     tokens = r.row_normed.shape[0]
-    block = r.x_in.shape[0]
+    block = r.x_held.shape[0]
     start = pl.multiple_of(w.tp * block, block)
-    shard = r.w_x.shape[0]
-    own = pl.ds(pl.multiple_of(w.dp * shard, 16), shard)
-    prepare_inputs(r)
-    greet(w)
-    r.shard_x.relay(0)
-    norm_rows(r.x_in, r.pre_gain[...].reshape(1, r.x_in.shape[1]), r.row_normed, start)
-    r.row_n.start()
-    moves = [
-        pltpu.make_async_copy(src, dst.at[own], r.s_m.at[i])
-        for i, (src, dst) in enumerate(((r.w_out, r.full_out), (r.w_z, r.full_z)))
-    ]
+    moves = input_moves(r)
     for move in moves:
         move.start()
-    r.row_cot[pl.ds(start, block), :] = r.cot[...]
+    place_steps(r)
+    greet(w)
+    moves[0].wait()
+    moves[1].wait()
+    r.shard_x.relay(0)
+    r.shard_dt.relay(0)
+    moves[2].wait()
+    norm_rows(r.x_held, r.pre_gain[...].reshape(1, r.x_held.shape[1]), r.row_normed, start)
+    r.row_n.start()
     r.state[...] = jnp.zeros_like(r.state)
     prepare_small(r)
-    for move in moves:
+    for move in moves[3:]:
         move.wait()
     r.shard_x.relay(1)
+    r.shard_dt.relay(1)
+    r.shard_x.relay(2)
+    r.shard_dt.relay(2)
     r.row_n.hand_on()
     r.row_c.start()
-    r.shard_x.relay(2)
     r.shard_x.relay(3)
+    r.shard_dt.relay(3)
     r.shard_z.relay(0)
+    r.shard_dt.finish()
+    turn_steps(r)
     r.row_n.finish()
     r.shard_x.finish()
-    r.shard_z.relay(1)
 
     def project_x(rows):
-        out = dot_nn(r.row_normed[rows, :], r.full_x[...])
+        normed = r.row_normed[rows, :]
+        out = dot_nn(normed, r.full_x[...])
         r.xr[rows, :] = out[:, :width]
-        r.bc[rows, :] = out[:, width : width + 2 * NSTATE]
-        r.dtr[rows, :] = out[:, width + 2 * NSTATE :]
+        r.bc[rows, :] = out[:, width:]
+        r.dtr[rows, :] = dot_nn(normed, r.full_dt[...])
 
     by_rows(tokens, 256, project_x)
-    r.shard_z.relay(2)
 
     def body(c):
         prepare_steps(c, r)
@@ -1006,17 +1085,10 @@
 
         @pl.when(c == 1)
         def _():
-            r.shard_z.relay(3)
-            r.shard_out.relay(0)
-
-        @pl.when(c == 3)
-        def _():
-            r.shard_out.relay(1)
+            r.shard_z.relay(1)
             r.row_c.hand_on()
 
-        @pl.when(c == 5)
-        def _():
-            r.shard_out.relay(2)
+        pl.when(c == 5)(lambda: r.shard_z.relay(2))
 
     over_chunks(r, body)
 
@@ -1024,6 +1096,9 @@
 def phase_mid(r):
     w = r.w
     tokens = r.row_normed.shape[0]
+    block = r.x_held.shape[0]
+    r.shard_z.relay(3)
+    r.shard_out.relay(0)
     r.shard_z.finish()
 
     def project_z(rows):
@@ -1032,22 +1107,26 @@
     by_rows(tokens, 256, project_z)
     over_chunks(r, lambda c: square_chunk(c, r))
     r.ex_squares.start()
-    r.shard_out.relay(3)
     r.row_c.finish()
     r.ex_squares.finish()
     over_chunks(r, lambda c: mix_chunk(c, r))
-    weight_parts(r.row_cot, r.mixed, r.grad_out, flat_store(r.out_part, r.shard_rows))
+    r.shard_out.relay(1)
+    weight_parts(
+        product_maker(r.row_cot, r.mixed, flat_store(r.out_part, r.shard_rows)), r.grad_out
+    )
+    tell(r.free_pair, device(w, dp=w.mate))
+    r.shard_out.relay(2)
+    r.grad_out.step(0)
+    r.shard_out.relay(3)
     r.shard_out.finish()
 
     def mix_back(rows):
         r.d_mixed[rows, :] = dot_nn(r.row_cot[rows, :], r.full_out[...])
 
     by_rows(tokens, 256, mix_back)
-    r.grad_out.pair_add()
-    r.grad_out.launch()
     over_chunks(r, lambda c: cross_chunk(c, r))
     r.ex_crosses.start()
-    block = r.x_in.shape[0]
+    r.grad_out.step(1)
 
     def share(slot):
         rows = pl.ds(pl.multiple_of(slot * block, block), block)
@@ -1067,71 +1146,90 @@
     share(w.near_y)
     r.out_rows.start(3)
     share(w.tp)
+    for item in (r.shard_x, r.shard_dt, r.shard_z, r.shard_out, r.row_n, r.row_c):
+        item.drain()
     r.ex_crosses.finish()
-    for item in (r.shard_x, r.shard_z, r.shard_out, r.row_n, r.row_c):
-        item.drain()
     r.g_gate[...] = jnp.zeros_like(r.g_gate)
     over_chunks(r, lambda c: gate_back_chunk(c, r))
-    r.grad_out.step(0)
-    r.out_rows.hand_on()
+    pl.semaphore_wait(r.free_pair, 1)
+    weight_parts(
+        product_maker(r.row_normed, r.d_z, flat_store(r.full_out, r.shard_rows)), r.grad_z
+    )
     tell(r.free_pair, device(w, dp=w.mate))
-    pl.semaphore_wait(r.free_pair, 1)
-    weight_parts(r.row_normed, r.d_z, r.grad_z, flat_store(r.full_out, r.shard_rows))
 
 
 def phase_back(r):
     w = r.w
-    block = r.x_in.shape[0]
+    block = r.x_held.shape[0]
     start_back(r)
-    r.grad_z.pair_add()
-    tell(r.free_pair, device(w, dp=w.mate))
-    r.grad_z.launch()
 
     def body(i, carry):
         scan_chunk_back(r.chunks - 1 - i, r)
 
-        @pl.when(i == 1)
+        @pl.when(i == 0)
         def _():
-            r.grad_out.step(1)
-
-        @pl.when(i == 3)
-        def _():
-            r.grad_out.finish(r.o_w_out)
+            r.grad_out.finish(r.v_w_out)
+            r.put(r.v_w_out, r.o_w_out, 0).start()
             r.grad_out.drain()
             tell(r.free_line, device(w, dp=other_z(w, 1)))
             tell(r.free_line, device(w, dp=other_z(w, 3)))
+
+        @pl.when(i == 2)
+        def _():
+            r.out_rows.hand_on()
             r.grad_z.step(0)
 
-        @pl.when(i == 5)
-        def _():
-            r.out_rows.finish()
-            step = 64
-
-            def add(k, carry):
-                here = pl.ds(pl.multiple_of(k * step, step), step)
-                there = pl.ds(pl.multiple_of(w.tp * block + k * step, 16), step)
-                total = r.x_in[here, :].astype(F32) + r.out_rows.total(here, there)
-                r.o_block[here, :] = total.astype(BF16)
-                return carry
-
-            lax.fori_loop(0, block // step, add, 0)
-            r.out_rows.drain()
-            tell(r.free_row, device(w, tp=w.near_x))
-            tell(r.free_row, device(w, tp=w.near_y))
-            r.grad_z.step(1)
-
+        pl.when(i == 5)(lambda: r.grad_z.step(1))
         return carry
 
     lax.fori_loop(0, r.chunks, body, 0)
+
+
+def finish_block(r):
+    w = r.w
+    block = r.x_held.shape[0]
+    step = 64
+    r.out_rows.finish()
+
+    def add(k, carry):
+        here = pl.ds(pl.multiple_of(k * step, step), step)
+        there = pl.ds(pl.multiple_of(w.tp * block + k * step, 16), step)
+        total = r.x_held[here, :].astype(F32) + r.out_rows.total(here, there)
+        r.v_block[here, :] = total.astype(BF16)
+        return carry
+
+    lax.fori_loop(0, block // step, add, 0)
+    r.put(r.v_block, r.o_block, 1).start()
+    r.out_rows.drain()
+    tell(r.free_row, device(w, tp=w.near_x))
+    tell(r.free_row, device(w, tp=w.near_y))
+
+
+def step_parts(r, at):
+    shard = r.shard_rows
+    out = dot_tn(r.d_rest[:, at : at + LANES], r.row_normed[...])[:STEP_ROWS]
+    for d in range(2 * (LAST_Z + 1)):
+        here = slice(d * STEP_ROWS, (d + 1) * STEP_ROWS)
+        r.dt_part[here, 0:shard] = out[:, d * shard : (d + 1) * shard]
 
 
 def phase_last(r):
     w = r.w
     width = r.pairs * LANES
-    block = r.x_in.shape[0]
+    block = r.x_held.shape[0]
+    edge = width + 2 * NSTATE
     weight_parts(
-        r.row_normed, r.d_rest.at[:, pl.ds(width, 2 * NSTATE + LANES)], r.grad_bc, flat_store(r.bc_part, r.shard_rows)
-    )
+        product_maker(
+            r.row_normed,
+            r.d_rest.at[:, pl.ds(width, 2 * NSTATE)],
+            flat_store(r.bc_part, r.shard_rows),
+        ),
+        r.grad_bc,
+    )
+    step_parts(r, edge)
+    for z in range(LAST_Z + 1):
+        r.grad_dt.pair_copy(z).start()
+    finish_block(r)
     r.g_pre[...] = jnp.zeros_like(r.g_pre)
     pl.semaphore_wait(r.free_row, 2)
 
@@ -1141,81 +1239,120 @@
 
         def body(n, carry):
             cols = pl.ds(pl.multiple_of(n * tile, tile), tile)
-            out = dot_nt(r.d_z[rows, :], r.full_z[cols, :]) + dot_nt(
-                r.d_rest[rows, :], r.full_x[cols, :]
-            )
+            out = dot_nt(r.d_z[rows, :], r.full_z[cols, :])
+            out = out + dot_nt(r.d_rest[rows, :edge], r.full_x[cols, :])
+            out = out + dot_nt(r.d_rest[rows, edge:], r.full_dt[cols, :])
             r.part[rows, cols] = out.astype(BF16)
             r.g_pre[:, cols] += fold_rows(out * r.row_normed[rows, cols].astype(F32))
             return carry
 
         lax.fori_loop(0, r.part.shape[1] // tile, body, 0)
 
-    r.grad_bc.pair_add()
-    r.grad_bc.launch()
     share(w.across)
     r.in_rows.start(0, 1)
+    for z in (3, 0, 2, 1):
+        r.grad_dt.launch(z)
+    r.grad_dt.drain_pair()
+    pl.semaphore_wait(r.free_pair, 1)
+    pl.semaphore_wait(r.free_line, 2)
+    weight_parts(
+        product_maker(
+            r.row_normed,
+            r.d_rest.at[:, pl.ds(0, width)],
+            side_store(r.row_cot, r.shard_rows, width),
+        ),
+        r.grad_x_part,
+    )
+    r.grad_bc.step(0)
+    r.grad_dt.step(0)
     share(w.near_x)
     r.in_rows.start(2)
-    r.grad_bc.step(0)
     share(w.near_y)
     r.in_rows.start(3)
+    r.grad_bc.step(1)
+    r.grad_dt.step(1)
     share(w.tp)
     pack_small(r)
     r.ex_pair.start()
-    r.grad_bc.step(1)
-    pl.semaphore_wait(r.free_pair, 1)
-    weight_parts(
-        r.row_normed,
-        r.d_rest.at[:, pl.ds(0, width)],
-        r.grad_x_part,
-        side_store(r.row_cot, r.shard_rows, width),
-    )
-    r.grad_z.finish(r.o_w_z)
+    r.grad_z.finish(r.v_w_z)
+    r.put(r.v_w_z, r.o_w_z, 2).start()
+    r.grad_x_part.step(0)
     r.in_rows.hand_on()
+    again = [
+        pltpu.make_async_copy(r.cot.at[pl.ds(k * (block // 2), block // 2)], r.far.at[k], r.s_m.at[k])
+        for k in range(2)
+    ]
+    for copy in again:
+        copy.start()
     r.ex_pair.finish()
     r.small_z.at[w.z][...] = r.ex_pair.total()
     r.ex_z.start()
-    r.grad_x_part.pair_add()
-    pl.semaphore_wait(r.free_line, 2)
-    r.grad_x_part.launch()
     r.grad_bc.finish(r.bc_sum)
-    r.o_w_dt[...] = r.bc_sum[:, 2 * NSTATE :]
-    r.bc_slots.at[w.tp][...] = r.bc_sum[:, : 2 * NSTATE].astype(BF16)
+    r.grad_dt.finish(r.v_w_dt)
+    r.put(r.v_w_dt, r.o_w_dt, 3).start()
+    r.bc_slots.at[w.tp][...] = r.bc_sum[...].astype(BF16)
     r.ex_bc.start()
     r.ex_z.finish()
     total = r.ex_z.total()
-    r.o_small[...] = total[:SMALL_DP]
+    r.v_small[...] = total[:SMALL_DP]
+    r.put(r.v_small, r.o_small, 4).start()
     r.small_t.at[w.tp][...] = total[SMALL_DP:]
     r.ex_t.start()
-    r.grad_x_part.step(0)
+    r.grad_x_part.step(1)
     r.ex_bc.finish()
-    r.o_w_bc[...] = r.ex_bc.total()
+    r.v_w_bc[...] = r.ex_bc.total()
+    r.put(r.v_w_bc, r.o_w_bc, 5).start()
     r.ex_t.finish()
-    r.o_shared[...] = r.ex_t.total()
-    r.grad_x_part.step(1)
+    shared = r.ex_t.total()
+    gain = r.pre_gain[...].reshape(1, r.x_held.shape[1])
+    count = gain.shape[1] // LANES
+    r.v_shared[...] = shared
+    for p in range(count):
+        r.v_shared[p : p + 1, :] = shared[p : p + 1, :] / gain[:, p * LANES : (p + 1) * LANES]
+    r.put(r.v_shared, r.o_shared, 6).start()
+    for copy in again:
+        copy.wait()
     r.in_rows.finish()
-    gain = r.pre_gain[...].reshape(1, r.x_in.shape[1])
     step = 64
 
     def body(k, carry):
         here = pl.ds(pl.multiple_of(k * step, step), step)
         there = pl.ds(pl.multiple_of(w.tp * block + k * step, 16), step)
-        values = r.x_in[here, :].astype(F32)
+        half = k // (block // 2 // step)
+        inner = pl.ds(pl.multiple_of(k * step - half * (block // 2), step), step)
+        values = r.x_held[here, :].astype(F32)
         scale = lax.rsqrt(jnp.mean(values * values, axis=1, keepdims=True) + EPS)
         weighted = r.in_rows.total(here, there) * gain
         along = jnp.mean(weighted * values, axis=1, keepdims=True)
-        grad = r.cot[here, :].astype(F32) + scale * weighted
-        r.o_grad_x[here, :] = (grad - values * (scale * scale * scale * along)).astype(BF16)
+        grad = r.far[half, inner, :].astype(F32) + scale * weighted
+        r.v_grad_x[here, :] = (grad - values * (scale * scale * scale * along)).astype(BF16)
         return carry
 
     lax.fori_loop(0, block // step, body, 0)
-    r.grad_x_part.finish(r.o_w_x)
-    for item in (r.grad_z, r.grad_bc, r.grad_x_part, r.in_rows):
+    r.put(r.v_grad_x, r.o_grad_x, 7).start()
+    for item in (r.grad_z, r.grad_bc, r.grad_dt, r.in_rows):
         item.drain()
-
-
-SMALL_DP = 48
+    r.grad_x_part.finish(r.v_w_x)
+    r.put(r.v_w_x, r.o_w_x, 8).start()
+    r.grad_x_part.drain()
+    ends = ("w_out", "block", "w_z", "w_dt", "small", "w_bc", "shared", "grad_x", "w_x")
+    for i, name in enumerate(ends):
+        r.put(getattr(r, "v_" + name), getattr(r, "o_" + name), i).wait()
+
+
+SMALL_DP = 40
 SMALL_ALL = 24
+
+
+def head_row(r):
+    lane = lax.broadcasted_iota(jnp.int32, (1, LANES), 1)
+    out = jnp.zeros((1, LANES), F32)
+    for p in range(r.pairs):
+        tile = jnp.sum(r.g_skip[:, p * LANES : (p + 1) * LANES], axis=0, keepdims=True)
+        for k, part in enumerate((lane < HEADDIM, lane >= HEADDIM)):
+            head = jnp.sum(jnp.where(part, tile, 0.0), axis=1, keepdims=True)
+            out = jnp.where(lane == 2 * p + k, head, out)
+    return out
 
 
 def pack_small(r):
@@ -1234,7 +1371,8 @@
     for k in range(4):
         at = put(at, r.g_cxw, 8 * k, r.pairs)
     at = put(at, r.g_cxb, 0, r.pairs)
-    at = put(at, r.g_skip, 0, r.pairs)
+    mine[at : at + 1, :] = head_row(r)
+    at = at + 1
     at = put(at, r.g_alog, 0, 1)
     at = put(at, r.g_dtb, 0, 1)
     at = put(SMALL_DP, r.g_pre, 0, r.g_pre.shape[1] // LANES)
@@ -1272,29 +1410,33 @@
     r.shard_rows = r.w_x.shape[0]
     r.xr_at = r.bc_at = r.dtr_at = 0
     r.dx_at, r.dbc_at, r.ddt_at = 0, width, width + 2 * NSTATE
-    r.shard_x = LineGather(w, r.full_x, r.s_w.at[0], r.r_w.at[0])
-    r.shard_z = LineGather(w, r.full_z, r.s_w.at[1], r.r_w.at[1])
-    r.shard_out = LineGather(w, r.full_out, r.s_w.at[2], r.r_w.at[2])
+    gather = lambda i, ref: LineGather(w, ref, r.s_w.at[i], r.r_w.at[i], PARTS)
+    r.shard_x = gather(0, r.full_x)
+    r.shard_z = gather(1, r.full_z)
+    r.shard_out = gather(2, r.full_out)
+    r.shard_dt = LineGather(w, r.steps_t, r.s_d, r.r_d, 1)
     r.row_n = RowGather(w, r.row_normed, r.s_r.at[0], r.r_r.at[0])
     r.row_c = RowGather(w, r.row_cot, r.s_r.at[1], r.r_r.at[1])
-    r.out_rows = RowScatter(w, r.part, r.far, r.near, r.s_q.at[0], r.r_q.at[0])
-    r.in_rows = RowScatter(w, r.part, r.far, r.near, r.s_q.at[1], r.r_q.at[1])
+    r.out_rows = r.in_rows = RowScatter(w, r.part, r.far, r.near, r.s_q.at[0], r.r_q)
     rows = r.shard_rows
-    scatter = lambda i, shard, pair, up, down: LineScatter(
-        w, shard, pair, up, down, r.s_l.at[i], r.r_l.at[i]
-    )
-    r.grad_out = scatter(0, flat_shard(r.out_part, rows), r.pair, r.up, r.down)
-    r.grad_z = scatter(1, flat_shard(r.full_out, rows), r.pair, r.up_z, r.down_z)
-    r.grad_x_part = scatter(3, side_shard(r.row_cot, rows, width), r.pair, r.up, r.down)
+    held = (r.pair, r.up, r.down, r.p_main, r.l_main, PARTS)
+    r.grad_out = LineScatter(w, flat_shard(r.out_part, rows), *held)
+    r.grad_x_part = LineScatter(w, side_shard(r.row_cot, rows, width), *held)
+    r.grad_z = LineScatter(
+        w, flat_shard(r.full_out, rows), r.pair, r.up_z, r.down_z, r.p_main, r.l_z, PARTS
+    )
+    held_dt = (r.pair_dt, r.up_dt, r.down_dt, r.p_dt, r.l_dt, 1)
+    r.grad_dt = LineScatter(w, flat_shard(r.dt_part, STEP_ROWS), *held_dt)
     in_row = [device(w, tp=t) for t in (w.near_x, w.near_y, w.across)]
     in_line = [device(w, dp=other_z(w, k)) for k in (1, 2, 3)]
-    exchange = lambda i, ref, mine, targets: Exchange(ref, mine, targets, r.s_e.at[i], r.r_e.at[i])
+    exchange = lambda i, ref, mine, targets: Exchange(ref, mine, targets, r.s_e.at[i])
     r.ex_squares = exchange(0, r.squares, w.tp, in_row)
     r.ex_crosses = exchange(1, r.crosses, w.tp, in_row)
     r.ex_pair = exchange(2, r.small_pair, w.core, [device(w, dp=w.mate)])
     r.ex_z = exchange(3, r.small_z, w.z, in_line)
     r.ex_t = exchange(4, r.small_t, w.tp, in_row)
     r.ex_bc = exchange(5, r.bc_slots, w.tp, in_row)
+    r.put = lambda src, dst, i: pltpu.make_async_copy(src, dst, r.s_o.at[i])
     tokens = r.chunks * CHUNK
     phase_one(r)
 
@@ -1308,13 +1450,14 @@
         pltpu.VMEM((tokens, width), F32),
         pltpu.VMEM((tokens, width), BF16),
     )
-    later = dict(BACK_SCRATCH(width), bc_part=((r.full_x.shape[0], 2 * NSTATE + LANES), BF16))
+    later = dict(BACK_SCRATCH(width), bc_part=((r.full_x.shape[0], 2 * NSTATE), BF16))
 
     def rest(d_rest, *buffers):
         r.d_rest = r.d_proj = d_rest
         for name, buffer in zip(later, buffers):
             setattr(r, name, buffer)
-        r.grad_bc = scatter(2, flat_shard(r.bc_part, rows), r.pair_bc, r.up_bc, r.down_bc)
+        held_bc = (r.pair_bc, r.up_bc, r.down_bc, r.p_bc, r.l_bc, 1)
+        r.grad_bc = LineScatter(w, flat_shard(r.bc_part, rows), *held_bc)
         phase_back(r)
         phase_last(r)
 
@@ -1330,32 +1473,36 @@
     features, block = x_in.shape[1], x_in.shape[0]
     tokens = block * 4
     shard = w_x.shape[0]
-    rest = 2 * NSTATE + LANES
+    maps = 2 * NSTATE
     chunks = tokens // CHUNK
+    turned_step = (STEP_ROWS, 2 * LANES)
     outs = dict(
-        o_block=((block, features), BF16),
-        o_grad_x=((block, features), BF16),
-        o_w_z=((shard, width), F32),
-        o_w_x=((shard, width), F32),
-        o_w_bc=((shard, 2 * NSTATE), F32),
-        o_w_dt=((shard, LANES), F32),
-        o_w_out=((shard, width), F32),
-        o_small=((SMALL_DP, LANES), F32),
-        o_shared=((SMALL_ALL, LANES), F32),
+        block=((block, features), BF16),
+        grad_x=((block, features), BF16),
+        w_z=((shard, width), F32),
+        w_x=((shard, width), F32),
+        w_bc=((shard, maps), F32),
+        w_dt=(turned_step, F32),
+        w_out=((shard, width), F32),
+        small=((SMALL_DP, LANES), F32),
+        shared=((SMALL_ALL, LANES), F32),
     )
     scratch = dict(
+        x_held=((block, features), BF16),
         row_normed=((tokens, features), BF16),
         row_cot=((tokens, features), BF16),
-        full_x=((features, width + rest), BF16),
+        full_x=((features, width + maps), BF16),
         full_z=((features, width), BF16),
         full_out=((features, width), BF16),
+        full_dt=((features, LANES), BF16),
+        steps_t=((8 * STEP_ROWS, 2 * LANES), BF16),
         xr=((tokens, width), F32),
-        bc=((tokens, 2 * NSTATE), F32),
+        bc=((tokens, maps), F32),
         dtr=((tokens, LANES), F32),
         y=((tokens, width), F32),
         pre_x=((tokens, width), F32),
-        pre_bc=((tokens, 2 * NSTATE), F32),
-        maps=((tokens, 2 * NSTATE), BF16),
+        pre_bc=((tokens, maps), F32),
+        maps=((tokens, maps), BF16),
         states=((tokens, width), BF16),
         state=((NSTATE, width), F32),
         step=((tokens, LANES), F32),
@@ -1367,7 +1514,7 @@
         a_log=((1, LANES), F32),
         dt_bias=((1, LANES), F32),
         cxb=((1, width), F32),
-        cbb=((1, 2 * NSTATE), F32),
+        cbb=((1, maps), F32),
         gain=((1, width), F32),
         skip=((1, width), F32),
         squares=((4, chunks, LANES), F32),
@@ -1378,54 +1525,65 @@
         far=((2, block // 2, features), BF16),
         near=((2, block, features), BF16),
         out_part=((features, width), BF16),
+        dt_part=((8 * STEP_ROWS, 2 * LANES), F32),
         pair=((4 * shard, width), BF16),
-        pair_bc=((4 * shard, rest), BF16),
+        pair_bc=((4 * shard, maps), BF16),
+        pair_dt=((4 * STEP_ROWS, 2 * LANES), F32),
         up=((3 * shard, width), BF16),
         down=((3 * shard, width), BF16),
         up_z=((3 * shard, width), BF16),
         down_z=((3 * shard, width), BF16),
-        up_bc=((3 * shard, rest), BF16),
-        down_bc=((3 * shard, rest), BF16),
-        bc_sum=((shard, rest), F32),
-        bc_slots=((4, shard, 2 * NSTATE), BF16),
+        up_bc=((3 * shard, maps), BF16),
+        down_bc=((3 * shard, maps), BF16),
+        up_dt=((3 * STEP_ROWS, 2 * LANES), F32),
+        down_dt=((3 * STEP_ROWS, 2 * LANES), F32),
+        bc_sum=((shard, maps), F32),
+        bc_slots=((4, shard, maps), BF16),
         small_pair=((2, SMALL_DP + SMALL_ALL, LANES), F32),
         small_z=((4, SMALL_DP + SMALL_ALL, LANES), F32),
         small_t=((4, SMALL_ALL, LANES), F32),
         g_gate=((8, width), F32),
         g_pre=((8, features), F32),
         **GRAD_OUT(width),
+        **{"v_" + name: spec for name, spec in outs.items()},
     )
     dma = pltpu.SemaphoreType.DMA
     signal = pltpu.SemaphoreType.REGULAR
     semaphores = dict(
-        s_w=dma((3, 4, 4)),
-        r_w=dma((3, 8)),
-        s_r=dma((2, 4)),
-        r_r=dma((2, 4)),
-        s_q=dma((2, 6)),
-        r_q=dma((2, 6)),
-        s_l=dma((4, 10)),
-        r_l=dma((4, 10)),
-        s_e=dma((6, 3)),
-        r_e=dma((6, 3)),
-        s_m=dma((2,)),
+        s_w=dma((3, 3)),
+        r_w=dma((3, 4 * PARTS + 1)),
+        s_d=dma((3,)),
+        r_d=dma((5,)),
+        s_r=dma((2,)),
+        r_r=dma((2, 3)),
+        s_q=dma((1,)),
+        r_q=dma((3,)),
+        p_main=dma((5,)),
+        p_bc=dma((5,)),
+        p_dt=dma((5,)),
+        l_main=dma((2 + 6 * PARTS,)),
+        l_z=dma((2 + 6 * PARTS,)),
+        l_bc=dma((8,)),
+        l_dt=dma((8,)),
+        s_e=dma((6, 2)),
+        s_m=dma((6,)),
+        s_o=dma((len(outs),)),
         free_pair=signal,
         free_line=signal,
         free_row=signal,
     )
-    names = RAW_IN + tuple(outs) + tuple(scratch) + tuple(semaphores)
+    names = RAW_IN + tuple("o_" + name for name in outs) + tuple(scratch) + tuple(semaphores)
     values = list(args)
     values[6] = values[6].T
     values[15] = values[15].T
     whole = pl.BlockSpec(memory_space=pltpu.VMEM)
+    apart = pl.BlockSpec(memory_space=pl.ANY)
+    moved = ("x_in", "w_z", "w_x", "w_bc", "w_out", "cot")
     out = pl.pallas_call(
         functools.partial(whole_kernel, names=names, width=width),
         out_shape=tuple(jax.ShapeDtypeStruct(*spec) for spec in outs.values()),
-        in_specs=[
-            pl.BlockSpec(memory_space=pl.ANY) if name in ("w_z", "w_out") else whole
-            for name in RAW_IN
-        ],
-        out_specs=tuple([whole] * len(outs)),
+        in_specs=[apart if name in moved else whole for name in RAW_IN],
+        out_specs=tuple([apart] * len(outs)),
         scratch_shapes=[pltpu.VMEM(*spec) for spec in scratch.values()]
         + list(semaphores.values()),
         compiler_params=pltpu.CompilerParams(
@@ -1435,39 +1593,106 @@
             flops=5 * 10**10, bytes_accessed=1 << 26, transcendentals=0
         ),
     )(*values)
-    return types.SimpleNamespace(**dict(zip(outs, out)))
+    return dict(zip(outs, out))
+
+
+LARGE = ("block", "grad_x", "w_z", "w_x", "w_bc", "w_out")
+FINAL = ("pre", "dt", "cxw", "cxb", "cbw", "cbb", "alog", "dtb", "skip", "gate")
+
+
+def publish_kernel(*refs):
+    count = len(LARGE)
+    large_in, (steps, small, shared) = refs[:count], refs[count : count + 3]
+    large_out = refs[count + 3 : 2 * count + 3]
+    o = types.SimpleNamespace(**dict(zip(FINAL, refs[2 * count + 3 : -1])))
+    sem = refs[-1]
+    moves = [
+        pltpu.make_async_copy(src, dst, sem.at[i])
+        for i, (src, dst) in enumerate(zip(large_in, large_out))
+    ]
+    for move in moves:
+        move.start()
+    heads = o.alog.shape[0]
+
+    def line(out, src, at):
+        for p in range(out.shape[0] // LANES):
+            out[p * LANES : (p + 1) * LANES] = src[at + p : at + p + 1, :].reshape(LANES)
+        return at + out.shape[0] // LANES
+
+    def taps(out, src, at):
+        count = out.shape[1] // LANES
+        for k in range(4):
+            for p in range(count):
+                out[k : k + 1, p * LANES : (p + 1) * LANES] = src[at + p : at + p + 1, :]
+            at = at + count
+        return at
+
+    at = line(o.gate, small, 0)
+    at = taps(o.cxw, small, at)
+    at = line(o.cxb, small, at)
+    for out in (o.skip, o.alog, o.dtb):
+        out[...] = small[at : at + 1, 0:heads].reshape(heads)
+        at = at + 1
+    at = line(o.pre, shared, 0)
+    at = taps(o.cbw, shared, at)
+    line(o.cbb, shared, at)
+    o.dt[...] = steps[0:heads, 0 : o.dt.shape[1]]
+    for move in moves:
+        move.wait()
+
+
+def publish(o, width, heads):
+    features = o["block"].shape[1]
+    shard = o["w_z"].shape[0]
+    shapes = dict(
+        pre=(features,),
+        dt=(heads, shard),
+        cxw=(4, width),
+        cxb=(width,),
+        cbw=(4, 2 * NSTATE),
+        cbb=(2 * NSTATE,),
+        alog=(heads,),
+        dtb=(heads,),
+        skip=(heads,),
+        gate=(width,),
+    )
+    whole = pl.BlockSpec(memory_space=pltpu.VMEM)
+    apart = pl.BlockSpec(memory_space=pl.ANY)
+    large = [o[name] for name in LARGE]
+    out = pl.pallas_call(
+        publish_kernel,
+        out_shape=tuple(
+            [jax.ShapeDtypeStruct(v.shape, v.dtype) for v in large]
+            + [jax.ShapeDtypeStruct(shapes[name], F32) for name in FINAL]
+        ),
+        in_specs=[apart] * len(large) + [whole] * 3,
+        out_specs=tuple([whole] * (len(large) + len(FINAL))),
+        scratch_shapes=[pltpu.SemaphoreType.DMA((len(large),))],
+    )(*large, o["w_dt"], o["small"], o["shared"])
+    return types.SimpleNamespace(**dict(zip(LARGE + FINAL, out)))
 
 
 def on_device_whole(*args):
     width = args[3].shape[1]
     heads = args[11].shape[0]
-    features = args[0].shape[1]
-    o = whole_call(args, width)
-    pairs = width // LANES
-    small = o.o_small
-    rows = lambda at, count: small[at : at + count].reshape(count * LANES)
-    taps = small[pairs : 5 * pairs].reshape(4, width)
-    skip = jnp.sum(rows(6 * pairs, pairs).reshape(heads, HEADDIM), axis=1)
-    shared = o.o_shared.reshape(-1)
-    taps_bc = shared[features : features + 4 * 2 * NSTATE].reshape(4, 2 * NSTATE)
-    at = features + 4 * 2 * NSTATE
+    p = publish(whole_call(args, width), width, heads)
     return (
-        o.o_block,
-        o.o_grad_x,
-        shared[:features] / args[2],
-        o.o_w_z,
-        o.o_w_x,
-        o.o_w_bc,
-        o.o_w_dt[:, :heads],
-        taps,
-        rows(5 * pairs, pairs),
-        taps_bc,
-        shared[at : at + 2 * NSTATE],
-        small[7 * pairs, :heads],
-        small[7 * pairs + 1, :heads],
-        skip,
-        rows(0, pairs),
-        o.o_w_out.T,
+        p.block,
+        p.grad_x,
+        p.pre,
+        p.w_z,
+        p.w_x,
+        p.w_bc,
+        p.dt.T,
+        p.cxw,
+        p.cxb,
+        p.cbw,
+        p.cbb,
+        p.alog,
+        p.dtb,
+        p.skip,
+        p.gate,
+        p.w_out.T,
     )
 
 

time: 205 us -> 173 us (0.84)
  Pallas kernels: 189 us -> 170 us
  local copies, waits for them, and re-layouts: 13.4 us -> 0 us
    pallas_call x1, Pallas kernels: 189 us -> 165 us  [whole_call(): pl.pallas_call(functools.partial(whole_kernel, names=names, width=width),...]
    unnamed x23 -> x0, local copies, waits for them, and re-layouts: 8.16 us -> none
    pallas_call x0 -> x1, Pallas kernels: none -> 4.57 us  [publish(): pl.pallas_call(publish_kernel, out_shape=tuple([jax.ShapeDtypeStruct(v.sh...]
    reshape x3 -> x0, local copies, waits for them, and re-layouts: 2.58 us -> none  [the longest x1 1.37 us: on_device_whole(): rows = lambda at, count: small[at:at + count].reshape(count * LANES)]
where the time goes in v3:
time: 173 us; the launch traced here: 171 us
  Pallas kernels  170 us (98%)
    pallas_call x1, Pallas kernels, whole_call(): pl.pallas_call(functools.partial(whole_kernel, names=names, width=width),...  165 us
    pallas_call x1, Pallas kernels, publish(): pl.pallas_call(publish_kernel, out_shape=tuple([jax.ShapeDtypeStruct(v.sh...  4.57 us

profile of v3, /device:TPU:0, one launch (start us, length us, event | category | flops | bytes accessed | tf_op | source)
XLA Modules:
  0.0 170.7 jit_solution(14207629965772017199)
XLA Ops:
  0.7 165.3 %shard_map.288 = (bf16[256,1536]{1,0:T(8,128)(2,1)}, bf16[256,1536]{1,0:T(8,128)(2,1)}, f32[192,768]{1,0:T(8,128)}, f32[192,768]{1,0:T(8,128)}, f32[192,256]{1,0...) custom-call(bf16[256,1536]{1,0:T(8,128)(2,1)} %refs_0_.1, ...), custom_call_target="tpu_custom_call" | custom-call | flops 49999998976 | bytes 67108864 | tf_op jit(solution)/shard_map/pallas_call | solution.py:1582
  166.0 4.6 %shard_map.289 = (bf16[256,1536]{1,0:T(8,128)(2,1)}, bf16[256,1536]{1,0:T(8,128)(2,1)}, f32[192,768]{1,0:T(8,128)}, f32[192,768]{1,0:T(8,128)}, f32[192,256]{1,0...) custom-call(bf16[256,1536]{1,0:T(8,128)(2,1)} %get-tuple-element.41., ...), custom_call_target="tpu_custom_call" | custom-call | tf_op jit(solution)/shard_map/pallas_call | solution.py:1662

commit v4 on v3

--- a/solution.py
+++ b/solution.py
@@ -493,7 +493,6 @@
     def __init__(self, w, ref, send, recv, parts):
         self.w, self.ref, self.send, self.recv, self.parts = w, ref, send, recv, parts
         self.rows = ref.shape[0] // (2 * (LAST_Z + 1))
-        self.joint = recv.at[parts * (LAST_Z + 1)]
 
     def shard(self, z, core, part):
         rows = self.rows // self.parts
@@ -504,8 +503,8 @@
         w = self.w
         block = self.shard(z, w.core, part)
         to = {UP: w.dp + 2, DOWN: w.dp - 2}.get(kind, w.mate)
-        recv = self.joint if kind == PAIR else self.recv.at[part * (LAST_Z + 1) + z]
-        return remote(block, block, self.send.at[kind], recv, device(w, dp=to))
+        first = (self.parts if kind == PAIR else part) * (LAST_Z + 1)
+        return remote(block, block, self.send.at[kind], self.recv.at[first + z], device(w, dp=to))
 
     def relay(self, step):
         for part in range(self.parts):
@@ -538,24 +537,25 @@
     def some(self, count):
         return self.ref.at[pl.ds(0, count * self.rows)]
 
+    def from_mate(self, z):
+        block = self.some(1)
+        recv = self.recv.at[self.parts * (LAST_Z + 1) + z]
+        settle(block, self.send.at[PAIR], recv, device(self.w, dp=self.w.mate), sent=False)
+
     def finish(self):
-        where = device(self.w, dp=self.w.mate)
-        settle(self.some(LAST_Z + 1), self.send.at[PAIR], self.joint, where, sent=False)
+        for z in range(LAST_Z + 1):
+            self.from_mate(z)
 
     def drain(self):
         w = self.w
-        settle(self.some(LAST_Z + 1), self.send.at[PAIR], self.joint, device(w, dp=w.mate))
+        where = device(w, dp=w.mate)
+        wait = lambda count, kind: settle(
+            self.some(count), self.send.at[kind], self.recv.at[0], where
+        )
+        wait(LAST_Z + 1, PAIR)
         for z in range(LAST_Z):
-            pl.when(w.z == z)(
-                lambda z=z: settle(
-                    self.some(z + 1), self.send.at[UP], self.joint, device(w, dp=w.mate)
-                )
-            )
-            pl.when(w.z == LAST_Z - z)(
-                lambda z=z: settle(
-                    self.some(z + 1), self.send.at[DOWN], self.joint, device(w, dp=w.mate)
-                )
-            )
+            pl.when(w.z == z)(lambda z=z: wait(z + 1, UP))
+            pl.when(w.z == LAST_Z - z)(lambda z=z: wait(z + 1, DOWN))
 
 
 class RowGather:
@@ -911,21 +911,75 @@
         r.d_z[rows, lanes] = (d_gated * y * (gate * (1.0 + z * (1.0 - gate)))).astype(BF16)
 
 
-def ends_first(i):
-    odd = lax.rem(i, 2)
-    return (1 - odd) * (LAST_Z - i // 2) + odd * (i // 2)
+def by_distance(z, i):
+    upper = z // 2
+    low = z + upper * (LAST_Z - 2 * z)
+    chip = low + i * (1 - 2 * low) if i < 2 else i
+    return chip + upper * (LAST_Z - 2 * chip)
+
+
+def chip_rows(r, z):
+    count = 2 * r.shard_rows
+    return pl.ds(pl.multiple_of(z * count, LANES), count)
+
+
+def accumulate(ref, rows, value, first):
+    if first:
+        ref[rows, :] = value
+    else:
+        ref[rows, :] += value
+
+
+def project_z(r, i):
+    z = by_distance(r.w.z, i)
+    r.shard_z.from_mate(z)
+    here = chip_rows(r, z)
+
+    def body(rows):
+        accumulate(r.z, rows, dot_nn(r.row_normed[rows, here], r.full_z[here, :]), i == 0)
+
+    by_rows(r.row_normed.shape[0], 256, body)
+
+
+def output_back(r, i):
+    z = by_distance(r.w.z, i)
+    r.shard_out.from_mate(z)
+    here = chip_rows(r, z)
+
+    def body(rows):
+        accumulate(r.d_mixed, rows, dot_nn(r.row_cot[rows, here], r.full_out[here, :]), i == 0)
+
+    by_rows(r.row_normed.shape[0], 256, body)
+
+
+def output_share(r, slot):
+    block = r.x_held.shape[0]
+    rows = pl.ds(pl.multiple_of(slot * block, block), block)
+    tile = 512
+
+    def body(n, carry):
+        cols = pl.ds(pl.multiple_of(n * tile, tile), tile)
+        r.part[rows, cols] = dot_nt(r.mixed[rows, :], r.full_out[cols, :]).astype(BF16)
+        return carry
+
+    lax.fori_loop(0, r.part.shape[1] // tile, body, 0)
+
+
+def far_first(w, i):
+    upper = w.z // 2
+    return (1 - upper) * (LAST_Z - i) + upper * i
 
 
 def weight_parts(make, scatter):
     def body(i, carry):
-        z = ends_first(i)
+        z = far_first(scatter.w, i)
         make(z)
         scatter.pair_copy(z).start()
-        pl.when(i > 0)(lambda: scatter.launch(ends_first(i - 1)))
+        pl.when(i > 0)(lambda: scatter.launch(far_first(scatter.w, i - 1)))
         return carry
 
     lax.fori_loop(0, LAST_Z + 1, body, 0)
-    scatter.launch(ends_first(LAST_Z))
+    scatter.launch(far_first(scatter.w, LAST_Z))
     scatter.drain_pair()
 
 
@@ -1086,76 +1140,68 @@
         @pl.when(c == 1)
         def _():
             r.shard_z.relay(1)
+            r.shard_out.relay(0)
+            project_z(r, 0)
+
+        @pl.when(c == 3)
+        def _():
             r.row_c.hand_on()
-
-        pl.when(c == 5)(lambda: r.shard_z.relay(2))
+            project_z(r, 1)
+
+        @pl.when(c == 5)
+        def _():
+            r.shard_z.relay(2)
+            project_z(r, 2)
 
     over_chunks(r, body)
 
 
 def phase_mid(r):
     w = r.w
-    tokens = r.row_normed.shape[0]
-    block = r.x_held.shape[0]
+    r.shard_out.relay(1)
     r.shard_z.relay(3)
-    r.shard_out.relay(0)
-    r.shard_z.finish()
-
-    def project_z(rows):
-        r.z[rows, :] = dot_nn(r.row_normed[rows, :], r.full_z[...])
-
-    by_rows(tokens, 256, project_z)
+    project_z(r, 3)
     over_chunks(r, lambda c: square_chunk(c, r))
     r.ex_squares.start()
+    r.shard_out.relay(2)
     r.row_c.finish()
     r.ex_squares.finish()
     over_chunks(r, lambda c: mix_chunk(c, r))
-    r.shard_out.relay(1)
     weight_parts(
         product_maker(r.row_cot, r.mixed, flat_store(r.out_part, r.shard_rows)), r.grad_out
     )
     tell(r.free_pair, device(w, dp=w.mate))
-    r.shard_out.relay(2)
-    r.grad_out.step(0)
+    output_back(r, 0)
+    output_back(r, 1)
     r.shard_out.relay(3)
-    r.shard_out.finish()
-
-    def mix_back(rows):
-        r.d_mixed[rows, :] = dot_nn(r.row_cot[rows, :], r.full_out[...])
-
-    by_rows(tokens, 256, mix_back)
+    output_back(r, 2)
+    output_back(r, 3)
     over_chunks(r, lambda c: cross_chunk(c, r))
     r.ex_crosses.start()
-    r.grad_out.step(1)
-
-    def share(slot):
-        rows = pl.ds(pl.multiple_of(slot * block, block), block)
-        tile = 512
-
-        def body(n, carry):
-            cols = pl.ds(pl.multiple_of(n * tile, tile), tile)
-            r.part[rows, cols] = dot_nt(r.mixed[rows, :], r.full_out[cols, :]).astype(BF16)
-            return carry
-
-        lax.fori_loop(0, r.part.shape[1] // tile, body, 0)
-
-    share(w.across)
+    r.grad_out.step(0)
+    output_share(r, w.across)
     r.out_rows.start(0, 1)
-    share(w.near_x)
-    r.out_rows.start(2)
-    share(w.near_y)
-    r.out_rows.start(3)
-    share(w.tp)
+    r.g_gate[...] = jnp.zeros_like(r.g_gate)
+    r.ex_crosses.finish()
+    over_chunks(r, lambda c: gate_back_chunk(c, r))
     for item in (r.shard_x, r.shard_dt, r.shard_z, r.shard_out, r.row_n, r.row_c):
         item.drain()
-    r.ex_crosses.finish()
-    r.g_gate[...] = jnp.zeros_like(r.g_gate)
-    over_chunks(r, lambda c: gate_back_chunk(c, r))
     pl.semaphore_wait(r.free_pair, 1)
     weight_parts(
-        product_maker(r.row_normed, r.d_z, flat_store(r.full_out, r.shard_rows)), r.grad_z
+        product_maker(
+            r.row_normed, r.d_z, side_store(r.row_cot, r.shard_rows, r.pairs * LANES)
+        ),
+        r.grad_z,
     )
     tell(r.free_pair, device(w, dp=w.mate))
+    r.grad_out.step(1)
+    for slot, copy in ((w.near_x, 2), (w.near_y, 3)):
+        output_share(r, slot)
+        r.out_rows.start(copy)
+    output_share(r, w.tp)
+    r.out_rows.hand_on()
+    tell(r.free_far, device(w, tp=w.near_x))
+    tell(r.free_far, device(w, tp=w.near_y))
 
 
 def phase_back(r):
@@ -1176,7 +1222,6 @@
 
         @pl.when(i == 2)
         def _():
-            r.out_rows.hand_on()
             r.grad_z.step(0)
 
         pl.when(i == 5)(lambda: r.grad_z.step(1))
@@ -1200,7 +1245,6 @@
 
     lax.fori_loop(0, block // step, add, 0)
     r.put(r.v_block, r.o_block, 1).start()
-    r.out_rows.drain()
     tell(r.free_row, device(w, tp=w.near_x))
     tell(r.free_row, device(w, tp=w.near_y))
 
@@ -1226,12 +1270,8 @@
         ),
         r.grad_bc,
     )
-    step_parts(r, edge)
-    for z in range(LAST_Z + 1):
-        r.grad_dt.pair_copy(z).start()
-    finish_block(r)
+    r.out_rows.drain()
     r.g_pre[...] = jnp.zeros_like(r.g_pre)
-    pl.semaphore_wait(r.free_row, 2)
 
     def share(slot):
         rows = pl.ds(pl.multiple_of(slot * block, block), block)
@@ -1249,59 +1289,65 @@
         lax.fori_loop(0, r.part.shape[1] // tile, body, 0)
 
     share(w.across)
+    pl.semaphore_wait(r.free_far, 2)
     r.in_rows.start(0, 1)
-    for z in (3, 0, 2, 1):
-        r.grad_dt.launch(z)
-    r.grad_dt.drain_pair()
     pl.semaphore_wait(r.free_pair, 1)
     pl.semaphore_wait(r.free_line, 2)
     weight_parts(
         product_maker(
             r.row_normed,
             r.d_rest.at[:, pl.ds(0, width)],
-            side_store(r.row_cot, r.shard_rows, width),
+            flat_store(r.full_out, r.shard_rows),
         ),
         r.grad_x_part,
     )
     r.grad_bc.step(0)
-    r.grad_dt.step(0)
+    finish_block(r)
     share(w.near_x)
+    pl.semaphore_wait(r.free_row, 2)
     r.in_rows.start(2)
+    r.grad_bc.step(1)
     share(w.near_y)
     r.in_rows.start(3)
-    r.grad_bc.step(1)
-    r.grad_dt.step(1)
     share(w.tp)
+    r.in_rows.hand_on()
+    r.grad_x_part.step(0)
+    step_parts(r, edge)
+    for z in range(LAST_Z + 1):
+        r.grad_dt.pair_copy(z).start()
     pack_small(r)
     r.ex_pair.start()
     r.grad_z.finish(r.v_w_z)
     r.put(r.v_w_z, r.o_w_z, 2).start()
-    r.grad_x_part.step(0)
-    r.in_rows.hand_on()
+    r.grad_bc.finish(r.bc_sum)
+    r.bc_slots.at[w.tp][...] = r.bc_sum[...].astype(BF16)
+    r.ex_bc.start()
     again = [
         pltpu.make_async_copy(r.cot.at[pl.ds(k * (block // 2), block // 2)], r.far.at[k], r.s_m.at[k])
         for k in range(2)
     ]
     for copy in again:
         copy.start()
+    for z in (3, 0, 2, 1):
+        r.grad_dt.launch(z)
+    r.grad_dt.drain_pair()
     r.ex_pair.finish()
     r.small_z.at[w.z][...] = r.ex_pair.total()
     r.ex_z.start()
-    r.grad_bc.finish(r.bc_sum)
-    r.grad_dt.finish(r.v_w_dt)
-    r.put(r.v_w_dt, r.o_w_dt, 3).start()
-    r.bc_slots.at[w.tp][...] = r.bc_sum[...].astype(BF16)
-    r.ex_bc.start()
+    r.grad_x_part.step(1)
+    r.grad_dt.step(0)
     r.ex_z.finish()
     total = r.ex_z.total()
     r.v_small[...] = total[:SMALL_DP]
     r.put(r.v_small, r.o_small, 4).start()
     r.small_t.at[w.tp][...] = total[SMALL_DP:]
     r.ex_t.start()
-    r.grad_x_part.step(1)
+    r.grad_dt.step(1)
     r.ex_bc.finish()
     r.v_w_bc[...] = r.ex_bc.total()
     r.put(r.v_w_bc, r.o_w_bc, 5).start()
+    for item in (r.grad_z, r.grad_bc):
+        item.drain()
     r.ex_t.finish()
     shared = r.ex_t.total()
     gain = r.pre_gain[...].reshape(1, r.x_held.shape[1])
@@ -1310,6 +1356,9 @@
     for p in range(count):
         r.v_shared[p : p + 1, :] = shared[p : p + 1, :] / gain[:, p * LANES : (p + 1) * LANES]
     r.put(r.v_shared, r.o_shared, 6).start()
+    r.grad_dt.finish(r.v_w_dt)
+    r.put(r.v_w_dt, r.o_w_dt, 3).start()
+    r.grad_dt.drain()
     for copy in again:
         copy.wait()
     r.in_rows.finish()
@@ -1330,8 +1379,7 @@
 
     lax.fori_loop(0, block // step, body, 0)
     r.put(r.v_grad_x, r.o_grad_x, 7).start()
-    for item in (r.grad_z, r.grad_bc, r.grad_dt, r.in_rows):
-        item.drain()
+    r.in_rows.drain()
     r.grad_x_part.finish(r.v_w_x)
     r.put(r.v_w_x, r.o_w_x, 8).start()
     r.grad_x_part.drain()
@@ -1421,10 +1469,9 @@
     rows = r.shard_rows
     held = (r.pair, r.up, r.down, r.p_main, r.l_main, PARTS)
     r.grad_out = LineScatter(w, flat_shard(r.out_part, rows), *held)
-    r.grad_x_part = LineScatter(w, side_shard(r.row_cot, rows, width), *held)
-    r.grad_z = LineScatter(
-        w, flat_shard(r.full_out, rows), r.pair, r.up_z, r.down_z, r.p_main, r.l_z, PARTS
-    )
+    r.grad_x_part = LineScatter(w, flat_shard(r.full_out, rows), *held)
+    side = side_shard(r.row_cot, rows, width)
+    r.grad_z = LineScatter(w, side, r.pair, r.up_z, r.down_z, r.p_main, r.l_z, PARTS)
     held_dt = (r.pair_dt, r.up_dt, r.down_dt, r.p_dt, r.l_dt, 1)
     r.grad_dt = LineScatter(w, flat_shard(r.dt_part, STEP_ROWS), *held_dt)
     in_row = [device(w, tp=t) for t in (w.near_x, w.near_y, w.across)]
@@ -1438,10 +1485,10 @@
     r.ex_bc = exchange(5, r.bc_slots, w.tp, in_row)
     r.put = lambda src, dst, i: pltpu.make_async_copy(src, dst, r.s_o.at[i])
     tokens = r.chunks * CHUNK
-    phase_one(r)
 
     def middle(z, d_mixed, mixed):
         r.z, r.d_mixed, r.mixed = z, d_mixed, mixed
+        phase_one(r)
         phase_mid(r)
 
     pl.run_scoped(
@@ -1551,9 +1598,9 @@
     signal = pltpu.SemaphoreType.REGULAR
     semaphores = dict(
         s_w=dma((3, 3)),
-        r_w=dma((3, 4 * PARTS + 1)),
+        r_w=dma((3, 4 * PARTS + 4)),
         s_d=dma((3,)),
-        r_d=dma((5,)),
+        r_d=dma((8,)),
         s_r=dma((2,)),
         r_r=dma((2, 3)),
         s_q=dma((1,)),
@@ -1571,6 +1618,7 @@
         free_pair=signal,
         free_line=signal,
         free_row=signal,
+        free_far=signal,
     )
     names = RAW_IN + tuple("o_" + name for name in outs) + tuple(scratch) + tuple(semaphores)
     values = list(args)

time: 173 us -> 166 us (0.960); the launches traced: 171 us -> 166 us
  Pallas kernels: 170 us -> 165 us
    pallas_call x1, Pallas kernels: 165 us -> 161 us  [whole_call(): pl.pallas_call(functools.partial(whole_kernel, names=names, width=width),...]
where the time goes in v4:
time: 166 us
  Pallas kernels  165 us (99%)
    pallas_call x1, Pallas kernels, whole_call(): pl.pallas_call(functools.partial(whole_kernel, names=names, width=width),...  161 us
    pallas_call x1, Pallas kernels, publish(): pl.pallas_call(publish_kernel, out_shape=tuple([jax.ShapeDtypeStruct(v.sh...  4.57 us

profile of v4, /device:TPU:0, one launch (start us, length us, event | category | flops | bytes accessed | tf_op | source)
XLA Modules:
  0.0 166.1 jit_solution(7410739372285647723)
XLA Ops:
  0.7 160.8 %shard_map.288 = (bf16[256,1536]{1,0:T(8,128)(2,1)}, bf16[256,1536]{1,0:T(8,128)(2,1)}, f32[192,768]{1,0:T(8,128)}, f32[192,768]{1,0:T(8,128)}, f32[192,256]{1,0...) custom-call(bf16[256,1536]{1,0:T(8,128)(2,1)} %refs_0_.1, ...), custom_call_target="tpu_custom_call" | custom-call | flops 49999998976 | bytes 67108864 | tf_op jit(solution)/shard_map/pallas_call | solution.py:1630
  161.4 4.6 %shard_map.289 = (bf16[256,1536]{1,0:T(8,128)(2,1)}, bf16[256,1536]{1,0:T(8,128)(2,1)}, f32[192,768]{1,0:T(8,128)}, f32[192,768]{1,0:T(8,128)}, f32[192,256]{1,0...) custom-call(bf16[256,1536]{1,0:T(8,128)(2,1)} %get-tuple-element.41., ...), custom_call_target="tpu_custom_call" | custom-call | tf_op jit(solution)/shard_map/pallas_call | solution.py:1710

commit v5 on v4

--- a/solution.py
+++ b/solution.py
@@ -665,8 +665,9 @@
 
 
 class LineScatter:
-    def __init__(self, w, shard, pair, up, down, pair_sem, line_sem, parts):
+    def __init__(self, w, shard, pair, up, down, pair_sem, line_sem, parts, hold=False):
         self.w, self.shard, self.pair, self.up, self.down = w, shard, pair, up, down
+        self.hold = hold
         self.pair_sem, self.line_sem, self.parts = pair_sem, line_sem, parts
         self.rows = pair.shape[0] // (LAST_Z + 1)
 
@@ -715,46 +716,53 @@
                 if send is not None:
                     send(z, part).start()
 
-        low = (w.z == 0) & (z > 0)
-        high = (w.z == LAST_Z) & (z < LAST_Z)
+        held = 1 if self.hold else 0
+        low = (w.z == 0) & (z > held)
+        high = (w.z == LAST_Z) & (z < LAST_Z - held)
         pl.when(low)(lambda: every(self.up_copy))
         pl.when(high)(lambda: every(self.down_copy))
         pl.when(jnp.logical_not(low | high))(lambda: every(None))
 
-    def pass_up(self, z):
+    def launch_last(self):
         for part in range(self.parts):
-            self.up_copy(z, part).wait_recv()
-            add_into(
-                self.piece(self.shard(z, self.w.core), part),
-                self.piece(self.slot(self.up, z - 1), part),
-            )
-            self.up_copy(z, part).start()
-
-    def pass_down(self, z):
-        for part in range(self.parts):
-            self.down_copy(z, part).wait_recv()
-            add_into(
-                self.piece(self.shard(z, self.w.core), part),
-                self.piece(self.slot(self.down, z), part),
-            )
-            self.down_copy(z, part).start()
-
-    def step(self, k):
+            pl.when(self.w.z == 0)(lambda part=part: self.up_copy(1, part).start())
+            pl.when(self.w.z == LAST_Z)(lambda part=part: self.down_copy(LAST_Z - 1, part).start())
+
+    def pass_up(self, z, part):
+        self.up_copy(z, part).wait_recv()
+        add_into(
+            self.piece(self.shard(z, self.w.core), part),
+            self.piece(self.slot(self.up, z - 1), part),
+        )
+        self.up_copy(z, part).start()
+
+    def pass_down(self, z, part):
+        self.down_copy(z, part).wait_recv()
+        add_into(
+            self.piece(self.shard(z, self.w.core), part),
+            self.piece(self.slot(self.down, z), part),
+        )
+        self.down_copy(z, part).start()
+
+    def step(self, k, part=None):
         w = self.w
-        if k == 0:
-            pl.when(w.z == 1)(lambda: self.pass_up(3))
-            pl.when(w.z == 2)(lambda: self.pass_down(0))
+        if part is None:
+            for part in range(self.parts):
+                self.step(k, part)
+        elif k == 0:
+            pl.when(w.z == 1)(lambda: self.pass_up(3, part))
+            pl.when(w.z == 2)(lambda: self.pass_down(0, part))
         else:
 
             @pl.when(w.z == 1)
             def _():
-                self.pass_up(2)
-                self.pass_down(0)
+                self.pass_up(2, part)
+                self.pass_down(0, part)
 
             @pl.when(w.z == 2)
             def _():
-                self.pass_down(1)
-                self.pass_up(3)
+                self.pass_down(1, part)
+                self.pass_up(3, part)
 
     def finish(self, out):
         w = self.w
@@ -1220,11 +1228,9 @@
             tell(r.free_line, device(w, dp=other_z(w, 1)))
             tell(r.free_line, device(w, dp=other_z(w, 3)))
 
-        @pl.when(i == 2)
-        def _():
-            r.grad_z.step(0)
-
-        pl.when(i == 5)(lambda: r.grad_z.step(1))
+        for at, k, part in ((1, 0, 0), (2, 0, 1), (4, 1, 0), (5, 1, 1)):
+            pl.when(i == at)(lambda k=k, part=part: r.grad_z.step(k, part))
+
         return carry
 
     lax.fori_loop(0, r.chunks, body, 0)
@@ -1262,14 +1268,6 @@
     width = r.pairs * LANES
     block = r.x_held.shape[0]
     edge = width + 2 * NSTATE
-    weight_parts(
-        product_maker(
-            r.row_normed,
-            r.d_rest.at[:, pl.ds(width, 2 * NSTATE)],
-            flat_store(r.bc_part, r.shard_rows),
-        ),
-        r.grad_bc,
-    )
     r.out_rows.drain()
     r.g_pre[...] = jnp.zeros_like(r.g_pre)
 
@@ -1291,6 +1289,27 @@
     share(w.across)
     pl.semaphore_wait(r.free_far, 2)
     r.in_rows.start(0, 1)
+    weight_parts(
+        product_maker(
+            r.row_normed,
+            r.d_rest.at[:, pl.ds(width, 2 * NSTATE)],
+            flat_store(r.bc_part, r.shard_rows),
+        ),
+        r.grad_bc,
+    )
+    step_parts(r, edge)
+    for z in range(LAST_Z + 1):
+        r.grad_dt.pair_copy(z).start()
+    finish_block(r)
+    share(w.near_x)
+    pl.semaphore_wait(r.free_row, 2)
+    r.in_rows.start(2)
+    r.grad_bc.step(0)
+    for i in range(LAST_Z + 1):
+        r.grad_dt.launch(far_first(w, i))
+    r.grad_dt.drain_pair()
+    share(w.near_y)
+    r.in_rows.start(3)
     pl.semaphore_wait(r.free_pair, 1)
     pl.semaphore_wait(r.free_line, 2)
     weight_parts(
@@ -1301,64 +1320,43 @@
         ),
         r.grad_x_part,
     )
-    r.grad_bc.step(0)
-    finish_block(r)
-    share(w.near_x)
-    pl.semaphore_wait(r.free_row, 2)
-    r.in_rows.start(2)
     r.grad_bc.step(1)
-    share(w.near_y)
-    r.in_rows.start(3)
+    r.grad_dt.step(0)
     share(w.tp)
     r.in_rows.hand_on()
-    r.grad_x_part.step(0)
-    step_parts(r, edge)
-    for z in range(LAST_Z + 1):
-        r.grad_dt.pair_copy(z).start()
-    pack_small(r)
-    r.ex_pair.start()
-    r.grad_z.finish(r.v_w_z)
-    r.put(r.v_w_z, r.o_w_z, 2).start()
-    r.grad_bc.finish(r.bc_sum)
-    r.bc_slots.at[w.tp][...] = r.bc_sum[...].astype(BF16)
-    r.ex_bc.start()
     again = [
         pltpu.make_async_copy(r.cot.at[pl.ds(k * (block // 2), block // 2)], r.far.at[k], r.s_m.at[k])
         for k in range(2)
     ]
     for copy in again:
         copy.start()
-    for z in (3, 0, 2, 1):
-        r.grad_dt.launch(z)
-    r.grad_dt.drain_pair()
+    r.grad_dt.step(1)
+    pack_small(r)
+    r.ex_pair.start()
+    r.grad_x_part.step(0, 0)
+    r.grad_bc.finish(r.bc_sum)
+    r.bc_slots.at[w.tp][...] = r.bc_sum[...].astype(BF16)
+    r.ex_bc.start()
     r.ex_pair.finish()
     r.small_z.at[w.z][...] = r.ex_pair.total()
     r.ex_z.start()
-    r.grad_x_part.step(1)
-    r.grad_dt.step(0)
+    r.grad_x_part.launch_last()
+    r.grad_x_part.step(0, 1)
+    r.grad_dt.finish(r.v_w_dt)
+    r.put(r.v_w_dt, r.o_w_dt, 3).start()
+    r.grad_z.finish(r.v_w_z)
+    r.put(r.v_w_z, r.o_w_z, 2).start()
+    r.grad_x_part.step(1, 0)
+    r.grad_x_part.step(1, 1)
     r.ex_z.finish()
     total = r.ex_z.total()
+    r.small_t.at[w.tp][...] = total[SMALL_DP:]
+    r.ex_t.start()
     r.v_small[...] = total[:SMALL_DP]
     r.put(r.v_small, r.o_small, 4).start()
-    r.small_t.at[w.tp][...] = total[SMALL_DP:]
-    r.ex_t.start()
-    r.grad_dt.step(1)
-    r.ex_bc.finish()
-    r.v_w_bc[...] = r.ex_bc.total()
-    r.put(r.v_w_bc, r.o_w_bc, 5).start()
-    for item in (r.grad_z, r.grad_bc):
+    for item in (r.grad_z, r.grad_bc, r.grad_dt):
         item.drain()
-    r.ex_t.finish()
-    shared = r.ex_t.total()
     gain = r.pre_gain[...].reshape(1, r.x_held.shape[1])
-    count = gain.shape[1] // LANES
-    r.v_shared[...] = shared
-    for p in range(count):
-        r.v_shared[p : p + 1, :] = shared[p : p + 1, :] / gain[:, p * LANES : (p + 1) * LANES]
-    r.put(r.v_shared, r.o_shared, 6).start()
-    r.grad_dt.finish(r.v_w_dt)
-    r.put(r.v_w_dt, r.o_w_dt, 3).start()
-    r.grad_dt.drain()
     for copy in again:
         copy.wait()
     r.in_rows.finish()
@@ -1380,9 +1378,19 @@
     lax.fori_loop(0, block // step, body, 0)
     r.put(r.v_grad_x, r.o_grad_x, 7).start()
     r.in_rows.drain()
+    r.ex_bc.finish()
+    r.v_w_bc[...] = r.ex_bc.total()
+    r.put(r.v_w_bc, r.o_w_bc, 5).start()
     r.grad_x_part.finish(r.v_w_x)
     r.put(r.v_w_x, r.o_w_x, 8).start()
     r.grad_x_part.drain()
+    r.ex_t.finish()
+    shared = r.ex_t.total()
+    count = gain.shape[1] // LANES
+    r.v_shared[...] = shared
+    for p in range(count):
+        r.v_shared[p : p + 1, :] = shared[p : p + 1, :] / gain[:, p * LANES : (p + 1) * LANES]
+    r.put(r.v_shared, r.o_shared, 6).start()
     ends = ("w_out", "block", "w_z", "w_dt", "small", "w_bc", "shared", "grad_x", "w_x")
     for i, name in enumerate(ends):
         r.put(getattr(r, "v_" + name), getattr(r, "o_" + name), i).wait()
@@ -1469,7 +1477,7 @@
     rows = r.shard_rows
     held = (r.pair, r.up, r.down, r.p_main, r.l_main, PARTS)
     r.grad_out = LineScatter(w, flat_shard(r.out_part, rows), *held)
-    r.grad_x_part = LineScatter(w, flat_shard(r.full_out, rows), *held)
+    r.grad_x_part = LineScatter(w, flat_shard(r.full_out, rows), *held, hold=True)
     side = side_shard(r.row_cot, rows, width)
     r.grad_z = LineScatter(w, side, r.pair, r.up_z, r.down_z, r.p_main, r.l_z, PARTS)
     held_dt = (r.pair_dt, r.up_dt, r.down_dt, r.p_dt, r.l_dt, 1)

time: 166 us -> 162 us (0.976)
  Pallas kernels: 165 us -> 160 us
    pallas_call x1, Pallas kernels: 161 us -> 156 us  [whole_call(): pl.pallas_call(functools.partial(whole_kernel, names=names, width=width),...]
where the time goes in v5:
time: 162 us; the launch traced here: 161 us
  Pallas kernels  160 us (99%)
    pallas_call x1, Pallas kernels, whole_call(): pl.pallas_call(functools.partial(whole_kernel, names=names, width=width),...  156 us
    pallas_call x1, Pallas kernels, publish(): pl.pallas_call(publish_kernel, out_shape=tuple([jax.ShapeDtypeStruct(v.sh...  4.57 us

profile of v5, /device:TPU:0, one launch (start us, length us, event | category | flops | bytes accessed | tf_op | source)
XLA Modules:
  0.0 161.3 jit_solution(17272605045616696915)
XLA Ops:
  0.7 155.9 %shard_map.288 = (bf16[256,1536]{1,0:T(8,128)(2,1)}, bf16[256,1536]{1,0:T(8,128)(2,1)}, f32[192,768]{1,0:T(8,128)}, f32[192,768]{1,0:T(8,128)}, f32[192,256]{1,0...) custom-call(bf16[256,1536]{1,0:T(8,128)(2,1)} %refs_0_.1, ...), custom_call_target="tpu_custom_call" | custom-call | flops 49999998976 | bytes 67108864 | tf_op jit(solution)/shard_map/pallas_call | solution.py:1638
  156.5 4.6 %shard_map.289 = (bf16[256,1536]{1,0:T(8,128)(2,1)}, bf16[256,1536]{1,0:T(8,128)(2,1)}, f32[192,768]{1,0:T(8,128)}, f32[192,768]{1,0:T(8,128)}, f32[192,256]{1,0...) custom-call(bf16[256,1536]{1,0:T(8,128)(2,1)} %get-tuple-element.41., ...), custom_call_target="tpu_custom_call" | custom-call | tf_op jit(solution)/shard_map/pallas_call | solution.py:1718

commit v6 on v5

--- a/solution.py
+++ b/solution.py
@@ -502,7 +502,7 @@
     def copy(self, z, kind, part):
         w = self.w
         block = self.shard(z, w.core, part)
-        to = {UP: w.dp + 2, DOWN: w.dp - 2}.get(kind, w.mate)
+        to = {UP: other_z(w, 1), DOWN: other_z(w, LAST_Z)}.get(kind, w.mate)
         first = (self.parts if kind == PAIR else part) * (LAST_Z + 1)
         return remote(block, block, self.send.at[kind], self.recv.at[first + z], device(w, dp=to))
 
@@ -694,7 +694,7 @@
             self.piece(self.slot(self.up, z - 1), part),
             self.line_sem.at[0],
             self.line_sem.at[2 + part * LAST_Z + z - 1],
-            device(self.w, dp=self.w.dp + 2),
+            device(self.w, dp=other_z(self.w, 1)),
         )
 
     def down_copy(self, z, part):
@@ -703,7 +703,7 @@
             self.piece(self.slot(self.down, z), part),
             self.line_sem.at[1],
             self.line_sem.at[2 + (self.parts + part) * LAST_Z + z],
-            device(self.w, dp=self.w.dp - 2),
+            device(self.w, dp=other_z(self.w, LAST_Z)),
         )
 
     def launch(self, z):
@@ -1148,7 +1148,6 @@
         @pl.when(c == 1)
         def _():
             r.shard_z.relay(1)
-            r.shard_out.relay(0)
             project_z(r, 0)
 
         @pl.when(c == 3)
@@ -1159,6 +1158,7 @@
         @pl.when(c == 5)
         def _():
             r.shard_z.relay(2)
+            r.shard_out.relay(0)
             project_z(r, 2)
 
     over_chunks(r, body)
@@ -1166,12 +1166,11 @@
 
 def phase_mid(r):
     w = r.w
-    r.shard_out.relay(1)
     r.shard_z.relay(3)
     project_z(r, 3)
     over_chunks(r, lambda c: square_chunk(c, r))
     r.ex_squares.start()
-    r.shard_out.relay(2)
+    r.shard_out.relay(1)
     r.row_c.finish()
     r.ex_squares.finish()
     over_chunks(r, lambda c: mix_chunk(c, r))
@@ -1180,6 +1179,7 @@
     )
     tell(r.free_pair, device(w, dp=w.mate))
     output_back(r, 0)
+    r.shard_out.relay(2)
     output_back(r, 1)
     r.shard_out.relay(3)
     output_back(r, 2)

time: 162 us -> 160 us (0.988)
    pallas_call x1, Pallas kernels: 156 us -> 154 us  [whole_call(): pl.pallas_call(functools.partial(whole_kernel, names=names, width=width),...]
where the time goes in v6:
time: 160 us; the launch traced here: 159 us
  Pallas kernels  159 us (99%)
    pallas_call x1, Pallas kernels, whole_call(): pl.pallas_call(functools.partial(whole_kernel, names=names, width=width),...  154 us
    pallas_call x1, Pallas kernels, publish(): pl.pallas_call(publish_kernel, out_shape=tuple([jax.ShapeDtypeStruct(v.sh...  4.57 us

profile of v6, /device:TPU:0, one launch (start us, length us, event | category | flops | bytes accessed | tf_op | source)
XLA Modules:
  0.0 159.4 jit_solution(12688672136789240300)
XLA Ops:
  0.7 154.0 %shard_map.288 = (bf16[256,1536]{1,0:T(8,128)(2,1)}, bf16[256,1536]{1,0:T(8,128)(2,1)}, f32[192,768]{1,0:T(8,128)}, f32[192,768]{1,0:T(8,128)}, f32[192,256]{1,0...) custom-call(bf16[256,1536]{1,0:T(8,128)(2,1)} %refs_0_.1, ...), custom_call_target="tpu_custom_call" | custom-call | flops 49999998976 | bytes 67108864 | tf_op jit(solution)/shard_map/pallas_call | solution.py:1638
  154.6 4.6 %shard_map.289 = (bf16[256,1536]{1,0:T(8,128)(2,1)}, bf16[256,1536]{1,0:T(8,128)(2,1)}, f32[192,768]{1,0:T(8,128)}, f32[192,768]{1,0:T(8,128)}, f32[192,256]{1,0...) custom-call(bf16[256,1536]{1,0:T(8,128)(2,1)} %get-tuple-element.41., ...), custom_call_target="tpu_custom_call" | custom-call | tf_op jit(solution)/shard_map/pallas_call | solution.py:1718
